TPU v7x, 256 devices: a whole 4x4x8 slice. The times are simulated.
256 devices in a mesh: samples: 32 (over z, x_lo, core), mp: 8 (over y, x_hi).
Axes of the slice: x: 4 (x_hi: 2, x_lo: 2; x = x_hi * 2 + x_lo), y: 4, z: 8, core: 2. Of those that a mesh axis runs over, the one named last changes fastest.
Arguments:
- spin_values: int32 [128, 256], P('samples'), may hold values from -1 to 1, as said below
- features: bfloat16 [128, 256, 1024], P('samples'), may hold values from -6 to 6
- spin_embed: bfloat16 [1024], replicated, may hold values from -4 to 4
- norm_gain: bfloat16 [1024], replicated, may hold values from 0.25 to 1.75
- up_weight: bfloat16 [1024, 4096], P(None, 'mp'), may hold values from -0.1875 to 0.1875
- down_weight: bfloat16 [1024, 4096], P(None, 'mp'), may hold values from -0.09375 to 0.09375
- readout: bfloat16 [1024], replicated, may hold values from -0.00012207031 to 0.00012207031
- local_energy: float32 [128], P('samples'), may hold values from -60 to 60
- damping: float32 [1], replicated, may hold values from 7.1525574e-06 to 7.1525574e-05
Outputs:
- solution: float32 [1024, 4096], P('samples', 'mp')
Inputs may be any that keep to these rules, and one draw needn't show every extreme that they name: `spin_values`: every entry is -1 or +1.
All inputs are finite; a program needn't handle non-finite values.
Results may differ from a plain program's by a relative error of at most 0.0073.
Values may be sent and summed in bfloat16 or wider, within the bound.
No kernel may reach another device: no remote copies, remote signals or barrier semaphores. Data moves between devices by JAX's collectives and lax.ppermute only.
A program may use at most 64 MiB of HBM per device.

v0:
```python
import jax
import jax.numpy as jnp
from jax import lax
from jax.sharding import PartitionSpec as P

ITERS = 3


gelu_coef = 0.7978845608028654
cubic_coef = 0.044715


def gelu_value(value_in):
    return (
        0.5
        * value_in
        * (1.0 + jnp.tanh(gelu_coef * (value_in + cubic_coef * value_in * value_in * value_in)))
    )


def gelu_slope(value_in):
    inner_tanh = jnp.tanh(gelu_coef * (value_in + cubic_coef * value_in * value_in * value_in))
    return 0.5 * (1.0 + inner_tanh) + 0.5 * value_in * (
        1.0 - inner_tanh * inner_tanh
    ) * gelu_coef * (1.0 + 3.0 * cubic_coef * value_in * value_in)


def weighted_term(normed, pullback, weights, length):
    samp_dev = weights.shape[0]
    scaled = (
        (pullback.astype(jnp.float32).reshape(samp_dev, length, -1) * weights[:, None, None])
        .reshape(pullback.shape)
        .astype(jnp.bfloat16)
    )

    def term_rows(first_row, row_count):
        return lax.dot_general(
            normed, scaled, (((0,), (0,)), ((), ())), preferred_element_type=jnp.float32
        )

    return term_rows


def sample_values(projected, pullback, samp_dev):
    return jnp.sum((projected * pullback.astype(jnp.float32)).reshape(samp_dev, -1), axis=1)


def centered_weights(partial_value, samp_dev):
    sample_count = samp_dev * lax.axis_size("samples")
    values = lax.psum(partial_value, "mp")
    value_mean = lax.psum(jnp.sum(values), "samples") / sample_count
    return (values - value_mean) / sample_count


def copy_norm(residual):
    return lax.psum(jnp.sum(residual * residual), "mp")


def body(
    spin_values,
    features,
    spin_embed,
    norm_gain,
    up_weight,
    down_weight,
    readout,
    local_energy,
    damping,
):
    samp_dev, length, model_width = features.shape
    tokens = samp_dev * length
    inputs = (
        features.astype(jnp.float32)
        + spin_values.astype(jnp.float32)[:, :, None] * spin_embed.astype(jnp.float32)
    ).reshape(tokens, model_width)
    inv_scale = lax.rsqrt(jnp.mean(inputs * inputs, axis=1, keepdims=True) + 1e-05)
    normed = (inputs * inv_scale * norm_gain.astype(jnp.float32)).astype(jnp.bfloat16)
    hidden_pre = jnp.dot(normed, up_weight, preferred_element_type=jnp.float32)
    activated = gelu_value(hidden_pre).astype(jnp.bfloat16)
    mixed_rows = lax.psum_scatter(
        lax.dot_general(
            activated, down_weight, (((1,), (1,)), ((), ())), preferred_element_type=jnp.float32
        ),
        "mp",
        scatter_dimension=0,
        tiled=True,
    )
    share_rows = mixed_rows.shape[0]
    own_inputs = lax.dynamic_slice_in_dim(inputs, lax.axis_index("mp") * share_rows, share_rows, 0)
    slope_rows = (readout.astype(jnp.float32) * jnp.tanh(own_inputs + mixed_rows)).astype(
        jnp.bfloat16
    )
    slope_all = lax.all_gather(slope_rows, "mp", axis=0, tiled=True)
    back_proj = jnp.dot(slope_all, down_weight, preferred_element_type=jnp.float32)
    pullback = (gelu_slope(hidden_pre) * back_proj).astype(jnp.bfloat16)
    sample_count = samp_dev * lax.axis_size("samples")
    rows_dev = model_width // lax.axis_size("samples")
    energy_mean = lax.psum(jnp.sum(local_energy), "samples") / sample_count
    force_shard = lax.psum_scatter(
        weighted_term(normed, pullback, (local_energy - energy_mean) / sample_count, length)(
            jnp.int32(0), rows_dev * lax.axis_size("samples")
        ),
        "samples",
        scatter_dimension=0,
        tiled=True,
    )
    force_all = lax.all_gather(force_shard, "samples", axis=0, tiled=True)
    solution = jnp.zeros_like(force_all)
    residual = force_all
    direction = force_all
    norm_now = copy_norm(residual)
    for iteration in range(ITERS):
        direction_half = direction.astype(jnp.bfloat16)
        projected = jnp.dot(normed, direction_half, preferred_element_type=jnp.float32)
        weights = centered_weights(sample_values(projected, pullback, samp_dev), samp_dev)
        term_rows = weighted_term(normed, pullback, weights, length)
        image_all = lax.psum(term_rows(0, model_width), "samples") + damping[0] * direction
        step_size = norm_now / lax.psum(jnp.sum(direction * image_all), "mp")
        solution = solution + step_size * direction
        residual = residual - step_size * image_all
        norm_next = copy_norm(residual)
        direction = residual + norm_next / norm_now * direction
        norm_now = norm_next
    return lax.dynamic_slice_in_dim(solution, lax.axis_index("samples") * rows_dev, rows_dev, 0)


def solution(mesh):
    in_specs = (
        P("samples", None),
        P("samples", None, None),
        P(),
        P(),
        P(None, "mp"),
        P(None, "mp"),
        P(),
        P("samples"),
        P(),
    )
    out_specs = P("samples", "mp")
    return jax.shard_map(body, mesh=mesh, in_specs=in_specs, out_specs=out_specs, check_vma=False)
```

profile of v0, /device:TPU:1, one launch (start us, length us, event | category | flops | bytes accessed | tf_op | source)
XLA Modules:
  0.0 1442.8 jit_solution(5719722257568637607)
XLA Ops:
  15.8 3.5 fusion.14
  20.0 91.9 %reduce-scatter.3.cloned.1.call-done = f32[128,1024]{1,0:T(8,128)} async-done(((f32[1024,1024]{1,0:T(8,128)}), f32[128,1024]{1,0:T(8,128)}) %reduce-scatter.3.cloned.1.call-update) | async-done | bytes 524304 | tf_op jit(solution)/shard_map/reduce_scatter | solution.py:80
  114.5 55.2 %psum.112 = f32[]{:T(128)} all-reduce(f32[]{:T(128)} %reduce_sum.148), channel_id=1, replica_groups=mesh['samples'=32,'mp'=8] {'samples'}, use_global_device_ids=true, to_apply=%region_3.0 | all-reduce | flops 1 | bytes 8 | tf_op jit(solution)/shard_map/psum | solution.py:98
  170.5 3.2 all-gather.3.cloned.1.call-done
  173.6 4.5 fusion.6
  181.9 113.6 %reduce-scatter.5.cloned.1.call-done = f32[32,512]{1,0:T(8,128)} async-done(((f32[1024,512]{1,0:T(8,128)}), f32[32,512]{1,0:T(8,128)}) %reduce-scatter.5.cloned.1.call-update) | async-done | bytes 65552 | tf_op jit(solution)/shard_map/reduce_scatter | solution.py:99
  295.5 68.4 %all-gather.5.cloned.1.call-done = f32[1024,512]{1,0:T(8,128)} async-done(((f32[32,512]{1,0:T(8,128)}), f32[1024,512]{1,0:T(8,128)}) %all-gather.5.cloned.1.call-update) | async-done | bytes 2097168 | tf_op jit(solution)/shard_map/all_gather | solution.py:107
  363.9 3.2 fusion.8
  367.2 20.1 %psum.114 = f32[4]{0:T(128)S(1)} all-reduce(f32[4]{0:T(128)S(1)} %reduce_sum.152), channel_id=1, replica_groups=mesh['samples'=32,'mp'=8] {'mp'}, use_global_device_ids=true, to_apply=%region_9.0 | all-reduce | flops 4 | bytes 32 | tf_op jit(solution)/shard_map/psum | solution.py:50
  388.0 57.0 %psum.115 = f32[]{:T(128)} all-reduce(f32[]{:T(128)} %reduce_sum.153), channel_id=1, replica_groups=mesh['samples'=32,'mp'=8] {'samples'}, use_global_device_ids=true, to_apply=%region_11.0 | all-reduce | flops 1 | bytes 8 | tf_op jit(solution)/shard_map/psum | solution.py:51
  445.8 3.8 fusion.19
  450.5 225.1 %all-reduce.5.cloned.1.call-done = f32[1024,512]{1,0:T(8,128)} async-done(((f32[1024,512]{1,0:T(8,128)}), f32[1024,512]{1,0:T(8,128)}) %all-reduce.5.cloned.1.call-update) | async-done | bytes 2097168 | tf_op jit(solution)/shard_map/psum | solution.py:117
  675.6 2.8 multiply_reduce_fusion.5
  678.4 20.7 %all-reduce = (f32[]{:T(128)}, f32[]{:T(128)}) all-reduce(f32[]{:T(128)} %get-tuple-element.6, f32[]{:T(128)} %get-tuple-element.5), channel_id=1, replica_groups=mesh['samples'=32,'mp'=8] {'mp'}, use_global_device_ids=true, to_apply=%region_6.0 | all-reduce | flops 2 | bytes 16 | tf_op jit(solution)/shard_map/psum | solution.py:56
  700.4 4.0 multiply_reduce_fusion.4
  704.4 16.2 %psum.118 = f32[]{:T(128)} all-reduce(f32[]{:T(128)} %get-tuple-element.9), channel_id=1, replica_groups=mesh['samples'=32,'mp'=8] {'mp'}, use_global_device_ids=true, to_apply=%region_16.0 | all-reduce | flops 1 | bytes 8 | tf_op jit(solution)/shard_map/psum | solution.py:56
  721.8 2.9 multiply_add_fusion.4
  726.4 18.8 %psum.119 = f32[4]{0:T(128)S(1)} all-reduce(f32[4]{0:T(128)S(1)} %reduce_sum.158), channel_id=1, replica_groups=mesh['samples'=32,'mp'=8] {'mp'}, use_global_device_ids=true, to_apply=%region_19.0 | all-reduce | flops 4 | bytes 32 | tf_op jit(solution)/shard_map/psum | solution.py:50
  745.8 64.3 %psum.120 = f32[]{:T(128)} all-reduce(f32[]{:T(128)} %reduce_sum.159), channel_id=1, replica_groups=mesh['samples'=32,'mp'=8] {'samples'}, use_global_device_ids=true, to_apply=%region_21.0 | all-reduce | flops 1 | bytes 8 | tf_op jit(solution)/shard_map/psum | solution.py:51
  810.8 4.5 fusion.17
  815.4 226.7 %all-reduce.7.cloned.1.call-done = f32[1024,512]{1,0:T(8,128)} async-done(((f32[1024,512]{1,0:T(8,128)}), f32[1024,512]{1,0:T(8,128)}) %all-reduce.7.cloned.1.call-update) | async-done | bytes 2097168 | tf_op jit(solution)/shard_map/psum | solution.py:117
  1042.1 2.7 multiply_reduce_fusion.3
  1044.8 20.5 %psum.122 = f32[]{:T(128)} all-reduce(f32[]{:T(128)} %multiply_reduce_fusion.3), channel_id=1, replica_groups=mesh['samples'=32,'mp'=8] {'mp'}, use_global_device_ids=true, to_apply=%region_24.0 | all-reduce | flops 1 | bytes 8 | tf_op jit(solution)/shard_map/psum | solution.py:118
  1066.5 3.4 multiply_reduce_fusion.2
  1070.0 16.2 %psum.123 = f32[]{:T(128)} all-reduce(f32[]{:T(128)} %multiply_reduce_fusion.2), channel_id=1, replica_groups=mesh['samples'=32,'mp'=8] {'mp'}, use_global_device_ids=true, to_apply=%region_26.0 | all-reduce | flops 1 | bytes 8 | tf_op jit(solution)/shard_map/psum | solution.py:56
  1087.6 3.2 multiply_add_fusion.2
  1093.5 18.8 %psum.124 = f32[4]{0:T(128)S(1)} all-reduce(f32[4]{0:T(128)S(1)} %reduce_sum.164), channel_id=1, replica_groups=mesh['samples'=32,'mp'=8] {'mp'}, use_global_device_ids=true, to_apply=%region_29.0 | all-reduce | flops 4 | bytes 32 | tf_op jit(solution)/shard_map/psum | solution.py:50
  1112.9 64.3 %psum.125 = f32[]{:T(128)} all-reduce(f32[]{:T(128)} %reduce_sum.165), channel_id=1, replica_groups=mesh['samples'=32,'mp'=8] {'samples'}, use_global_device_ids=true, to_apply=%region_31.0 | all-reduce | flops 1 | bytes 8 | tf_op jit(solution)/shard_map/psum | solution.py:51
  1177.9 4.5 fusion.15
  1182.4 226.7 %all-reduce.9.cloned.1.call-done = f32[1024,512]{1,0:T(8,128)} async-done(((f32[1024,512]{1,0:T(8,128)}), f32[1024,512]{1,0:T(8,128)}) %all-reduce.9.cloned.1.call-update) | async-done | bytes 2097168 | tf_op jit(solution)/shard_map/psum | solution.py:117
  1409.2 3.4 multiply_reduce_fusion.1
  1412.6 20.5 %psum.127 = f32[]{:T(128)} all-reduce(f32[]{:T(128)} %multiply_reduce_fusion.1), channel_id=1, replica_groups=mesh['samples'=32,'mp'=8] {'mp'}, use_global_device_ids=true, to_apply=%region_34.35 | all-reduce | flops 1 | bytes 8 | tf_op jit(solution)/shard_map/psum | solution.py:118
  (78 shorter events, 24.6 us)
Async XLA Ops:
  6.5 9.3 copy-start
  6.5 105.3 %reduce-scatter.3.cloned.1.call-start = ((), (), s32[]{:S(2)}) async-start(), calls=%async_computation.2 | async-start | bytes 4718592 | tf_op jit(solution)/shard_map/reduce_scatter | solution.py:80
  11.2 1.9 copy-start.2
  11.2 2.0 copy-start.8
  13.2 432.6 %copy-start.4 = (bf16[1024,1024]{1,0:T(8,128)(2,1)}, bf16[1024,1024]{1,0:T(8,128)(2,1)S(1)}, u32[]{:S(2)}) copy-start(bf16[1024,1024]{1,0:T(8,128)(2,1)S(1)} %multiply_convert_fusion) | copy-start | bytes 6291460
  14.5 1.3 copy-start.10
  19.3 0.7 copy-start.7
  19.3 94.6 %copy-start.9 = (f32[4]{0:T(128)S(1)}, f32[4]{0:T(128)}, u32[]{:S(2)}) copy-start(f32[4]{0:T(128)} %param.16) | copy-start | bytes 52
  19.3 154.3 %all-gather.3.cloned.1.call-start = ((), (), s32[]{:S(2)}) async-start(), calls=%async_computation.3 | async-start | bytes 2359296 | tf_op jit(solution)/shard_map/all_gather | solution.py:93
  113.9 181.6 %reduce-scatter.5.cloned.1.call-start = ((), (), s32[]{:S(2)}) async-start(), calls=%async_computation.4 | async-start | bytes 2162688 | tf_op jit(solution)/shard_map/reduce_scatter | solution.py:99
  178.1 1.0 copy-start.11
  181.8 182.1 %all-gather.5.cloned.1.call-start = ((), (), s32[]{:S(2)}) async-start(), calls=%async_computation.5 | async-start | bytes 2162688 | tf_op jit(solution)/shard_map/all_gather | solution.py:107
  295.5 380.1 %all-reduce.5.cloned.1.call-start = ((), (), s32[]{:S(2)}) async-start(), calls=%async_computation.6 | async-start | bytes 4194304 | tf_op jit(solution)/shard_map/psum | solution.py:117
  449.6 226.0 %copy-start.1 = (f32[1024,512]{1,0:T(8,128)S(1)}, f32[1024,512]{1,0:T(8,128)}, u32[]{:S(2)}) copy-start(f32[1024,512]{1,0:T(8,128)} %all-gather.5.cloned.1.call-done) | copy-start | bytes 6291460
  449.6 592.4 %all-reduce.7.cloned.1.call-start = ((), (), s32[]{:S(2)}) async-start(), calls=%async_computation.7 | async-start | bytes 4194304 | tf_op jit(solution)/shard_map/psum | solution.py:117
  721.8 2.9 copy-start.5
  721.8 3.1 copy-start.12
  815.3 593.9 %all-reduce.9.cloned.1.call-start = ((), (), s32[]{:S(2)}) async-start(), calls=%async_computation.8 | async-start | bytes 4194304 | tf_op jit(solution)/shard_map/psum | solution.py:117
  1087.5 4.5 copy-start.6
  1087.6 4.5 copy-start.13
  1090.7 1.3 copy-start.3
Sparse Core Ops, SparseCore 0:
  19.5 92.3 reduce-scatter.2
  114.9 58.7 all-gather.2
  181.9 113.4 reduce-scatter.4
  297.2 66.7 all-gather.4
  449.7 225.7 all-reduce.4
  815.4 226.5 all-reduce.6
  1182.5 226.5 all-reduce.8
where the time goes:
time: 1440 us
  waiting for transfers between devices  956 us (66%)
  blocking collectives  393 us (27%)
  other arithmetic  33.8 us (2%)
  matrix products  30.6 us (2%)
  between operations  23.4 us (2%)
    psum x3, waiting for transfers between devices, body(): lax.psum(term_rows(0, model_width), 'samples') + damping[0] * direction  679 us
    psum x3, blocking collectives, centered_weights(): value_mean = lax.psum(jnp.sum(values), 'samples') / sample_count  186 us
    reduce_scatter x1, waiting for transfers between devices, body(): lax.psum_scatter(weighted_term(normed, pullback, (local_energy - energy_m...  114 us
    reduce_scatter x1, waiting for transfers between devices, body(): lax.psum_scatter(lax.dot_general(activated, down_weight, (((1,), (1,)), (...  91.9 us
    all_gather x1, waiting for transfers between devices, body(): force_all = lax.all_gather(force_shard, 'samples', axis=0, tiled=True)  68.4 us
    psum x3, blocking collectives, centered_weights(): values = lax.psum(partial_value, 'mp')  57.8 us
    psum x1, blocking collectives, body(): energy_mean = lax.psum(jnp.sum(local_energy), 'samples') / sample_count  55.2 us
    psum x3, blocking collectives, copy_norm(): return lax.psum(jnp.sum(residual * residual), 'mp')  53.2 us
  transfers between devices with their start and end apart: 7, of which 7 were waited for; matrix products, arithmetic and copies ran while one was open for 0% of the time, Pallas kernels for 0%

commit v1 on v0

v1 whole, which is shorter than its diff:
```python
import jax
import jax.numpy as jnp
from jax import lax
from jax.experimental import pallas as pl
from jax.experimental.pallas import tpu as pltpu
from jax.sharding import PartitionSpec as P

ITERS = 3


gelu_coef = 0.7978845608028654
cubic_coef = 0.044715


def gelu_value(value_in):
    return (
        0.5
        * value_in
        * (1.0 + jnp.tanh(gelu_coef * (value_in + cubic_coef * value_in * value_in * value_in)))
    )


def gelu_slope(value_in):
    inner_tanh = jnp.tanh(gelu_coef * (value_in + cubic_coef * value_in * value_in * value_in))
    return 0.5 * (1.0 + inner_tanh) + 0.5 * value_in * (
        1.0 - inner_tanh * inner_tanh
    ) * gelu_coef * (1.0 + 3.0 * cubic_coef * value_in * value_in)


def encode(value):
    square = value * value
    return jnp.where(value < 0, -square * square, square * square).astype(jnp.bfloat16)


def decode(code):
    code = code.astype(jnp.float32)
    root = lax.rsqrt(lax.rsqrt(jnp.abs(code)))
    root = jnp.where(code == 0, 0.0, root)
    return jnp.where(code < 0, -root, root)


def share(array, axis):
    size = lax.axis_size(axis)
    return lax.all_to_all(jnp.broadcast_to(array, (size,) + array.shape), axis, 0, 0)


def solve_kernel(gram_ref, energy_row_ref, energy_col_ref, damping_ref, coef_ref):
    count = gram_ref.shape[0]
    gram = gram_ref[...]
    gram = gram - jnp.sum(gram, axis=1, keepdims=True) / count
    gram = gram - jnp.sum(gram, axis=0, keepdims=True) / count
    damping = damping_ref[0]

    def center(row, col):
        return (
            (row - jnp.sum(row, axis=1, keepdims=True) / count) / count,
            (col - jnp.sum(col, axis=0, keepdims=True) / count) / count,
        )

    def apply(row, col):
        return jnp.sum(gram * col, axis=0, keepdims=True), jnp.sum(gram * row, axis=1, keepdims=True)

    def inner(row, other):
        return jnp.sum(row * other, axis=1, keepdims=True)

    residual = center(energy_row_ref[...], energy_col_ref[...])
    direction = residual
    solution = jnp.zeros_like(residual[1])
    norm_now = inner(residual[0], apply(*residual)[0])
    for _ in range(ITERS):
        values = apply(*direction)
        weights = center(*values)
        image = tuple(w + damping * d for w, d in zip(weights, direction))
        step_size = norm_now / inner(values[0], image[0])
        solution = solution + step_size * direction[1]
        residual = tuple(r - step_size * i for r, i in zip(residual, image))
        norm_next = inner(residual[0], apply(*residual)[0])
        ratio = norm_next / norm_now
        direction = tuple(r + ratio * d for r, d in zip(residual, direction))
        norm_now = norm_next
    coef_ref[...] = solution


def solve(gram, energy, damping):
    count = energy.shape[0]
    vmem = pl.BlockSpec(memory_space=pltpu.VMEM)
    return pl.pallas_call(
        solve_kernel,
        out_shape=jax.ShapeDtypeStruct((count, 1), jnp.float32),
        in_specs=[vmem, vmem, vmem, pl.BlockSpec(memory_space=pltpu.SMEM)],
        out_specs=vmem,
    )(gram, energy.reshape(1, count), energy.reshape(count, 1), damping)


def body(
    spin_values,
    features,
    spin_embed,
    norm_gain,
    up_weight,
    down_weight,
    readout,
    local_energy,
    damping,
):
    samp_dev, length, model_width = features.shape
    hidden_dev = up_weight.shape[1]
    tokens = samp_dev * length
    samp_size = lax.axis_size("samples")
    mp_size = lax.axis_size("mp")
    sample_count = samp_dev * samp_size
    rows_dev = model_width // samp_size
    share_rows = tokens // mp_size
    with jax.named_scope("forward"):
        inputs = (
            features.astype(jnp.float32)
            + spin_values.astype(jnp.float32)[:, :, None] * spin_embed.astype(jnp.float32)
        ).reshape(tokens, model_width)
        inv_scale = lax.rsqrt(jnp.mean(inputs * inputs, axis=1, keepdims=True) + 1e-05)
        normed = (inputs * inv_scale * norm_gain.astype(jnp.float32)).astype(jnp.bfloat16)
        hidden_pre = jnp.dot(normed, up_weight, preferred_element_type=jnp.float32)
        activated = gelu_value(hidden_pre).astype(jnp.bfloat16)
        mixed_part = lax.dot_general(
            activated, down_weight, (((1,), (1,)), ((), ())), preferred_element_type=jnp.float32
        ).astype(jnp.bfloat16)
    with jax.named_scope("mixed_exchange"):
        mixed_parts = lax.all_to_all(
            mixed_part.reshape(mp_size, share_rows, model_width), "mp", 0, 0
        )
    with jax.named_scope("slope"):
        mixed_rows = jnp.sum(mixed_parts.astype(jnp.float32), axis=0)
        own_inputs = lax.dynamic_slice_in_dim(
            inputs, lax.axis_index("mp") * share_rows, share_rows, 0
        )
        slope_rows = (readout.astype(jnp.float32) * jnp.tanh(own_inputs + mixed_rows)).astype(
            jnp.bfloat16
        )
    with jax.named_scope("slope_share"):
        slope_all = share(slope_rows, "mp").reshape(tokens, model_width)
    with jax.named_scope("pullback"):
        back_proj = jnp.dot(slope_all, down_weight, preferred_element_type=jnp.float32)
        pullback = (gelu_slope(hidden_pre) * back_proj).astype(jnp.bfloat16)
    with jax.named_scope("derivatives"):
        unit = jnp.maximum(jnp.max(jnp.abs(readout.astype(jnp.float32))), 1e-30)
        derivs = lax.dot_general(
            normed.reshape(samp_dev, length, model_width),
            pullback.reshape(samp_dev, length, hidden_dev),
            (((1,), (1,)), ((0,), (0,))),
            preferred_element_type=jnp.float32,
        )
        coded = encode(derivs * (1.0 / unit)).reshape(samp_dev, samp_size, rows_dev, hidden_dev)
        coded = jnp.swapaxes(coded, 0, 1)
    with jax.named_scope("derivative_exchange"):
        coded = lax.all_to_all(coded, "samples", 0, 0)
        coded = coded.reshape(sample_count, rows_dev, hidden_dev)
    with jax.named_scope("gram"):
        half = decode(coded).astype(jnp.bfloat16)
        gram_part = lax.dot_general(
            half, half, (((1, 2), (1, 2)), ((), ())), preferred_element_type=jnp.float32
        )
    with jax.named_scope("gram_sum"):
        gram_rows = sample_count // mp_size
        gram_mp = jnp.sum(
            lax.all_to_all(gram_part.reshape(mp_size, gram_rows, sample_count), "mp", 0, 0), axis=0
        )
        energy_row = lax.dynamic_update_slice(
            jnp.zeros((8, sample_count), jnp.float32),
            local_energy.reshape(1, samp_dev),
            (0, lax.axis_index("samples") * samp_dev),
        )
        summed = jnp.sum(share(jnp.concatenate([gram_mp, energy_row], axis=0), "samples"), axis=0)
        energy = summed[gram_rows]
        gram = share(summed[:gram_rows], "mp").reshape(sample_count, sample_count)
    with jax.named_scope("solve"):
        coef = solve(gram * (unit * unit), energy, damping)
    with jax.named_scope("combine"):
        return unit * jnp.sum(coef[:, :, None] * decode(coded), axis=0)


def solution(mesh):
    in_specs = (
        P("samples", None),
        P("samples", None, None),
        P(),
        P(),
        P(None, "mp"),
        P(None, "mp"),
        P(),
        P("samples"),
        P(),
    )
    out_specs = P("samples", "mp")
    return jax.shard_map(body, mesh=mesh, in_specs=in_specs, out_specs=out_specs, check_vma=False)
```

time: 1440 us -> 257 us (0.18)
  waiting for transfers between devices: 956 us -> 78 us
  blocking collectives: 393 us -> 106 us
  starting transfers between devices: 0.25 us -> 24.2 us
  between operations: 23.4 us -> 1.56 us
  other arithmetic: 33.8 us -> 15.8 us
    psum x3 -> x0, waiting for transfers between devices: 679 us -> none  [body(): lax.psum(term_rows(0, model_width), 'samples') + damping[0] * direction]
    psum x12 -> x0, blocking collectives: 393 us -> none  [the longest x3 186 us: centered_weights(): value_mean = lax.psum(jnp.sum(values), 'samples') / sample_count]
    reduce_scatter x2 -> x0, waiting for transfers between devices: 205 us -> none  [the longest x1 114 us: body(): lax.psum_scatter(weighted_term(normed, pullback, (local_energy - energy_m...]
    all_to_all x0 -> x1, blocking collectives: none -> 106 us  [body(): coded = lax.all_to_all(coded, 'samples', 0, 0)]
    all_to_all x0 -> x5, waiting for transfers between devices: none -> 78 us  [the longest x3 44.2 us: share(): lax.all_to_all(jnp.broadcast_to(array, (size,) + array.shape), axis, 0, 0)]
    all_gather x2 -> x0, waiting for transfers between devices: 71.6 us -> none  [the longest x1 68.4 us: body(): force_all = lax.all_gather(force_shard, 'samples', axis=0, tiled=True)]
    all_to_all x0 -> x5, starting transfers between devices: none -> 24.2 us  [the longest x3 13.2 us: share(): lax.all_to_all(jnp.broadcast_to(array, (size,) + array.shape), axis, 0, 0)]
  transfers between devices with their start and end apart: 7 -> 5, of which waited for: 7 -> 5; matrix products, arithmetic and copies ran while one was open for 0% -> 1% of each run, Pallas kernels for 0% -> 0%
where the time goes in v1:
time: 257 us; the launch traced here: 255 us
  blocking collectives  106 us (41%)
  waiting for transfers between devices  78 us (30%)
  starting transfers between devices  24.2 us (9%)
  matrix products  20.7 us (8%)
  other arithmetic  15.8 us (6%)
  local copies, waits for them, and re-layouts  5.84 us (2%)
  Pallas kernels  2.69 us (1%)
    all_to_all x1, blocking collectives, body(): coded = lax.all_to_all(coded, 'samples', 0, 0)  106 us
    all_to_all x3, waiting for transfers between devices, share(): lax.all_to_all(jnp.broadcast_to(array, (size,) + array.shape), axis, 0, 0)  44.2 us
    all_to_all x1, waiting for transfers between devices, body(): lax.all_to_all(mixed_part.reshape(mp_size, share_rows, model_width), 'mp'...  27.5 us
    all_to_all x3, starting transfers between devices, share(): lax.all_to_all(jnp.broadcast_to(array, (size,) + array.shape), axis, 0, 0)  13.2 us
    dot_general x1, matrix products, body(): lax.dot_general(half, half, (((1, 2), (1, 2)), ((), ())), preferred_eleme...  9.38 us
    all_to_all x1, starting transfers between devices, body(): lax.all_to_all(mixed_part.reshape(mp_size, share_rows, model_width), 'mp'...  7.62 us
    all_to_all x1, waiting for transfers between devices, body(): lax.all_to_all(gram_part.reshape(mp_size, gram_rows, sample_count), 'mp',...  6.31 us
  transfers between devices with their start and end apart: 5, of which 5 were waited for; matrix products, arithmetic and copies ran while one was open for 1% of the time, Pallas kernels for 0%

profile of v1, /device:TPU:1, one launch (start us, length us, event | category | flops | bytes accessed | tf_op | source)
XLA Modules:
  0.0 255.2 jit_solution(13684350743695375242)
XLA Ops:
  0.0 0.8 convert_element_type.60
  0.8 0.7 convert_element_type.61
  1.5 2.5 multiply_reduce_fusion.1
  4.1 1.3 fusion.17
  5.9 2.7 %convolution_convert_fusion = bf16[1024,1024]{1,0:T(8,128)(2,1)} fusion(bf16[1024,512]{1,0:T(8,128)(2,1)S(1)} %copy-done, f32[1024,512]{1,0:T(8,128)S(1)} %fusion.17), kind=kOutput, calls=%fused_computation.37 | convolution fusion | flops 1079508992 | bytes 5242880 | tf_op jit(solution)/shard_map/forward/dot_general | solution.py:123
  8.7 7.6 %all-to-all-start = ((bf16[8,128,1024]{2,1,0:T(8,128)(2,1)}), bf16[8,128,1024]{2,1,0:T(8,128)(2,1)S(1)}, u32[]{:S(2)}, u32[]{:S(2)}) async-start(bf16[8,128,1024]{2,1,0:T(8,128)(2,1)} %bitcast.36), calls=%async_computation | async-start | bytes 4194304 | tf_op jit(solution)/shard_map/mixed_exchange/all_to_all | solution.py:127
  16.3 27.5 %all-to-all-done = bf16[8,128,1024]{2,1,0:T(8,128)(2,1)S(1)} async-done(((bf16[8,128,1024]{2,1,0:T(8,128)(2,1)}), bf16[8,128,1024]{2,1,0:T(8,128)(2,1)S(1)}, u32[]{:S(2)}, u32[]{:S(2)}) %all-to-all-start) | async-done | bytes 2097184 | tf_op jit(solution)/shard_map/mixed_exchange/all_to_all | solution.py:127
  44.2 1.1 multiply_convert_fusion.6
  45.3 1.6 broadcast_in_dim.11
  47.0 3.8 %all-to-all-start.1 = ((bf16[8,128,1024]{2,1,0:T(8,128)(2,1)}), bf16[8,128,1024]{2,1,0:T(8,128)(2,1)S(1)}, u32[]{:S(2)}, u32[]{:S(2)}) async-start(bf16[8,128,1024]{2,1,0:T(8,128)(2,1)} %broadcast_in_dim.11), calls=%async_computation.1 | async-start | bytes 4194304 | tf_op jit(solution)/shard_map/slope_share/all_to_all | solution.py:44
  50.8 0.6 abs_reduce_fusion
  52.1 25.6 %all-to-all-done.1 = bf16[8,128,1024]{2,1,0:T(8,128)(2,1)S(1)} async-done(((bf16[8,128,1024]{2,1,0:T(8,128)(2,1)}), bf16[8,128,1024]{2,1,0:T(8,128)(2,1)S(1)}, u32[]{:S(2)}, u32[]{:S(2)}) %all-to-all-start.1) | async-done | bytes 2097184 | tf_op jit(solution)/shard_map/slope_share/all_to_all | solution.py:44
  77.6 4.0 %fusion.16 = bf16[1024,512]{1,0:T(8,128)(2,1)S(1)} fusion(f32[1024,512]{1,0:T(8,128)} %copy-done.8, bf16[1024,1024]{1,0:T(8,128)(2,1)S(1)} %bitcast.37, bf16[1024,512]{1,0:T(8,128)(2,1)S(1)} %copy-done), kind=kOutput, calls=%fused_computation.30 | convolution fusion | flops 1083703296 | bytes 6291456 | tf_op jit(solution)/shard_map/pullback/dot_general | solution.py:141
  81.6 3.3 %fusion.1 = bf16[4,1024,512]{2,1,0:T(8,128)(2,1)S(1)} fusion(f32[]{:T(128)S(6)} %div.11, bf16[4,256,512]{2,1,0:T(8,128)(2,1)S(1)} %bitcast.41, f32[1024]{0:T(1024)S(1)} %convert_element_type.62, f32[4,256]{1,0:T(4,128)S(1)} %get-tuple-element.9, bf16[4,256,1024]{2,1,0:T(8,128)(2,1)S(1)} %copy-done.3, f32[1024]{0:T(1024)S(1)} %convert_element_type.61, ...), kind=kOutput, calls=%fused_computation.6 | convolution fusion | flops 1096810496 | bytes 7356420 | tf_op jit(solution)/shard_map/derivatives/dot_general | solution.py:145
  84.9 0.6 copy.38
  85.5 106.4 %all_to_all.30 = bf16[32,4,32,512]{3,2,1,0:T(8,128)(2,1)S(1)} all-to-all(bf16[32,4,32,512]{3,2,1,0:T(8,128)(2,1)S(1)} %bitcast.30), channel_id=1, replica_groups=mesh['samples'=32,'mp'=8] {'samples'}, dimensions={0} | all-to-all | bytes 8388608 | tf_op jit(solution)/shard_map/derivative_exchange/all_to_all | solution.py:154
  191.9 2.8 %fusion.5 = bf16[32,4,32,512]{3,2,1,0:T(8,128)(2,1)S(1)} fusion(bf16[32,4,32,512]{3,2,1,0:T(8,128)(2,1)S(1)} %all_to_all.30), kind=kLoop, calls=%fused_computation.11 | loop fusion | flops 16777216 | bytes 8388608 | tf_op jit(solution)/shard_map/gram/convert_element_type | solution.py:157
  194.7 9.4 %fusion.22 = f32[8,16,128]{2,1,0:T(8,128)} fusion(bf16[128,32,512]{2,1,0:T(8,128)(2,1)S(1)} %bitcast.34, bf16[8,16,32,512]{3,2,1,0:T(8,128)(2,1)S(1)} %bitcast.35), kind=kOutput, calls=%fused_computation.38 | convolution fusion | flops 536870912 | bytes 8454144 | tf_op jit(solution)/shard_map/gram/dot_general | solution.py:158
  204.1 3.4 %all-to-all-start.3 = ((f32[8,16,128]{2,1,0:T(8,128)}), f32[8,16,128]{2,1,0:T(8,128)S(1)}, u32[]{:S(2)}, u32[]{:S(2)}) async-start(f32[8,16,128]{2,1,0:T(8,128)} %fusion.22), calls=%async_computation.3 | async-start | bytes 131072 | tf_op jit(solution)/shard_map/gram_sum/all_to_all | solution.py:164
  207.8 6.3 %all-to-all-done.3 = f32[8,16,128]{2,1,0:T(8,128)S(1)} async-done(((f32[8,16,128]{2,1,0:T(8,128)}), f32[8,16,128]{2,1,0:T(8,128)S(1)}, u32[]{:S(2)}, u32[]{:S(2)}) %all-to-all-start.3) | async-done | bytes 65568 | tf_op jit(solution)/shard_map/gram_sum/all_to_all | solution.py:164
  214.1 0.8 broadcast_in_dim.23
  214.9 6.1 %all-to-all-start.4 = ((f32[32,24,128]{2,1,0:T(8,128)}), f32[32,24,128]{2,1,0:T(8,128)S(1)}, u32[]{:S(2)}, u32[]{:S(2)}) async-start(f32[32,24,128]{2,1,0:T(8,128)} %broadcast_in_dim.23), calls=%async_computation.4 | async-start | bytes 786432 | tf_op jit(solution)/shard_map/gram_sum/all_to_all | solution.py:44
  221.6 13.3 %all-to-all-done.4 = f32[32,24,128]{2,1,0:T(8,128)S(1)} async-done(((f32[32,24,128]{2,1,0:T(8,128)}), f32[32,24,128]{2,1,0:T(8,128)S(1)}, u32[]{:S(2)}, u32[]{:S(2)}) %all-to-all-start.4) | async-done | bytes 393248 | tf_op jit(solution)/shard_map/gram_sum/all_to_all | solution.py:44
  234.9 0.6 broadcast_in_dim.24
  235.5 3.4 %all-to-all-start.5 = ((f32[8,16,128]{2,1,0:T(8,128)}), f32[8,16,128]{2,1,0:T(8,128)S(1)}, u32[]{:S(2)}, u32[]{:S(2)}) async-start(f32[8,16,128]{2,1,0:T(8,128)} %broadcast_in_dim.24), calls=%async_computation.5 | async-start | bytes 131072 | tf_op jit(solution)/shard_map/gram_sum/all_to_all | solution.py:44
  239.4 0.7 copy.23.energy_col_ref
  240.1 5.4 %all-to-all-done.5 = f32[8,16,128]{2,1,0:T(8,128)S(1)} async-done(((f32[8,16,128]{2,1,0:T(8,128)}), f32[8,16,128]{2,1,0:T(8,128)S(1)}, u32[]{:S(2)}, u32[]{:S(2)}) %all-to-all-start.5) | async-done | bytes 65568 | tf_op jit(solution)/shard_map/gram_sum/all_to_all | solution.py:44
  245.5 0.6 broadcast_multiply_fusion
  246.1 2.7 %solve.1 = f32[128,1]{1,0:T(8,128)} custom-call(f32[128,128]{1,0:T(8,128)} %bitcast.38, f32[1,128]{1,0:T(1,128)} %get-tuple-element.8.energy_row_ref, f32[128,1]{1,0:T(8,128)} %copy.23.energy_col_ref, f32[1]{0:T(128)S(6)} %copy.40.damping_ref), custom_call_target="tpu_custom_call" | custom-call | tf_op jit(solution)/shard_map/solve/pallas_call | solution.py:87
  248.8 0.9 reduce.2
  249.9 4.6 %multiply_reduce_fusion = f32[32,512]{1,0:T(8,128)S(1)} fusion(bf16[32,4,32,512]{3,2,1,0:T(8,128)(2,1)} %copy-done.1, f32[32,4]{1,0:T(8,128)S(1)} %mul.191), kind=kLoop, calls=%fused_computation.10 | loop fusion | flops 18857984 | bytes 4260352 | tf_op jit(solution)/shard_map/combine/reduce_sum | solution.py:177
  254.6 0.6 broadcast_multiply_fusion.1
  (31 shorter events, 1.9 us)
Async XLA Ops:
  0.0 5.9 %copy-start = (bf16[1024,512]{1,0:T(8,128)(2,1)S(1)}, bf16[1024,512]{1,0:T(8,128)(2,1)}, u32[]{:S(2)}) copy-start(bf16[1024,512]{1,0:T(8,128)(2,1)} %param.14) | copy-start | bytes 3145732
  0.0 4.0 %copy-start.5 = (bf16[1024]{0:T(1024)(128)(2,1)S(1)}, bf16[1024]{0:T(1024)(128)(2,1)}, u32[]{:S(2)}) copy-start(bf16[1024]{0:T(1024)(128)(2,1)} %param.12) | copy-start | bytes 6148
  0.0 4.1 %copy-start.7 = (bf16[1024,512]{1,0:T(8,128)(2,1)S(1)}, bf16[1024,512]{1,0:T(8,128)(2,1)}, u32[]{:S(2)}) copy-start(bf16[1024,512]{1,0:T(8,128)(2,1)} %param.13) | copy-start | bytes 3145732
  4.0 1.9 copy-start.2
  5.9 2.8 %copy-start.8 = (f32[1024,512]{1,0:T(8,128)}, f32[1024,512]{1,0:T(8,128)S(1)}, u32[]{:S(2)}) copy-start(f32[1024,512]{1,0:T(8,128)S(1)} %fusion.17) | copy-start | bytes 6291460
  8.7 7.6 %copy-start.4 = (bf16[1024]{0:T(1024)(128)(2,1)S(1)}, bf16[1024]{0:T(1024)(128)(2,1)}, u32[]{:S(2)}) copy-start(bf16[1024]{0:T(1024)(128)(2,1)} %param.15) | copy-start | bytes 6148
  8.7 35.1 %all-to-all-start = ((bf16[8,128,1024]{2,1,0:T(8,128)(2,1)}), bf16[8,128,1024]{2,1,0:T(8,128)(2,1)S(1)}, u32[]{:S(2)}, u32[]{:S(2)}) async-start(bf16[8,128,1024]{2,1,0:T(8,128)(2,1)} %bitcast.36), calls=%async_computation | async-start | bytes 4194304 | tf_op jit(solution)/shard_map/mixed_exchange/all_to_all | solution.py:127
  47.0 30.7 %all-to-all-start.1 = ((bf16[8,128,1024]{2,1,0:T(8,128)(2,1)}), bf16[8,128,1024]{2,1,0:T(8,128)(2,1)S(1)}, u32[]{:S(2)}, u32[]{:S(2)}) async-start(bf16[8,128,1024]{2,1,0:T(8,128)(2,1)} %broadcast_in_dim.11), calls=%async_computation.1 | async-start | bytes 4194304 | tf_op jit(solution)/shard_map/slope_share/all_to_all | solution.py:44
  77.6 4.0 %copy-start.3 = (bf16[4,256,1024]{2,1,0:T(8,128)(2,1)S(1)}, bf16[4,256,1024]{2,1,0:T(8,128)(2,1)}, u32[]{:S(2)}) copy-start(bf16[4,256,1024]{2,1,0:T(8,128)(2,1)} %param.10) | copy-start | bytes 6291460
  191.9 2.8 %copy-start.1 = (bf16[32,4,32,512]{3,2,1,0:T(8,128)(2,1)}, bf16[32,4,32,512]{3,2,1,0:T(8,128)(2,1)S(1)}, u32[]{:S(2)}) copy-start(bf16[32,4,32,512]{3,2,1,0:T(8,128)(2,1)S(1)} %all_to_all.30) | copy-start | bytes 12582916
  194.7 12.8 %copy-start.6 = (f32[4]{0:T(128)S(1)}, f32[4]{0:T(128)}, u32[]{:S(2)}) copy-start(f32[4]{0:T(128)} %param.16) | copy-start | bytes 52
  204.1 10.0 %all-to-all-start.3 = ((f32[8,16,128]{2,1,0:T(8,128)}), f32[8,16,128]{2,1,0:T(8,128)S(1)}, u32[]{:S(2)}, u32[]{:S(2)}) async-start(f32[8,16,128]{2,1,0:T(8,128)} %fusion.22), calls=%async_computation.3 | async-start | bytes 131072 | tf_op jit(solution)/shard_map/gram_sum/all_to_all | solution.py:164
  214.9 20.0 %all-to-all-start.4 = ((f32[32,24,128]{2,1,0:T(8,128)}), f32[32,24,128]{2,1,0:T(8,128)S(1)}, u32[]{:S(2)}, u32[]{:S(2)}) async-start(f32[32,24,128]{2,1,0:T(8,128)} %broadcast_in_dim.23), calls=%async_computation.4 | async-start | bytes 786432 | tf_op jit(solution)/shard_map/gram_sum/all_to_all | solution.py:44
  235.5 10.0 %all-to-all-start.5 = ((f32[8,16,128]{2,1,0:T(8,128)}), f32[8,16,128]{2,1,0:T(8,128)S(1)}, u32[]{:S(2)}, u32[]{:S(2)}) async-start(f32[8,16,128]{2,1,0:T(8,128)} %broadcast_in_dim.24), calls=%async_computation.5 | async-start | bytes 131072 | tf_op jit(solution)/shard_map/gram_sum/all_to_all | solution.py:44

commit v2 on v1

v2 whole, which is shorter than its diff:
```python
import jax
import jax.numpy as jnp
from jax import lax
from jax.experimental import pallas as pl
from jax.experimental.pallas import tpu as pltpu
from jax.sharding import PartitionSpec as P

ITERS = 3
CHUNKS = (2, 2)
VMEM_LIMIT = 60 * 1024 * 1024
VMEM_SMALL = 32 * 1024 * 1024
SAMPLES = ("z", "x_lo", "core")
MP = ("y", "x_hi")
NEAR = ("x_lo", "core", "y")
FAR = ("z", "x_hi")


gelu_coef = 0.7978845608028654
cubic_coef = 0.044715


def encode(value):
    square = value * value
    return jnp.where(value < 0, -square * square, square * square).astype(jnp.bfloat16)


def decode(code):
    code = code.astype(jnp.float32)
    root = lax.rsqrt(lax.rsqrt(jnp.abs(code)))
    root = jnp.where(code == 0, 0.0, root)
    return jnp.where(code < 0, -root, root)


def share(array, axis):
    size = lax.axis_size(axis)
    return lax.all_to_all(jnp.broadcast_to(array, (size,) + array.shape), axis, 0, 0)


VMEM = pl.BlockSpec(memory_space=pltpu.VMEM)
SMEM = pl.BlockSpec(memory_space=pltpu.SMEM)


def forward_kernel(scalar_ref, spin_ref, feature_ref, embed_ref, gain_ref, up_ref, down_ref, *refs):
    normed_ref, own_ref, bend_ref, *part_refs = refs
    blocks, rows, width = feature_ref.shape[1:]
    order = scalar_ref[0]
    own_block = jnp.bitwise_xor(order, scalar_ref[1])
    spin_row = spin_ref[pl.ds(scalar_ref[2] + pl.program_id(0), 1)].astype(jnp.float32)
    offset = lax.broadcasted_iota(jnp.int32, (rows, blocks * rows), 1) - lax.broadcasted_iota(
        jnp.int32, (rows, blocks * rows), 0
    )
    embed = embed_ref[...].astype(jnp.float32).reshape(1, width)
    gain = gain_ref[...].astype(jnp.float32).reshape(1, width)

    def block_inputs(block):
        spin_col = jnp.sum(jnp.where(offset == block * rows, spin_row, 0.0), axis=1, keepdims=True)
        return feature_ref[0, block].astype(jnp.float32) + spin_col * embed

    own_ref[0] = block_inputs(scalar_ref[1])
    for k in range(blocks):
        inputs = block_inputs(jnp.bitwise_xor(order, k))
        inv_scale = lax.rsqrt(jnp.mean(inputs * inputs, axis=1, keepdims=True) + 1e-05)
        normed_ref[0, k * rows : (k + 1) * rows] = (inputs * inv_scale * gain).astype(jnp.bfloat16)
    hidden_pre = jnp.dot(normed_ref[0], up_ref[...], preferred_element_type=jnp.float32)
    square = hidden_pre * hidden_pre
    inner_tanh = jnp.tanh(gelu_coef * (hidden_pre + cubic_coef * square * hidden_pre))
    activated = (0.5 * hidden_pre * (1.0 + inner_tanh)).astype(jnp.bfloat16)
    bend_ref[0] = 0.5 * (1.0 + inner_tanh) + 0.5 * hidden_pre * (
        1.0 - inner_tanh * inner_tanh
    ) * gelu_coef * (1.0 + 3.0 * cubic_coef * square)
    mixed = lax.dot_general(
        activated, down_ref[...], (((1,), (1,)), ((), ())), preferred_element_type=jnp.float32
    ).astype(jnp.bfloat16)
    for k in range(blocks):
        part = mixed[k * rows : (k + 1) * rows]
        if len(part_refs) == 1:
            part_refs[0][k, 0] = part
        else:
            part_refs[k][0] = part


def forward(order, own, spins, features, embed, gain, up, down, first, samples, apart):
    _, blocks, rows, width = features.shape
    hidden = up.shape[1]
    tokens = blocks * rows
    whole = lambda array: pl.BlockSpec(array.shape, lambda s: (0,) * array.ndim)
    block = lambda *shape: pl.BlockSpec((1,) + shape, lambda s: (s,) + (0,) * len(shape))
    result = lambda dtype, *shape: jax.ShapeDtypeStruct((samples,) + shape, dtype)
    if not apart:
        part_specs = [pl.BlockSpec((blocks, 1, rows, width), lambda s: (0, s, 0, 0))]
        part_shapes = [jax.ShapeDtypeStruct((blocks, samples, rows, width), jnp.bfloat16)]
    else:
        part_specs = [block(rows, width)] * blocks
        part_shapes = [result(jnp.bfloat16, rows, width)] * blocks
    scalars = jnp.stack([order, own, jnp.int32(first)])
    return pl.pallas_call(
        forward_kernel,
        grid=(samples,),
        in_specs=[
            SMEM,
            whole(spins),
            pl.BlockSpec((1, blocks, rows, width), lambda s: (s + first, 0, 0, 0)),
            whole(embed),
            whole(gain),
            whole(up),
            whole(down),
        ],
        out_specs=[block(tokens, width), block(rows, width), block(tokens, hidden)] + part_specs,
        out_shape=[
            result(jnp.bfloat16, tokens, width),
            result(jnp.float32, rows, width),
            result(jnp.float32, tokens, hidden),
        ]
        + part_shapes,
        compiler_params=pltpu.CompilerParams(vmem_limit_bytes=VMEM_LIMIT if first == 0 else VMEM_SMALL),
    )(scalars, spins, features, embed, gain, up, down)


def slope_kernel(part_ref, own_ref, readout_ref, *refs):
    slope_ref = refs[-1]
    blocks, samples, rows, width = part_ref.shape
    readout = readout_ref[...].astype(jnp.float32).reshape(1, width)
    for s in range(samples):
        outputs = own_ref[s]
        for k in range(blocks):
            outputs = outputs + part_ref[k, s].astype(jnp.float32)
        slope = (readout * jnp.tanh(outputs)).astype(jnp.bfloat16)
        for k in range(blocks):
            slope_ref[k, s] = slope


def own_slope(parts, own, readout, after):
    return pl.pallas_call(
        slope_kernel,
        out_shape=jax.ShapeDtypeStruct(parts.shape, parts.dtype),
        in_specs=[VMEM] * 3 + [pl.BlockSpec(memory_space=pl.ANY)] * len(after),
        out_specs=VMEM,
        compiler_params=pltpu.CompilerParams(vmem_limit_bytes=VMEM_SMALL),
    )(parts, own, readout, *after)


def derivative_kernel(scale_ref, normed_ref, bend_ref, down_ref, *refs):
    slope_refs, coded_ref = refs[:-1], refs[-1]
    tokens, width = normed_ref.shape[1:]
    if len(slope_refs) == 1:
        slope = slope_refs[0][:, 0].reshape(tokens, width)
    else:
        slope = jnp.concatenate([r[0] for r in slope_refs], axis=0)
    back_proj = jnp.dot(slope, down_ref[...], preferred_element_type=jnp.float32)
    pullback = (bend_ref[0] * back_proj).astype(jnp.bfloat16)
    deriv = lax.dot_general(
        normed_ref[0], pullback, (((0,), (0,)), ((), ())), preferred_element_type=jnp.float32
    )
    coded = encode(deriv * scale_ref[0])
    coded_ref[:, 0] = coded.reshape(coded_ref.shape[0], coded_ref.shape[2], coded_ref.shape[3])


def derivative(scale, normed, bend, down, slopes, parts):
    samples, tokens, width = normed.shape
    hidden = down.shape[1]
    block = lambda *shape: pl.BlockSpec((1,) + shape, lambda s: (s,) + (0,) * len(shape))
    return pl.pallas_call(
        derivative_kernel,
        grid=(samples,),
        in_specs=[
            SMEM,
            block(tokens, width),
            block(tokens, hidden),
            pl.BlockSpec(down.shape, lambda s: (0, 0)),
        ]
        + [
            block(*a.shape[1:])
            if a.ndim == 3
            else pl.BlockSpec((a.shape[0], 1) + a.shape[2:], lambda s: (0, s, 0, 0))
            for a in slopes
        ],
        out_specs=pl.BlockSpec((parts, 1, width // parts, hidden), lambda s: (0, s, 0, 0)),
        out_shape=jax.ShapeDtypeStruct((parts, samples, width // parts, hidden), jnp.bfloat16),
        compiler_params=pltpu.CompilerParams(vmem_limit_bytes=VMEM_SMALL),
    )(scale, normed, bend, down, *slopes)


def widen(code_ref, wide_ref):
    count, rows, lanes = code_ref.shape
    for n in range(0, count, 8):
        wide_ref[0, n * rows : (n + 8) * rows] = decode(code_ref[n : n + 8]).reshape(8 * rows, lanes)


def row_of_all(wide_ref, row, rows):
    count = wide_ref.shape[1] // rows
    return wide_ref[0, pl.ds(row, count, stride=rows)].astype(jnp.bfloat16)


def rows_first_kernel(code_ref, half_ref, wide_ref):
    rows = code_ref.shape[1]
    widen(code_ref, wide_ref)
    for r in range(rows):
        half_ref[r] = row_of_all(wide_ref, r, rows)


LANES = 128


def wide_out(count, rows, width):
    return (
        pl.BlockSpec((1, count * rows, LANES), lambda f: (f, 0, 0)),
        jax.ShapeDtypeStruct((width // LANES, count * rows, LANES), jnp.float32),
    )


def rows_first(code):
    count, rows, width = code.shape
    wide_spec, wide_shape = wide_out(count, rows, width)
    return pl.pallas_call(
        rows_first_kernel,
        grid=(width // LANES,),
        in_specs=[pl.BlockSpec((count, rows, LANES), lambda f: (0, 0, f))],
        out_specs=[pl.BlockSpec((rows, count, LANES), lambda f: (0, 0, f)), wide_spec],
        out_shape=[jax.ShapeDtypeStruct((rows, count, width), jnp.bfloat16), wide_shape],
        compiler_params=pltpu.CompilerParams(vmem_limit_bytes=VMEM_SMALL),
    )(code)


def gram_kernel(energy_ref, code_ref, *refs):
    half_refs, gram_ref, wide_ref = refs[:-2], refs[-2], refs[-1]
    rows = code_ref.shape[1]
    widen(code_ref, wide_ref)
    gram = jnp.zeros(gram_ref.shape, jnp.float32)
    for r in range(0, rows, 4):
        half = jnp.concatenate(
            [
                jnp.concatenate([h[q] for h in half_refs] + [row_of_all(wide_ref, q, rows)], axis=0)
                for q in range(r, r + 4)
            ],
            axis=1,
        )
        gram += lax.dot_general(half, half, (((1,), (1,)), ((), ())), preferred_element_type=jnp.float32)

    @pl.when(pl.program_id(0) == 0)
    def _():
        gram_ref[...] = gram

    @pl.when(pl.program_id(0) > 0)
    def _():
        gram_ref[...] += gram

    @pl.when(pl.program_id(0) == pl.num_programs(0) - 1)
    def _():
        total = gram_ref[...]
        size = total.shape[0]
        row = lax.broadcasted_iota(jnp.int32, total.shape, 0)
        col = lax.broadcasted_iota(jnp.int32, total.shape, 1)
        energy = energy_ref[...]
        total = jnp.where((row == size - 1) & (col < size - 1), energy, total)
        last_energy = jnp.sum(jnp.where(col[:1] == size - 1, energy, 0.0), axis=1, keepdims=True)
        gram_ref[...] = jnp.where((row == size - 2) & (col == 0), last_energy, total)


def gram_matrix(energy, code, halves):
    count, rows, width = code.shape
    size = energy.shape[1]
    wide_spec, wide_shape = wide_out(count, rows, width)
    return pl.pallas_call(
        gram_kernel,
        grid=(width // LANES,),
        in_specs=[
            pl.BlockSpec(energy.shape, lambda f: (0, 0)),
            pl.BlockSpec((count, rows, LANES), lambda f: (0, 0, f)),
        ]
        + [pl.BlockSpec(h.shape[:2] + (LANES,), lambda f: (0, 0, f)) for h in halves],
        out_specs=[pl.BlockSpec((size, size), lambda f: (0, 0)), wide_spec],
        out_shape=[jax.ShapeDtypeStruct((size, size), jnp.float32), wide_shape],
        compiler_params=pltpu.CompilerParams(vmem_limit_bytes=VMEM_LIMIT),
    )(energy, code, *halves)


def solve_kernel(scalar_ref, shared_ref, *refs):
    chunk_count = (len(refs) - 4) // 2
    far_refs, out_ref, gram_ref, spread_ref = refs[:chunk_count], *refs[chunk_count : chunk_count + 3]
    chunk_refs, sems = refs[chunk_count + 3 : -1], refs[-1]
    copies = [
        pltpu.make_async_copy(far, near, sems.at[n])
        for n, (far, near) in enumerate(zip(far_refs, chunk_refs))
    ]
    for copy in copies:
        copy.start()
    count = gram_ref.shape[0]
    gram_rows = shared_ref.shape[1]
    damping, unit = scalar_ref[0], scalar_ref[1]
    for device in range(shared_ref.shape[0]):
        gram_ref[device * gram_rows : (device + 1) * gram_rows] = shared_ref[device]
    row = lax.broadcasted_iota(jnp.int32, (count, count), 0)
    col = lax.broadcasted_iota(jnp.int32, (count, count), 1)
    gram = gram_ref[...]
    energy_row = jnp.where(
        col[:1] == count - 1, gram_ref[count - 2 : count - 1, 0:1], gram_ref[count - 1 : count]
    )
    energy_col = jnp.sum(jnp.where(row == col, energy_row, 0.0), axis=1, keepdims=True)
    gram = jnp.where(row <= col, gram, gram.T) * (unit * unit)
    gram = gram - jnp.sum(gram, axis=1, keepdims=True) / count
    gram = gram - jnp.sum(gram, axis=0, keepdims=True) / count

    def center(row, col):
        return (
            (row - jnp.sum(row, axis=1, keepdims=True) / count) / count,
            (col - jnp.sum(col, axis=0, keepdims=True) / count) / count,
        )

    def apply(row, col):
        return jnp.sum(gram * col, axis=0, keepdims=True), jnp.sum(gram * row, axis=1, keepdims=True)

    def inner(row, other):
        return jnp.sum(row * other, axis=1, keepdims=True)

    residual = center(energy_row, energy_col)
    direction = residual
    coef = jnp.zeros_like(residual[1])
    norm_now = inner(residual[0], apply(*residual)[0])
    for iteration in range(ITERS):
        values = apply(*direction)
        weights = center(*values)
        image = tuple(w + damping * d for w, d in zip(weights, direction))
        step_size = norm_now / inner(values[0], image[0])
        coef = coef + step_size * direction[1]
        if iteration < ITERS - 1:
            residual = tuple(r - step_size * i for r, i in zip(residual, image))
            norm_next = inner(residual[0], apply(*residual)[0])
            ratio = norm_next / norm_now
            direction = tuple(r + ratio * d for r, d in zip(residual, direction))
            norm_now = norm_next
    spread_ref[...] = jnp.broadcast_to(coef * unit, spread_ref.shape)
    for copy in copies:
        copy.wait()
    rows, width = out_ref.shape
    lanes = spread_ref.shape[1]
    for f in range(width // lanes):
        total = jnp.zeros((rows, lanes), jnp.float32)
        first = 0
        for chunk_ref in chunk_refs:
            samples = chunk_ref.shape[1] // rows

            def add(s, total):
                start = pl.multiple_of(s * rows, rows)
                return total + spread_ref[pl.ds(first + s, 1)] * chunk_ref[f, pl.ds(start, rows)]

            total = lax.fori_loop(0, samples, add, total, unroll=8)
            first += samples
        out_ref[:, f * lanes : (f + 1) * lanes] = total


def solve(scalars, shared, chunks, rows):
    count = shared.shape[2]
    return pl.pallas_call(
        solve_kernel,
        out_shape=jax.ShapeDtypeStruct((rows, chunks[0].shape[0] * chunks[0].shape[2]), jnp.float32),
        in_specs=[SMEM, VMEM] + [pl.BlockSpec(memory_space=pl.ANY)] * len(chunks),
        out_specs=VMEM,
        scratch_shapes=[
            pltpu.VMEM((count, count), jnp.float32),
            pltpu.VMEM((count, LANES), jnp.float32),
        ]
        + [pltpu.VMEM(c.shape, c.dtype) for c in chunks]
        + [pltpu.SemaphoreType.DMA((len(chunks),))],
        compiler_params=pltpu.CompilerParams(vmem_limit_bytes=VMEM_LIMIT),
    )(scalars, shared, *chunks)


def body(
    spin_values,
    features,
    spin_embed,
    norm_gain,
    up_weight,
    down_weight,
    readout,
    local_energy,
    damping,
):
    samp_dev, length, model_width = features.shape
    hidden_dev = up_weight.shape[1]
    samp_size = lax.axis_size(SAMPLES)
    mp_size = lax.axis_size(MP)
    sample_count = samp_dev * samp_size
    rows_dev = model_width // samp_size
    share_rows = length // mp_size
    place = lax.axis_index(MP).astype(jnp.int32)
    readout_wide = readout.astype(jnp.float32)
    unit = jnp.maximum(jnp.max(jnp.abs(readout_wide)), 1e-30).reshape(1)
    feature_blocks = features.reshape(samp_dev, mp_size, share_rows, model_width)

    def partner(array, k):
        return lax.ppermute(array, MP, [(i, i ^ k) for i in range(mp_size)])

    with jax.named_scope("energy"):
        energy_row = jnp.zeros((1, sample_count), jnp.float32)
        first = 0
        for samples in CHUNKS:
            energy_row = lax.dynamic_update_slice(
                energy_row,
                local_energy[first : first + samples].reshape(1, samples),
                (0, first * samp_size + lax.axis_index(SAMPLES) * samples),
            )
            first += samples
        energy_row = jnp.where(place == 0, energy_row, 0.0)

    states = []
    first = 0
    for n, samples in enumerate(CHUNKS):
        with jax.named_scope("forward"):
            states.append(
                forward(
                    place if n else jnp.int32(0),
                    place,
                    spin_values,
                    feature_blocks,
                    spin_embed,
                    norm_gain,
                    up_weight,
                    down_weight,
                    first,
                    samples,
                    n > 0,
                )
            )
        first += samples
    coded_chunks = []
    for n, (normed, own_inputs, bend, *parts) in enumerate(states):
        with jax.named_scope("mixed_exchange"):
            if n == 0:
                mixed_parts = lax.all_to_all(parts[0], MP, 0, 0)
            else:
                mixed_parts = parts[:1] + [partner(parts[k], k) for k in range(1, mp_size)]
        with jax.named_scope("slope"):
            if n == 0:
                slope = own_slope(mixed_parts, own_inputs, readout, [s[1] for s in states[1:2]])
            else:
                outputs = own_inputs
                for part in mixed_parts:
                    outputs = outputs + part.astype(jnp.float32)
                slope = (readout_wide * jnp.tanh(outputs)).astype(jnp.bfloat16)
        with jax.named_scope("slope_share"):
            if n == 0:
                slopes = [lax.all_to_all(slope, MP, 0, 0)]
            else:
                slopes = [slope] + [partner(slope, k) for k in range(1, mp_size)]
        with jax.named_scope("derivatives"):
            coded_chunks.append(
                derivative(1.0 / unit, normed, bend, down_weight, slopes, samp_size)
            )
    with jax.named_scope("derivative_exchange"):
        chunks = [lax.all_to_all(c, SAMPLES, 0, 0) for c in coded_chunks]
        chunks = [c.reshape(-1, rows_dev, hidden_dev) for c in chunks]
    with jax.named_scope("gram"):
        halves, wides = zip(*[rows_first(c) for c in chunks[:-1]])
        gram_part, last_wide = gram_matrix(energy_row, chunks[-1], halves)
        wides = wides + (last_wide,)
    with jax.named_scope("gram_sum"):
        near_size = lax.axis_size(NEAR)
        blocks = lax.all_to_all(
            gram_part.reshape(near_size, sample_count // near_size, sample_count), NEAR, 0, 0
        )
        blocks = share(jnp.sum(blocks, axis=0), FAR)
        shared = share(jnp.sum(blocks, axis=0), NEAR)
    with jax.named_scope("solve"):
        return solve(jnp.concatenate([damping, unit]), shared, wides, rows_dev)


def solution(mesh):
    samples, mp = mesh.devices.shape
    fine = jax.sharding.Mesh(
        mesh.devices.reshape(samples // 4, 2, 2, mp // 2, 2), SAMPLES + MP
    )
    in_specs = (
        P(SAMPLES, None),
        P(SAMPLES, None, None),
        P(),
        P(),
        P(None, MP),
        P(None, MP),
        P(),
        P(SAMPLES),
        P(),
    )
    out_specs = P(SAMPLES, MP)
    return jax.shard_map(body, mesh=fine, in_specs=in_specs, out_specs=out_specs, check_vma=False)
```

time: 257 us -> 236 us (0.918)
  blocking collectives: 106 us -> 10.8 us
  starting transfers between devices: 24.2 us -> 65.7 us
  Pallas kernels: 2.69 us -> 35.7 us
  waiting for transfers between devices: 78 us -> 101 us
  matrix products: 20.7 us -> 0 us
  other arithmetic: 15.8 us -> 2.69 us
  local copies, waits for them, and re-layouts: 5.84 us -> 17.5 us
    all_to_all x1, blocking collectives: 106 us -> 10.8 us  [body(): lax.all_to_all(gram_part.reshape(near_size, sample_count // near_size, sa...]
    pallas_call x1 -> x8, Pallas kernels: 2.69 us -> 35.7 us  [the longest x2 8.75 us: forward(): pl.pallas_call(forward_kernel, grid=(samples,), in_specs=[SMEM, whole(spi...]
    all_to_all x3 -> x2, waiting for transfers between devices: 44.2 us -> 14 us  [share(): lax.all_to_all(jnp.broadcast_to(array, (size,) + array.shape), axis, 0, 0)]
    ppermute x0 -> x14, waiting for transfers between devices: none -> 26.9 us  [partner(): return lax.ppermute(array, MP, [(i, i ^ k) for i in range(mp_size)])]
    all_to_all x2 -> x4, waiting for transfers between devices: 33.8 us -> 59.7 us  [the longest x2 41.1 us: body(): chunks = [lax.all_to_all(c, SAMPLES, 0, 0) for c in coded_chunks]]
    ppermute x0 -> x14, starting transfers between devices: none -> 22.7 us  [partner(): return lax.ppermute(array, MP, [(i, i ^ k) for i in range(mp_size)])]
    all_to_all x2 -> x4, starting transfers between devices: 11 us -> 33 us  [the longest x2 21.2 us: body(): chunks = [lax.all_to_all(c, SAMPLES, 0, 0) for c in coded_chunks]]
    dot_general x5 -> x0, matrix products: 20.7 us -> none  [the longest x1 9.38 us: body(): lax.dot_general(half, half, (((1, 2), (1, 2)), ((), ())), preferred_eleme...]
  transfers between devices with their start and end apart: 5 -> 20, of which waited for: 5 -> 14; matrix products, arithmetic and copies ran while one was open for 1% -> 1% of each run, Pallas kernels for 0% -> 5%
where the time goes in v2:
time: 236 us; the launch traced here: 235 us
  waiting for transfers between devices  101 us (43%)
  starting transfers between devices  65.7 us (28%)
  Pallas kernels  35.7 us (15%)
  local copies, waits for them, and re-layouts  17.5 us (7%)
  blocking collectives  10.8 us (5%)
  other arithmetic  2.69 us (1%)
    all_to_all x2, waiting for transfers between devices, body(): chunks = [lax.all_to_all(c, SAMPLES, 0, 0) for c in coded_chunks]  41.1 us
    ppermute x14, waiting for transfers between devices, partner(): return lax.ppermute(array, MP, [(i, i ^ k) for i in range(mp_size)])  26.9 us
    ppermute x14, starting transfers between devices, partner(): return lax.ppermute(array, MP, [(i, i ^ k) for i in range(mp_size)])  22.7 us
    all_to_all x2, starting transfers between devices, body(): chunks = [lax.all_to_all(c, SAMPLES, 0, 0) for c in coded_chunks]  21.2 us
    unnamed x52, local copies, waits for them, and re-layouts  15.7 us
    all_to_all x1, waiting for transfers between devices, body(): slopes = [lax.all_to_all(slope, MP, 0, 0)]  14.1 us
    all_to_all x2, waiting for transfers between devices, share(): lax.all_to_all(jnp.broadcast_to(array, (size,) + array.shape), axis, 0, 0)  14 us
    all_to_all x1, blocking collectives, body(): lax.all_to_all(gram_part.reshape(near_size, sample_count // near_size, sa...  10.8 us
  transfers between devices with their start and end apart: 20, of which 14 were waited for; matrix products, arithmetic and copies ran while one was open for 1% of the time, Pallas kernels for 5%

profile of v2, /device:TPU:1, one launch (start us, length us, event | category | flops | bytes accessed | tf_op | source)
XLA Modules:
  0.0 234.7 jit_solution(5273767598104270934)
XLA Ops:
  0.6 5.6 %forward.3 = (bf16[2,256,1024]{2,1,0:T(8,128)(2,1)}, f32[2,32,1024]{2,1,0:T(8,128)}, f32[2,256,512]{2,1,0:T(8,128)}, bf16[8,2,32,1024]{3,2,1,0:T(8,128)(2,1)}) custom-call(s32[3]{0:T(128)} %get-tuple-element.46.scalar_ref, s32[4,256]{1,0:T(4,128)} %spin_ref.3, bf16[4,8,32,1024]{3,2,1,0:T(8,128)(2,1)} %bitcast.10, bf16[1024]{0:T(1024)(128)(2,1)} %embed_ref.3, ...), custom_call_target="tpu_custom_call" | custom-call | tf_op jit(solution)/shard_map/forward/pallas_call | solution.py:96
  6.2 7.6 %all-to-all-start.1 = ((bf16[8,2,32,1024]{3,2,1,0:T(8,128)(2,1)}), bf16[8,2,32,1024]{3,2,1,0:T(8,128)(2,1)}, u32[]{:S(2)}, u32[]{:S(2)}) async-start(bf16[8,2,32,1024]{3,2,1,0:T(8,128)(2,1)} %get-tuple-element.37), calls=%async_computation.1 | async-start | bytes 2097152 | tf_op jit(solution)/shard_map/mixed_exchange/all_to_all | solution.py:430
  15.8 3.2 %forward.2 = (bf16[2,256,1024]{2,1,0:T(8,128)(2,1)S(1)}, f32[2,32,1024]{2,1,0:T(8,128)S(1)}, f32[2,256,512]{2,1,0:T(8,128)S(1)}, bf16[2,32,1024]{2,1,0:T(8,128)(...) custom-call(s32[3]{0:T(128)S(1)} %copy-done.16, ...), custom_call_target="tpu_custom_call" | custom-call | tf_op jit(solution)/shard_map/forward/pallas_call | solution.py:96
  25.4 4.5 %all-to-all-done.1.part_ref = bf16[8,2,32,1024]{3,2,1,0:T(8,128)(2,1)} async-done(((bf16[8,2,32,1024]{3,2,1,0:T(8,128)(2,1)}), bf16[8,2,32,1024]{3,2,1,0:T(8,128)(2,1)}, u32[]{:S(2)}, u32[]{:S(2)}) %all-to-all-start.1) | async-done | bytes 1048608 | tf_op jit(solution)/shard_map/mixed_exchange/all_to_all | solution.py:430
  30.9 2.5 %slope.1 = bf16[8,2,32,1024]{3,2,1,0:T(8,128)(2,1)} custom-call(bf16[8,2,32,1024]{3,2,1,0:T(8,128)(2,1)} %all-to-all-done.1.part_ref, f32[2,32,1024]{2,1,0:T(8,128)S(1)} %copy-done.11, bf16[1024]{0:T(1024)(128)(2,1)S(1)} %copy-done.12, f32[2,32,1024]{2,1,0:T(8,128)S(1)} %get-tuple-element.26.refs_0_), custom_call_target="tpu_custom_call" | custom-call | tf_op jit(solution)/shard_map/slope/pallas_call | solution.py:133
  33.4 4.1 %all-to-all-start.2 = ((bf16[8,2,32,1024]{3,2,1,0:T(8,128)(2,1)}), bf16[8,2,32,1024]{3,2,1,0:T(8,128)(2,1)S(1)}, u32[]{:S(2)}, u32[]{:S(2)}) async-start(bf16[8,2,32,1024]{3,2,1,0:T(8,128)(2,1)} %slope.1), calls=%async_computation.2 | async-start | bytes 2097152 | tf_op jit(solution)/shard_map/slope_share/all_to_all | solution.py:443
  38.8 14.1 %all-to-all-done.2.refs_0_ = bf16[8,2,32,1024]{3,2,1,0:T(8,128)(2,1)S(1)} async-done(((bf16[8,2,32,1024]{3,2,1,0:T(8,128)(2,1)}), bf16[8,2,32,1024]{3,2,1,0:T(8,128)(2,1)S(1)}, u32[]{:S(2)}, u32[]{:S(2)}) %all-to-all-start.2) | async-done | bytes 1048608 | tf_op jit(solution)/shard_map/slope_share/all_to_all | solution.py:443
  54.1 3.3 %derivatives.3 = bf16[32,2,32,512]{3,2,1,0:T(8,128)(2,1)} custom-call(f32[1]{0:T(128)S(6)} %div.4.scale_ref, bf16[2,256,1024]{2,1,0:T(8,128)(2,1)S(1)} %copy-done.9, f32[2,256,512]{2,1,0:T(8,128)S(1)} %copy-done.10, bf16[1024,512]{1,0:T(8,128)(2,1)S(1)} %copy-done, bf16[8,2,32,1024]{3,2,1,0:T(8,128)(2,1)S(1)} %all-to-all-done.2.refs_0_), custom_call_target="tpu_custom_call" | custom-call | tf_op jit(solution)/shard_map/derivatives/pallas_call | solution.py:162
  57.5 11.4 %all-to-all-start.3 = ((bf16[32,2,32,512]{3,2,1,0:T(8,128)(2,1)}), bf16[32,2,32,512]{3,2,1,0:T(8,128)(2,1)S(1)}, u32[]{:S(2)}, u32[]{:S(2)}) async-start(bf16[32,2,32,512]{3,2,1,0:T(8,128)(2,1)} %derivatives.3), calls=%async_computation.3 | async-start | bytes 4194304 | tf_op jit(solution)/shard_map/derivative_exchange/all_to_all | solution.py:451
  70.5 2.7 %collective-permute-start.2 = (bf16[2,32,1024]{2,1,0:T(8,128)(2,1)}, bf16[2,32,1024]{2,1,0:T(8,128)(2,1)S(1)}, u32[]{:S(2)}, u32[]{:S(2)}) collective-permute-start(bf16[2,32,1024]{2,1,0:T(8,128)(2,1)} %copy-done.21), channel_id=1, source_target_pairs={{0,3},{1,2},{2,1},{3,0},{4,7},{5,6},{6,5},{7,4},{8,11},{9,10},{10,... | collective-permute-start | bytes 393224 | tf_op jit(solution)/shard_map/mixed_exchange/ppermute | solution.py:392
  73.7 3.3 %collective-permute-start.4 = (bf16[2,32,1024]{2,1,0:T(8,128)(2,1)}, bf16[2,32,1024]{2,1,0:T(8,128)(2,1)S(1)}, u32[]{:S(2)}, u32[]{:S(2)}) collective-permute-start(bf16[2,32,1024]{2,1,0:T(8,128)(2,1)} %copy-done.19), channel_id=1, source_target_pairs={{0,5},{1,4},{2,7},{3,6},{4,1},{5,0},{6,3},{7,2},{8,13},{9,12},{10,... | collective-permute-start | bytes 393224 | tf_op jit(solution)/shard_map/mixed_exchange/ppermute | solution.py:392
  77.0 2.6 %collective-permute-done = bf16[2,32,1024]{2,1,0:T(8,128)(2,1)S(1)} collective-permute-done((bf16[2,32,1024]{2,1,0:T(8,128)(2,1)}, bf16[2,32,1024]{2,1,0:T(8,128)(2,1)S(1)}, u32[]{:S(2)}, u32[]{:S(2)}) %collective-permute-start) | collective-permute-done | bytes 131104 | tf_op jit(solution)/shard_map/mixed_exchange/ppermute | solution.py:392
  80.5 3.3 %collective-permute-start.6 = (bf16[2,32,1024]{2,1,0:T(8,128)(2,1)}, bf16[2,32,1024]{2,1,0:T(8,128)(2,1)S(1)}, u32[]{:S(2)}, u32[]{:S(2)}) collective-permute-start(bf16[2,32,1024]{2,1,0:T(8,128)(2,1)} %copy-done.17), channel_id=1, source_target_pairs={{0,7},{1,6},{2,5},{3,4},{4,3},{5,2},{6,1},{7,0},{8,15},{9,14},{10,... | collective-permute-start | bytes 393224 | tf_op jit(solution)/shard_map/mixed_exchange/ppermute | solution.py:392
  83.8 3.4 %collective-permute-done.2 = bf16[2,32,1024]{2,1,0:T(8,128)(2,1)S(1)} collective-permute-done((bf16[2,32,1024]{2,1,0:T(8,128)(2,1)}, bf16[2,32,1024]{2,1,0:T(8,128)(2,1)S(1)}, u32[]{:S(2)}, u32[]{:S(2)}) %collective-permute-start.2) | collective-permute-done | bytes 131104 | tf_op jit(solution)/shard_map/mixed_exchange/ppermute | solution.py:392
  87.2 5.3 %collective-permute-done.4 = bf16[2,32,1024]{2,1,0:T(8,128)(2,1)S(1)} collective-permute-done((bf16[2,32,1024]{2,1,0:T(8,128)(2,1)}, bf16[2,32,1024]{2,1,0:T(8,128)(2,1)S(1)}, u32[]{:S(2)}, u32[]{:S(2)}) %collective-permute-start.4) | collective-permute-done | bytes 131104 | tf_op jit(solution)/shard_map/mixed_exchange/ppermute | solution.py:392
  92.5 3.5 %collective-permute-done.6 = bf16[2,32,1024]{2,1,0:T(8,128)(2,1)S(1)} collective-permute-done((bf16[2,32,1024]{2,1,0:T(8,128)(2,1)}, bf16[2,32,1024]{2,1,0:T(8,128)(2,1)S(1)}, u32[]{:S(2)}, u32[]{:S(2)}) %collective-permute-start.6) | collective-permute-done | bytes 131104 | tf_op jit(solution)/shard_map/mixed_exchange/ppermute | solution.py:392
  96.2 3.4 %collective-permute-start.13 = (bf16[2,32,1024]{2,1,0:T(8,128)(2,1)S(1)}, bf16[2,32,1024]{2,1,0:T(8,128)(2,1)S(1)}, u32[]{:S(2)}, u32[]{:S(2)}) collective-permute-start(bf16[2,32,1024]{2,1,0:T(8,128)(2,1)S(1)} %multiply_convert_fusion.refs_0_), channel_id=1, source_target_pairs={{0,7},{1,6},{2,5},{3,4},{4,3},{5,2},{6,1},{7,0},{8,15},{9,14},{10,... | collective-permute-start | bytes 393224 | tf_op jit(solution)/shard_map/slope_share/ppermute | solution.py:392
  101.5 2.9 %collective-permute-start.10 = (bf16[2,32,1024]{2,1,0:T(8,128)(2,1)S(1)}, bf16[2,32,1024]{2,1,0:T(8,128)(2,1)S(1)}, u32[]{:S(2)}, u32[]{:S(2)}) collective-permute-start(bf16[2,32,1024]{2,1,0:T(8,128)(2,1)S(1)} %multiply_convert_fusion.refs_0_), channel_id=1, source_target_pairs={{0,4},{1,5},{2,6},{3,7},{4,0},{5,1},{6,2},{7,3},{8,12},{9,13},{10,... | collective-permute-start | bytes 393224 | tf_op jit(solution)/shard_map/slope_share/ppermute | solution.py:392
  105.3 2.4 %collective-permute-done.13.refs_7_ = bf16[2,32,1024]{2,1,0:T(8,128)(2,1)S(1)} collective-permute-done((bf16[2,32,1024]{2,1,0:T(8,128)(2,1)S(1)}, bf16[2,32,1024]{2,1,0:T(8,128)(2,1)S(1)}, u32[]{:S(2)}, u32[]{:S(2)}) %collective-permute-start.13) | collective-permute-done | bytes 131104 | tf_op jit(solution)/shard_map/slope_share/ppermute | solution.py:392
  108.6 3.4 %collective-permute-done.12.refs_6_ = bf16[2,32,1024]{2,1,0:T(8,128)(2,1)S(1)} collective-permute-done((bf16[2,32,1024]{2,1,0:T(8,128)(2,1)S(1)}, bf16[2,32,1024]{2,1,0:T(8,128)(2,1)S(1)}, u32[]{:S(2)}, u32[]{:S(2)}) %collective-permute-start.12) | collective-permute-done | bytes 131104 | tf_op jit(solution)/shard_map/slope_share/ppermute | solution.py:392
  113.9 2.8 %collective-permute-done.9.refs_3_ = bf16[2,32,1024]{2,1,0:T(8,128)(2,1)S(1)} collective-permute-done((bf16[2,32,1024]{2,1,0:T(8,128)(2,1)S(1)}, bf16[2,32,1024]{2,1,0:T(8,128)(2,1)S(1)}, u32[]{:S(2)}, u32[]{:S(2)}) %collective-permute-start.9) | collective-permute-done | bytes 131104 | tf_op jit(solution)/shard_map/slope_share/ppermute | solution.py:392
  119.9 3.3 %derivatives.2 = bf16[32,2,32,512]{3,2,1,0:T(8,128)(2,1)} custom-call(f32[1]{0:T(128)S(6)} %div.4.scale_ref, bf16[2,256,1024]{2,1,0:T(8,128)(2,1)S(1)} %copy-done.6, f32[2,256,512]{2,1,0:T(8,128)S(1)} %copy-done.8, bf16[1024,512]{1,0:T(8,128)(2,1)S(1)} %copy-done, bf16[2,32,1024]{2,1,0:T(8,128)(2,1)S(1)} %multiply_convert_fusion.refs_0_, ...), custom_call_target="tpu_custom_call" | custom-call | tf_op jit(solution)/shard_map/derivatives/pallas_call | solution.py:162
  123.2 9.8 %all-to-all-start = ((bf16[32,2,32,512]{3,2,1,0:T(8,128)(2,1)}), bf16[32,2,32,512]{3,2,1,0:T(8,128)(2,1)}, u32[]{:S(2)}, u32[]{:S(2)}) async-start(bf16[32,2,32,512]{3,2,1,0:T(8,128)(2,1)} %derivatives.2), calls=%async_computation | async-start | bytes 4194304 | tf_op jit(solution)/shard_map/derivative_exchange/all_to_all | solution.py:451
  134.1 4.5 %gram.2 = (bf16[32,64,512]{2,1,0:T(8,128)(2,1)S(1)}, f32[4,2048,128]{2,1,0:T(8,128)S(1)}) custom-call(bf16[64,32,512]{2,1,0:T(8,128)(2,1)S(1)} %bitcast.12), custom_call_target="tpu_custom_call" | custom-call | tf_op jit(solution)/shard_map/gram/pallas_call | solution.py:214
  142.0 41.1 %all-to-all-done = bf16[32,2,32,512]{3,2,1,0:T(8,128)(2,1)} async-done(((bf16[32,2,32,512]{3,2,1,0:T(8,128)(2,1)}), bf16[32,2,32,512]{3,2,1,0:T(8,128)(2,1)}, u32[]{:S(2)}, u32[]{:S(2)}) %all-to-all-start) | async-done | bytes 2097184 | tf_op jit(solution)/shard_map/derivative_exchange/all_to_all | solution.py:451
  183.1 7.6 %gram.3 = (f32[128,128]{1,0:T(8,128)}, f32[4,2048,128]{2,1,0:T(8,128)}) custom-call(f32[1,128]{1,0:T(1,128)} %broadcast_select_fusion.energy_ref, bf16[64,32,512]{2,1,0:T(8,128)(2,1)} %bitcast.5.code_ref, bf16[32,64,512]{2,1,0:T(8,128)(2,1)} %copy-done.4), custom_call_target="tpu_custom_call" | custom-call | tf_op jit(solution)/shard_map/gram/pallas_call | solution.py:263
  190.7 10.8 %all_to_all.35 = f32[16,8,128]{2,1,0:T(8,128)S(1)} all-to-all(f32[16,8,128]{2,1,0:T(8,128)} %bitcast.13), channel_id=1, replica_groups=mesh['z'=8,'x_lo'=2,'core'=2,'y'=4,'x_hi'=2] {'x_lo','core','y'}, dimensions={0} | all-to-all | bytes 131072 | tf_op jit(solution)/shard_map/gram_sum/all_to_all | solution.py:459
  202.1 4.9 %all-to-all-start.5 = ((f32[16,8,128]{2,1,0:T(8,128)}), f32[16,8,128]{2,1,0:T(8,128)S(1)}, u32[]{:S(2)}, u32[]{:S(2)}) async-start(f32[16,8,128]{2,1,0:T(8,128)} %broadcast_in_dim.13), calls=%async_computation.5 | async-start | bytes 131072 | tf_op jit(solution)/shard_map/gram_sum/all_to_all | solution.py:36
  207.7 8.8 %all-to-all-done.5 = f32[16,8,128]{2,1,0:T(8,128)S(1)} async-done(((f32[16,8,128]{2,1,0:T(8,128)}), f32[16,8,128]{2,1,0:T(8,128)S(1)}, u32[]{:S(2)}, u32[]{:S(2)}) %all-to-all-start.5) | async-done | bytes 65568 | tf_op jit(solution)/shard_map/gram_sum/all_to_all | solution.py:36
  217.2 5.1 %all-to-all-start.6 = ((f32[16,8,128]{2,1,0:T(8,128)}), f32[16,8,128]{2,1,0:T(8,128)S(1)}, u32[]{:S(2)}, u32[]{:S(2)}) async-start(f32[16,8,128]{2,1,0:T(8,128)} %broadcast_in_dim.14), calls=%async_computation.6 | async-start | bytes 131072 | tf_op jit(solution)/shard_map/gram_sum/all_to_all | solution.py:36
  222.9 5.2 %all-to-all-done.6.shared_ref = f32[16,8,128]{2,1,0:T(8,128)S(1)} async-done(((f32[16,8,128]{2,1,0:T(8,128)}), f32[16,8,128]{2,1,0:T(8,128)S(1)}, u32[]{:S(2)}, u32[]{:S(2)}) %all-to-all-start.6) | async-done | bytes 65568 | tf_op jit(solution)/shard_map/gram_sum/all_to_all | solution.py:36
  228.8 5.8 %solve.1 = f32[32,512]{1,0:T(8,128)} custom-call(f32[2]{0:T(128)} %pad_maximum_fusion.scalar_ref, f32[16,8,128]{2,1,0:T(8,128)} %copy-done.24, f32[4,2048,128]{2,1,0:T(8,128)} %copy-done.3, f32[4,2048,128]{2,1,0:T(8,128)} %get-tuple-element.42.refs_1_), custom_call_target="tpu_custom_call" | custom-call | tf_op jit(solution)/shard_map/solve/pallas_call | solution.py:353
  (83 shorter events, 30.8 us)
Async XLA Ops:
  0.6 13.2 %copy-start.1 = (bf16[4,256,1024]{2,1,0:T(8,128)(2,1)S(1)}, bf16[4,256,1024]{2,1,0:T(8,128)(2,1)}, u32[]{:S(2)}) copy-start(bf16[4,256,1024]{2,1,0:T(8,128)(2,1)} %param.10) | copy-start | bytes 6291460
  6.2 7.7 %copy-start = (bf16[1024,512]{1,0:T(8,128)(2,1)S(1)}, bf16[1024,512]{1,0:T(8,128)(2,1)}, u32[]{:S(2)}) copy-start(bf16[1024,512]{1,0:T(8,128)(2,1)} %down_ref.7) | copy-start | bytes 3145732
  6.2 7.7 %copy-start.13 = (s32[4,256]{1,0:T(4,128)S(1)}, s32[4,256]{1,0:T(4,128)}, u32[]{:S(2)}) copy-start(s32[4,256]{1,0:T(4,128)} %spin_ref.3) | copy-start | bytes 12292
  6.2 7.7 %copy-start.14 = (bf16[1024]{0:T(1024)(128)(2,1)S(1)}, bf16[1024]{0:T(1024)(128)(2,1)}, u32[]{:S(2)}) copy-start(bf16[1024]{0:T(1024)(128)(2,1)} %embed_ref.3) | copy-start | bytes 6148
  6.2 7.7 %copy-start.15 = (bf16[1024]{0:T(1024)(128)(2,1)S(1)}, bf16[1024]{0:T(1024)(128)(2,1)}, u32[]{:S(2)}) copy-start(bf16[1024]{0:T(1024)(128)(2,1)} %gain_ref.3) | copy-start | bytes 6148
  6.2 23.7 %all-to-all-start.1 = ((bf16[8,2,32,1024]{3,2,1,0:T(8,128)(2,1)}), bf16[8,2,32,1024]{3,2,1,0:T(8,128)(2,1)}, u32[]{:S(2)}, u32[]{:S(2)}) async-start(bf16[8,2,32,1024]{3,2,1,0:T(8,128)(2,1)} %get-tuple-element.37), calls=%async_computation.1 | async-start | bytes 2097152 | tf_op jit(solution)/shard_map/mixed_exchange/all_to_all | solution.py:430
  13.9 1.2 copy-start.2
  15.8 14.2 %copy-start.12 = (bf16[1024]{0:T(1024)(128)(2,1)S(1)}, bf16[1024]{0:T(1024)(128)(2,1)}, u32[]{:S(2)}) copy-start(bf16[1024]{0:T(1024)(128)(2,1)} %readout_ref.1) | copy-start | bytes 6148
  30.9 22.0 %copy-start.9 = (bf16[2,256,1024]{2,1,0:T(8,128)(2,1)S(1)}, bf16[2,256,1024]{2,1,0:T(8,128)(2,1)}, u32[]{:S(2)}) copy-start(bf16[2,256,1024]{2,1,0:T(8,128)(2,1)} %get-tuple-element.35.normed_ref) | copy-start | bytes 3145732
  33.4 19.5 %all-to-all-start.2 = ((bf16[8,2,32,1024]{3,2,1,0:T(8,128)(2,1)}), bf16[8,2,32,1024]{3,2,1,0:T(8,128)(2,1)S(1)}, u32[]{:S(2)}, u32[]{:S(2)}) async-start(bf16[8,2,32,1024]{3,2,1,0:T(8,128)(2,1)} %slope.1), calls=%async_computation.2 | async-start | bytes 2097152 | tf_op jit(solution)/shard_map/slope_share/all_to_all | solution.py:443
  57.5 65.7 %all-to-all-start.3 = ((bf16[32,2,32,512]{3,2,1,0:T(8,128)(2,1)}), bf16[32,2,32,512]{3,2,1,0:T(8,128)(2,1)S(1)}, u32[]{:S(2)}, u32[]{:S(2)}) async-start(bf16[32,2,32,512]{3,2,1,0:T(8,128)(2,1)} %derivatives.3), calls=%async_computation.3 | async-start | bytes 4194304 | tf_op jit(solution)/shard_map/derivative_exchange/all_to_all | solution.py:451
  68.9 49.8 %copy-start.6 = (bf16[2,256,1024]{2,1,0:T(8,128)(2,1)S(1)}, bf16[2,256,1024]{2,1,0:T(8,128)(2,1)}, u32[]{:S(2)}) copy-start(bf16[2,256,1024]{2,1,0:T(8,128)(2,1)} %copy-done.5) | copy-start | bytes 3145732
  68.9 10.8 %collective-permute-start = (bf16[2,32,1024]{2,1,0:T(8,128)(2,1)}, bf16[2,32,1024]{2,1,0:T(8,128)(2,1)S(1)}, u32[]{:S(2)}, u32[]{:S(2)}) collective-permute-start(bf16[2,32,1024]{2,1,0:T(8,128)(2,1)} %copy-done.23), channel_id=1, source_target_pairs={{0,1},{1,0},{2,3},{3,2},{4,5},{5,4},{6,7},{7,6},{8,9},{9,8},{10,11... | collective-permute-start | bytes 393224 | tf_op jit(solution)/shard_map/mixed_exchange/ppermute | solution.py:392
  70.2 10.4 %collective-permute-start.1 = (bf16[2,32,1024]{2,1,0:T(8,128)(2,1)}, bf16[2,32,1024]{2,1,0:T(8,128)(2,1)S(1)}, u32[]{:S(2)}, u32[]{:S(2)}) collective-permute-start(bf16[2,32,1024]{2,1,0:T(8,128)(2,1)} %copy-done.22), channel_id=1, source_target_pairs={{0,2},{1,3},{2,0},{3,1},{4,6},{5,7},{6,4},{7,5},{8,10},{9,11},{10,... | collective-permute-start | bytes 393224 | tf_op jit(solution)/shard_map/mixed_exchange/ppermute | solution.py:392
  70.5 16.8 %collective-permute-start.2 = (bf16[2,32,1024]{2,1,0:T(8,128)(2,1)}, bf16[2,32,1024]{2,1,0:T(8,128)(2,1)S(1)}, u32[]{:S(2)}, u32[]{:S(2)}) collective-permute-start(bf16[2,32,1024]{2,1,0:T(8,128)(2,1)} %copy-done.21), channel_id=1, source_target_pairs={{0,3},{1,2},{2,1},{3,0},{4,7},{5,6},{6,5},{7,4},{8,11},{9,10},{10,... | collective-permute-start | bytes 393224 | tf_op jit(solution)/shard_map/mixed_exchange/ppermute | solution.py:392
  73.1 14.1 %collective-permute-start.3 = (bf16[2,32,1024]{2,1,0:T(8,128)(2,1)}, bf16[2,32,1024]{2,1,0:T(8,128)(2,1)S(1)}, u32[]{:S(2)}, u32[]{:S(2)}) collective-permute-start(bf16[2,32,1024]{2,1,0:T(8,128)(2,1)} %copy-done.20), channel_id=1, source_target_pairs={{0,4},{1,5},{2,6},{3,7},{4,0},{5,1},{6,2},{7,3},{8,12},{9,13},{10,... | collective-permute-start | bytes 393224 | tf_op jit(solution)/shard_map/mixed_exchange/ppermute | solution.py:392
  73.7 18.8 %collective-permute-start.4 = (bf16[2,32,1024]{2,1,0:T(8,128)(2,1)}, bf16[2,32,1024]{2,1,0:T(8,128)(2,1)S(1)}, u32[]{:S(2)}, u32[]{:S(2)}) collective-permute-start(bf16[2,32,1024]{2,1,0:T(8,128)(2,1)} %copy-done.19), channel_id=1, source_target_pairs={{0,5},{1,4},{2,7},{3,6},{4,1},{5,0},{6,3},{7,2},{8,13},{9,12},{10,... | collective-permute-start | bytes 393224 | tf_op jit(solution)/shard_map/mixed_exchange/ppermute | solution.py:392
  79.7 12.8 %collective-permute-start.5 = (bf16[2,32,1024]{2,1,0:T(8,128)(2,1)}, bf16[2,32,1024]{2,1,0:T(8,128)(2,1)S(1)}, u32[]{:S(2)}, u32[]{:S(2)}) collective-permute-start(bf16[2,32,1024]{2,1,0:T(8,128)(2,1)} %copy-done.18), channel_id=1, source_target_pairs={{0,6},{1,7},{2,4},{3,5},{4,2},{5,3},{6,0},{7,1},{8,14},{9,15},{10,... | collective-permute-start | bytes 393224 | tf_op jit(solution)/shard_map/mixed_exchange/ppermute | solution.py:392
  80.5 15.5 %collective-permute-start.6 = (bf16[2,32,1024]{2,1,0:T(8,128)(2,1)}, bf16[2,32,1024]{2,1,0:T(8,128)(2,1)S(1)}, u32[]{:S(2)}, u32[]{:S(2)}) collective-permute-start(bf16[2,32,1024]{2,1,0:T(8,128)(2,1)} %copy-done.17), channel_id=1, source_target_pairs={{0,7},{1,6},{2,5},{3,4},{4,3},{5,2},{6,1},{7,0},{8,15},{9,14},{10,... | collective-permute-start | bytes 393224 | tf_op jit(solution)/shard_map/mixed_exchange/ppermute | solution.py:392
  96.2 11.5 %collective-permute-start.13 = (bf16[2,32,1024]{2,1,0:T(8,128)(2,1)S(1)}, bf16[2,32,1024]{2,1,0:T(8,128)(2,1)S(1)}, u32[]{:S(2)}, u32[]{:S(2)}) collective-permute-start(bf16[2,32,1024]{2,1,0:T(8,128)(2,1)S(1)} %multiply_convert_fusion.refs_0_), channel_id=1, source_target_pairs={{0,7},{1,6},{2,5},{3,4},{4,3},{5,2},{6,1},{7,0},{8,15},{9,14},{10,... | collective-permute-start | bytes 393224 | tf_op jit(solution)/shard_map/slope_share/ppermute | solution.py:392
  99.6 12.5 %collective-permute-start.12 = (bf16[2,32,1024]{2,1,0:T(8,128)(2,1)S(1)}, bf16[2,32,1024]{2,1,0:T(8,128)(2,1)S(1)}, u32[]{:S(2)}, u32[]{:S(2)}) collective-permute-start(bf16[2,32,1024]{2,1,0:T(8,128)(2,1)S(1)} %multiply_convert_fusion.refs_0_), channel_id=1, source_target_pairs={{0,6},{1,7},{2,4},{3,5},{4,2},{5,3},{6,0},{7,1},{8,14},{9,15},{10,... | collective-permute-start | bytes 393224 | tf_op jit(solution)/shard_map/slope_share/ppermute | solution.py:392
  100.2 13.8 %collective-permute-start.11 = (bf16[2,32,1024]{2,1,0:T(8,128)(2,1)S(1)}, bf16[2,32,1024]{2,1,0:T(8,128)(2,1)S(1)}, u32[]{:S(2)}, u32[]{:S(2)}) collective-permute-start(bf16[2,32,1024]{2,1,0:T(8,128)(2,1)S(1)} %multiply_convert_fusion.refs_0_), channel_id=1, source_target_pairs={{0,5},{1,4},{2,7},{3,6},{4,1},{5,0},{6,3},{7,2},{8,13},{9,12},{10,... | collective-permute-start | bytes 393224 | tf_op jit(solution)/shard_map/slope_share/ppermute | solution.py:392
  101.5 12.4 %collective-permute-start.10 = (bf16[2,32,1024]{2,1,0:T(8,128)(2,1)S(1)}, bf16[2,32,1024]{2,1,0:T(8,128)(2,1)S(1)}, u32[]{:S(2)}, u32[]{:S(2)}) collective-permute-start(bf16[2,32,1024]{2,1,0:T(8,128)(2,1)S(1)} %multiply_convert_fusion.refs_0_), channel_id=1, source_target_pairs={{0,4},{1,5},{2,6},{3,7},{4,0},{5,1},{6,2},{7,3},{8,12},{9,13},{10,... | collective-permute-start | bytes 393224 | tf_op jit(solution)/shard_map/slope_share/ppermute | solution.py:392
  104.4 12.3 %collective-permute-start.9 = (bf16[2,32,1024]{2,1,0:T(8,128)(2,1)S(1)}, bf16[2,32,1024]{2,1,0:T(8,128)(2,1)S(1)}, u32[]{:S(2)}, u32[]{:S(2)}) collective-permute-start(bf16[2,32,1024]{2,1,0:T(8,128)(2,1)S(1)} %multiply_convert_fusion.refs_0_), channel_id=1, source_target_pairs={{0,3},{1,2},{2,1},{3,0},{4,7},{5,6},{6,5},{7,4},{8,11},{9,10},{10,... | collective-permute-start | bytes 393224 | tf_op jit(solution)/shard_map/slope_share/ppermute | solution.py:392
  107.7 9.0 %collective-permute-start.8 = (bf16[2,32,1024]{2,1,0:T(8,128)(2,1)S(1)}, bf16[2,32,1024]{2,1,0:T(8,128)(2,1)S(1)}, u32[]{:S(2)}, u32[]{:S(2)}) collective-permute-start(bf16[2,32,1024]{2,1,0:T(8,128)(2,1)S(1)} %multiply_convert_fusion.refs_0_), channel_id=1, source_target_pairs={{0,2},{1,3},{2,0},{3,1},{4,6},{5,7},{6,4},{7,5},{8,10},{9,11},{10,... | collective-permute-start | bytes 393224 | tf_op jit(solution)/shard_map/slope_share/ppermute | solution.py:392
  112.1 6.6 %collective-permute-start.7 = (bf16[2,32,1024]{2,1,0:T(8,128)(2,1)S(1)}, bf16[2,32,1024]{2,1,0:T(8,128)(2,1)S(1)}, u32[]{:S(2)}, u32[]{:S(2)}) collective-permute-start(bf16[2,32,1024]{2,1,0:T(8,128)(2,1)S(1)} %multiply_convert_fusion.refs_0_), channel_id=1, source_target_pairs={{0,1},{1,0},{2,3},{3,2},{4,5},{5,4},{6,7},{7,6},{8,9},{9,8},{10,11... | collective-permute-start | bytes 393224 | tf_op jit(solution)/shard_map/slope_share/ppermute | solution.py:392
  123.2 9.8 %copy-start.25 = (f32[4]{0:T(128)S(1)}, f32[4]{0:T(128)}, u32[]{:S(2)}) copy-start(f32[4]{0:T(128)} %param.16) | copy-start | bytes 52
  123.2 59.9 %all-to-all-start = ((bf16[32,2,32,512]{3,2,1,0:T(8,128)(2,1)}), bf16[32,2,32,512]{3,2,1,0:T(8,128)(2,1)}, u32[]{:S(2)}, u32[]{:S(2)}) async-start(bf16[32,2,32,512]{3,2,1,0:T(8,128)(2,1)} %derivatives.2), calls=%async_computation | async-start | bytes 4194304 | tf_op jit(solution)/shard_map/derivative_exchange/all_to_all | solution.py:451
  138.6 2.0 copy-start.3
  140.6 1.4 copy-start.4
  202.1 14.4 %all-to-all-start.5 = ((f32[16,8,128]{2,1,0:T(8,128)}), f32[16,8,128]{2,1,0:T(8,128)S(1)}, u32[]{:S(2)}, u32[]{:S(2)}) async-start(f32[16,8,128]{2,1,0:T(8,128)} %broadcast_in_dim.13), calls=%async_computation.5 | async-start | bytes 131072 | tf_op jit(solution)/shard_map/gram_sum/all_to_all | solution.py:36
  217.2 11.0 %all-to-all-start.6 = ((f32[16,8,128]{2,1,0:T(8,128)}), f32[16,8,128]{2,1,0:T(8,128)S(1)}, u32[]{:S(2)}, u32[]{:S(2)}) async-start(f32[16,8,128]{2,1,0:T(8,128)} %broadcast_in_dim.14), calls=%async_computation.6 | async-start | bytes 131072 | tf_op jit(solution)/shard_map/gram_sum/all_to_all | solution.py:36
  (14 other events, 11.1 us)

commit v3 on v2

--- a/solution.py
+++ b/solution.py
@@ -1,3 +1,5 @@
+import functools
+
 import jax
 import jax.numpy as jnp
 from jax import lax
@@ -112,12 +114,11 @@
             result(jnp.float32, tokens, hidden),
         ]
         + part_shapes,
-        compiler_params=pltpu.CompilerParams(vmem_limit_bytes=VMEM_LIMIT if first == 0 else VMEM_SMALL),
+        compiler_params=pltpu.CompilerParams(vmem_limit_bytes=VMEM_LIMIT),
     )(scalars, spins, features, embed, gain, up, down)
 
 
-def slope_kernel(part_ref, own_ref, readout_ref, *refs):
-    slope_ref = refs[-1]
+def slope_kernel(part_ref, own_ref, readout_ref, slope_ref):
     blocks, samples, rows, width = part_ref.shape
     readout = readout_ref[...].astype(jnp.float32).reshape(1, width)
     for s in range(samples):
@@ -129,18 +130,18 @@
             slope_ref[k, s] = slope
 
 
-def own_slope(parts, own, readout, after):
+def own_slope(parts, own, readout):
     return pl.pallas_call(
         slope_kernel,
         out_shape=jax.ShapeDtypeStruct(parts.shape, parts.dtype),
-        in_specs=[VMEM] * 3 + [pl.BlockSpec(memory_space=pl.ANY)] * len(after),
+        in_specs=[VMEM] * 3,
         out_specs=VMEM,
         compiler_params=pltpu.CompilerParams(vmem_limit_bytes=VMEM_SMALL),
-    )(parts, own, readout, *after)
-
-
-def derivative_kernel(scale_ref, normed_ref, bend_ref, down_ref, *refs):
-    slope_refs, coded_ref = refs[:-1], refs[-1]
+    )(parts, own, readout)
+
+
+def derivative_kernel(slope_count, scale_ref, normed_ref, bend_ref, down_ref, *refs):
+    slope_refs, coded_ref = refs[:slope_count], refs[-1]
     tokens, width = normed_ref.shape[1:]
     if len(slope_refs) == 1:
         slope = slope_refs[0][:, 0].reshape(tokens, width)
@@ -155,12 +156,12 @@
     coded_ref[:, 0] = coded.reshape(coded_ref.shape[0], coded_ref.shape[2], coded_ref.shape[3])
 
 
-def derivative(scale, normed, bend, down, slopes, parts):
+def derivative(scale, normed, bend, down, slopes, parts, after):
     samples, tokens, width = normed.shape
     hidden = down.shape[1]
     block = lambda *shape: pl.BlockSpec((1,) + shape, lambda s: (s,) + (0,) * len(shape))
     return pl.pallas_call(
-        derivative_kernel,
+        functools.partial(derivative_kernel, len(slopes)),
         grid=(samples,),
         in_specs=[
             SMEM,
@@ -173,39 +174,45 @@
             if a.ndim == 3
             else pl.BlockSpec((a.shape[0], 1) + a.shape[2:], lambda s: (0, s, 0, 0))
             for a in slopes
-        ],
+        ]
+        + [pl.BlockSpec((1, 16, 128), lambda s: (0, 0, 0))] * len(after),
         out_specs=pl.BlockSpec((parts, 1, width // parts, hidden), lambda s: (0, s, 0, 0)),
         out_shape=jax.ShapeDtypeStruct((parts, samples, width // parts, hidden), jnp.bfloat16),
         compiler_params=pltpu.CompilerParams(vmem_limit_bytes=VMEM_SMALL),
-    )(scale, normed, bend, down, *slopes)
-
-
-def widen(code_ref, wide_ref):
-    count, rows, lanes = code_ref.shape
-    for n in range(0, count, 8):
-        wide_ref[0, n * rows : (n + 8) * rows] = decode(code_ref[n : n + 8]).reshape(8 * rows, lanes)
-
-
-def row_of_all(wide_ref, row, rows):
-    count = wide_ref.shape[1] // rows
-    return wide_ref[0, pl.ds(row, count, stride=rows)].astype(jnp.bfloat16)
-
-
-def rows_first_kernel(code_ref, half_ref, wide_ref):
-    rows = code_ref.shape[1]
-    widen(code_ref, wide_ref)
-    for r in range(rows):
-        half_ref[r] = row_of_all(wide_ref, r, rows)
+    )(scale, normed, bend, down, *slopes, *after)
 
 
 LANES = 128
+
+
+def widen(code_ref, wide_ref, apart_ref):
+    count, rows, _ = code_ref.shape
+    for n in range(count):
+        values = decode(code_ref[n])
+        wide_ref[0, n * rows : (n + 1) * rows] = values
+        apart_ref[n * (rows + 1) : n * (rows + 1) + rows] = values
+
+
+def row_of_all(apart_ref, row, count, rows):
+    return apart_ref[pl.ds(row, count, stride=rows + 1)].astype(jnp.bfloat16)
+
+
+def apart_scratch(count, rows):
+    return pltpu.VMEM((-(-count * (rows + 1) // 8) * 8, LANES), jnp.float32)
 
 
 def wide_out(count, rows, width):
     return (
         pl.BlockSpec((1, count * rows, LANES), lambda f: (f, 0, 0)),
-        jax.ShapeDtypeStruct((width // LANES, count * rows, LANES), jnp.float32),
-    )
+        pltpu.HBM((width // LANES, count * rows, LANES), jnp.float32),
+    )
+
+
+def rows_first_kernel(code_ref, half_ref, wide_ref, apart_ref):
+    count, rows, _ = code_ref.shape
+    widen(code_ref, wide_ref, apart_ref)
+    for r in range(rows):
+        half_ref[r] = row_of_all(apart_ref, r, count, rows)
 
 
 def rows_first(code):
@@ -217,19 +224,20 @@
         in_specs=[pl.BlockSpec((count, rows, LANES), lambda f: (0, 0, f))],
         out_specs=[pl.BlockSpec((rows, count, LANES), lambda f: (0, 0, f)), wide_spec],
         out_shape=[jax.ShapeDtypeStruct((rows, count, width), jnp.bfloat16), wide_shape],
-        compiler_params=pltpu.CompilerParams(vmem_limit_bytes=VMEM_SMALL),
+        scratch_shapes=[apart_scratch(count, rows)],
+        compiler_params=pltpu.CompilerParams(vmem_limit_bytes=VMEM_LIMIT),
     )(code)
 
 
 def gram_kernel(energy_ref, code_ref, *refs):
-    half_refs, gram_ref, wide_ref = refs[:-2], refs[-2], refs[-1]
-    rows = code_ref.shape[1]
-    widen(code_ref, wide_ref)
+    half_refs, gram_ref, wide_ref, apart_ref = refs[:-3], *refs[-3:]
+    count, rows, _ = code_ref.shape
+    widen(code_ref, wide_ref, apart_ref)
     gram = jnp.zeros(gram_ref.shape, jnp.float32)
     for r in range(0, rows, 4):
         half = jnp.concatenate(
             [
-                jnp.concatenate([h[q] for h in half_refs] + [row_of_all(wide_ref, q, rows)], axis=0)
+                jnp.concatenate([h[q] for h in half_refs] + [row_of_all(apart_ref, q, count, rows)], axis=0)
                 for q in range(r, r + 4)
             ],
             axis=1,
@@ -270,7 +278,8 @@
         + [pl.BlockSpec(h.shape[:2] + (LANES,), lambda f: (0, 0, f)) for h in halves],
         out_specs=[pl.BlockSpec((size, size), lambda f: (0, 0)), wide_spec],
         out_shape=[jax.ShapeDtypeStruct((size, size), jnp.float32), wide_shape],
-        compiler_params=pltpu.CompilerParams(vmem_limit_bytes=VMEM_LIMIT),
+        scratch_shapes=[apart_scratch(count, rows)],
+        compiler_params=pltpu.CompilerParams(vmem_limit_bytes=VMEM_SMALL),
     )(energy, code, *halves)
 
 
@@ -333,19 +342,22 @@
         copy.wait()
     rows, width = out_ref.shape
     lanes = spread_ref.shape[1]
-    for f in range(width // lanes):
-        total = jnp.zeros((rows, lanes), jnp.float32)
+    groups = 2
+    for f in range(0, width // lanes, groups):
+        total = (jnp.zeros((rows, lanes), jnp.float32),) * groups
         first = 0
         for chunk_ref in chunk_refs:
             samples = chunk_ref.shape[1] // rows
 
             def add(s, total):
                 start = pl.multiple_of(s * rows, rows)
-                return total + spread_ref[pl.ds(first + s, 1)] * chunk_ref[f, pl.ds(start, rows)]
+                spread = spread_ref[pl.ds(first + s, 1)]
+                return tuple(t + spread * chunk_ref[f + g, pl.ds(start, rows)] for g, t in enumerate(total))
 
             total = lax.fori_loop(0, samples, add, total, unroll=8)
             first += samples
-        out_ref[:, f * lanes : (f + 1) * lanes] = total
+        for g in range(groups):
+            out_ref[:, (f + g) * lanes : (f + g + 1) * lanes] = total[g]
 
 
 def solve(scalars, shared, chunks, rows):
@@ -353,7 +365,7 @@
     return pl.pallas_call(
         solve_kernel,
         out_shape=jax.ShapeDtypeStruct((rows, chunks[0].shape[0] * chunks[0].shape[2]), jnp.float32),
-        in_specs=[SMEM, VMEM] + [pl.BlockSpec(memory_space=pl.ANY)] * len(chunks),
+        in_specs=[SMEM, VMEM] + [pl.BlockSpec(memory_space=pltpu.HBM)] * len(chunks),
         out_specs=VMEM,
         scratch_shapes=[
             pltpu.VMEM((count, count), jnp.float32),
@@ -432,7 +444,7 @@
                 mixed_parts = parts[:1] + [partner(parts[k], k) for k in range(1, mp_size)]
         with jax.named_scope("slope"):
             if n == 0:
-                slope = own_slope(mixed_parts, own_inputs, readout, [s[1] for s in states[1:2]])
+                slope = own_slope(mixed_parts, own_inputs, readout)
             else:
                 outputs = own_inputs
                 for part in mixed_parts:
@@ -444,8 +456,9 @@
             else:
                 slopes = [slope] + [partner(slope, k) for k in range(1, mp_size)]
         with jax.named_scope("derivatives"):
+            after = [state[3] for state in states[n + 1 : n + 2]]
             coded_chunks.append(
-                derivative(1.0 / unit, normed, bend, down_weight, slopes, samp_size)
+                derivative(1.0 / unit, normed, bend, down_weight, slopes, samp_size, after)
             )
     with jax.named_scope("derivative_exchange"):
         chunks = [lax.all_to_all(c, SAMPLES, 0, 0) for c in coded_chunks]

time: 236 us -> 231 us (0.979)
  blocking collectives: 10.8 us -> 34.5 us
  local copies, waits for them, and re-layouts: 17.5 us -> 6.16 us
  starting transfers between devices: 65.7 us -> 56.9 us
  waiting for transfers between devices: 101 us -> 94.2 us
    all_to_all x0 -> x1, blocking collectives: none -> 23.9 us  [body(): mixed_parts = lax.all_to_all(parts[0], MP, 0, 0)]
    unnamed x52 -> x26, local copies, waits for them, and re-layouts: 15.7 us -> 4.39 us
    all_to_all x1 -> x0, starting transfers between devices: 7.63 us -> none  [body(): mixed_parts = lax.all_to_all(parts[0], MP, 0, 0)]
    all_to_all x1, waiting for transfers between devices: 14.1 us -> 7.93 us  [body(): slopes = [lax.all_to_all(slope, MP, 0, 0)]]
    all_to_all x1 -> x0, waiting for transfers between devices: 4.5 us -> none  [body(): mixed_parts = lax.all_to_all(parts[0], MP, 0, 0)]
    all_to_all x2, waiting for transfers between devices: 41.1 us -> 44.3 us  [body(): chunks = [lax.all_to_all(c, SAMPLES, 0, 0) for c in coded_chunks]]
    pallas_call x1, Pallas kernels: 7.59 us -> 4.93 us  [gram_matrix(): pl.pallas_call(gram_kernel, grid=(width // LANES,), in_specs=[pl.BlockSpe...]
    pallas_call x2, Pallas kernels: 8.75 us -> 11.2 us  [forward(): pl.pallas_call(forward_kernel, grid=(samples,), in_specs=[SMEM, whole(spi...]
  transfers between devices with their start and end apart: 20 -> 19, of which waited for: 14 -> 13; matrix products, arithmetic and copies ran while one was open for 1% -> 1% of each run, Pallas kernels for 5% -> 6%
where the time goes in v3:
time: 231 us; the launch traced here: 230 us
  waiting for transfers between devices  94.2 us (41%)
  starting transfers between devices  56.9 us (25%)
  Pallas kernels  35 us (15%)
  blocking collectives  34.5 us (15%)
  local copies, waits for them, and re-layouts  6.16 us (3%)
    all_to_all x2, waiting for transfers between devices, body(): chunks = [lax.all_to_all(c, SAMPLES, 0, 0) for c in coded_chunks]  44.3 us
    ppermute x14, waiting for transfers between devices, partner(): return lax.ppermute(array, MP, [(i, i ^ k) for i in range(mp_size)])  27.9 us
    all_to_all x1, blocking collectives, body(): mixed_parts = lax.all_to_all(parts[0], MP, 0, 0)  23.9 us
    all_to_all x2, starting transfers between devices, body(): chunks = [lax.all_to_all(c, SAMPLES, 0, 0) for c in coded_chunks]  22 us
    ppermute x14, starting transfers between devices, partner(): return lax.ppermute(array, MP, [(i, i ^ k) for i in range(mp_size)])  21.6 us
    all_to_all x2, waiting for transfers between devices, share(): lax.all_to_all(jnp.broadcast_to(array, (size,) + array.shape), axis, 0, 0)  14 us
    pallas_call x2, Pallas kernels, forward(): pl.pallas_call(forward_kernel, grid=(samples,), in_specs=[SMEM, whole(spi...  11.2 us
    all_to_all x1, blocking collectives, body(): lax.all_to_all(gram_part.reshape(near_size, sample_count // near_size, sa...  10.6 us
  transfers between devices with their start and end apart: 19, of which 13 were waited for; matrix products, arithmetic and copies ran while one was open for 1% of the time, Pallas kernels for 6%

profile of v3, /device:TPU:1, one launch (start us, length us, event | category | flops | bytes accessed | tf_op | source)
XLA Modules:
  0.0 230.5 jit_solution(8210822482430005476)
XLA Ops:
  0.6 5.4 %forward.3 = (bf16[2,256,1024]{2,1,0:T(8,128)(2,1)}, f32[2,32,1024]{2,1,0:T(8,128)}, f32[2,256,512]{2,1,0:T(8,128)}, bf16[8,2,32,1024]{3,2,1,0:T(8,128)(2,1)}) custom-call(s32[3]{0:T(128)} %get-tuple-element.46.scalar_ref, s32[4,256]{1,0:T(4,128)} %spin_ref.3, bf16[4,8,32,1024]{3,2,1,0:T(8,128)(2,1)} %bitcast.12, bf16[1024]{0:T(1024)(128)(2,1)} %embed_ref.3, ...), custom_call_target="tpu_custom_call" | custom-call | tf_op jit(solution)/shard_map/forward/pallas_call | solution.py:98
  6.1 23.9 %all_to_all.35.part_ref = bf16[8,2,32,1024]{3,2,1,0:T(8,128)(2,1)S(1)} all-to-all(bf16[8,2,32,1024]{3,2,1,0:T(8,128)(2,1)} %get-tuple-element.37), channel_id=1, replica_groups=mesh['z'=8,'x_lo'=2,'core'=2,'y'=4,'x_hi'=2] {'y','x_hi'}, dimensions={0} | all-to-all | bytes 2097152 | tf_op jit(solution)/shard_map/mixed_exchange/all_to_all | solution.py:442
  31.2 3.6 %all-to-all-start.2 = ((bf16[8,2,32,1024]{3,2,1,0:T(8,128)(2,1)}), bf16[8,2,32,1024]{3,2,1,0:T(8,128)(2,1)S(1)}, u32[]{:S(2)}, u32[]{:S(2)}) async-start(bf16[8,2,32,1024]{3,2,1,0:T(8,128)(2,1)} %slope.1), calls=%async_computation.2 | async-start | bytes 2097152 | tf_op jit(solution)/shard_map/slope_share/all_to_all | solution.py:455
  34.8 5.8 %forward.2 = (bf16[2,256,1024]{2,1,0:T(8,128)(2,1)}, f32[2,32,1024]{2,1,0:T(8,128)}, f32[2,256,512]{2,1,0:T(8,128)}, bf16[2,32,1024]{2,1,0:T(8,128)(2,1)}, bf16[...) custom-call(s32[3]{0:T(128)} %get-tuple-element.45.scalar_ref, ...), custom_call_target="tpu_custom_call" | custom-call | tf_op jit(solution)/shard_map/forward/pallas_call | solution.py:98
  41.8 7.9 %all-to-all-done.2.refs_0_ = bf16[8,2,32,1024]{3,2,1,0:T(8,128)(2,1)S(1)} async-done(((bf16[8,2,32,1024]{3,2,1,0:T(8,128)(2,1)}), bf16[8,2,32,1024]{3,2,1,0:T(8,128)(2,1)S(1)}, u32[]{:S(2)}, u32[]{:S(2)}) %all-to-all-start.2) | async-done | bytes 1048608 | tf_op jit(solution)/shard_map/slope_share/all_to_all | solution.py:455
  51.9 3.4 %derivatives.3 = bf16[32,2,32,512]{3,2,1,0:T(8,128)(2,1)} custom-call(f32[1]{0:T(128)S(6)} %div.4.scale_ref, bf16[2,256,1024]{2,1,0:T(8,128)(2,1)S(1)} %copy-done.4, f32[2,256,512]{2,1,0:T(8,128)S(1)} %copy-done.5, bf16[1024,512]{1,0:T(8,128)(2,1)S(1)} %copy-done, bf16[8,2,32,1024]{3,2,1,0:T(8,128)(2,1)S(1)} %all-to-all-done.2.refs_0_, ...), custom_call_target="tpu_custom_call" | custom-call | tf_op jit(solution)/shard_map/derivatives/pallas_call | solution.py:163
  55.3 12.0 %all-to-all-start.3 = ((bf16[32,2,32,512]{3,2,1,0:T(8,128)(2,1)}), bf16[32,2,32,512]{3,2,1,0:T(8,128)(2,1)}, u32[]{:S(2)}, u32[]{:S(2)}) async-start(bf16[32,2,32,512]{3,2,1,0:T(8,128)(2,1)} %derivatives.3), calls=%async_computation.3 | async-start | bytes 4194304 | tf_op jit(solution)/shard_map/derivative_exchange/all_to_all | solution.py:464
  68.8 2.7 %collective-permute-start.2 = (bf16[2,32,1024]{2,1,0:T(8,128)(2,1)}, bf16[2,32,1024]{2,1,0:T(8,128)(2,1)S(1)}, u32[]{:S(2)}, u32[]{:S(2)}) collective-permute-start(bf16[2,32,1024]{2,1,0:T(8,128)(2,1)} %get-tuple-element.30), channel_id=1, source_target_pairs={{0,3},{1,2},{2,1},{3,0},{4,7},{5,6},{6,5},{7,4},{8,11},{9,10},{10,... | collective-permute-start | bytes 393224 | tf_op jit(solution)/shard_map/mixed_exchange/ppermute | solution.py:404
  72.1 3.3 %collective-permute-start.4 = (bf16[2,32,1024]{2,1,0:T(8,128)(2,1)}, bf16[2,32,1024]{2,1,0:T(8,128)(2,1)S(1)}, u32[]{:S(2)}, u32[]{:S(2)}) collective-permute-start(bf16[2,32,1024]{2,1,0:T(8,128)(2,1)} %get-tuple-element.32), channel_id=1, source_target_pairs={{0,5},{1,4},{2,7},{3,6},{4,1},{5,0},{6,3},{7,2},{8,13},{9,12},{10,... | collective-permute-start | bytes 393224 | tf_op jit(solution)/shard_map/mixed_exchange/ppermute | solution.py:404
  75.4 2.6 %collective-permute-done = bf16[2,32,1024]{2,1,0:T(8,128)(2,1)S(1)} collective-permute-done((bf16[2,32,1024]{2,1,0:T(8,128)(2,1)}, bf16[2,32,1024]{2,1,0:T(8,128)(2,1)S(1)}, u32[]{:S(2)}, u32[]{:S(2)}) %collective-permute-start) | collective-permute-done | bytes 131104 | tf_op jit(solution)/shard_map/mixed_exchange/ppermute | solution.py:404
  78.9 3.4 %collective-permute-start.6 = (bf16[2,32,1024]{2,1,0:T(8,128)(2,1)}, bf16[2,32,1024]{2,1,0:T(8,128)(2,1)S(1)}, u32[]{:S(2)}, u32[]{:S(2)}) collective-permute-start(bf16[2,32,1024]{2,1,0:T(8,128)(2,1)} %get-tuple-element.34), channel_id=1, source_target_pairs={{0,7},{1,6},{2,5},{3,4},{4,3},{5,2},{6,1},{7,0},{8,15},{9,14},{10,... | collective-permute-start | bytes 393224 | tf_op jit(solution)/shard_map/mixed_exchange/ppermute | solution.py:404
  82.2 3.4 %collective-permute-done.2 = bf16[2,32,1024]{2,1,0:T(8,128)(2,1)S(1)} collective-permute-done((bf16[2,32,1024]{2,1,0:T(8,128)(2,1)}, bf16[2,32,1024]{2,1,0:T(8,128)(2,1)S(1)}, u32[]{:S(2)}, u32[]{:S(2)}) %collective-permute-start.2) | collective-permute-done | bytes 131104 | tf_op jit(solution)/shard_map/mixed_exchange/ppermute | solution.py:404
  85.6 5.1 %collective-permute-done.4 = bf16[2,32,1024]{2,1,0:T(8,128)(2,1)S(1)} collective-permute-done((bf16[2,32,1024]{2,1,0:T(8,128)(2,1)}, bf16[2,32,1024]{2,1,0:T(8,128)(2,1)S(1)}, u32[]{:S(2)}, u32[]{:S(2)}) %collective-permute-start.4) | collective-permute-done | bytes 131104 | tf_op jit(solution)/shard_map/mixed_exchange/ppermute | solution.py:404
  90.7 3.5 %collective-permute-done.6 = bf16[2,32,1024]{2,1,0:T(8,128)(2,1)S(1)} collective-permute-done((bf16[2,32,1024]{2,1,0:T(8,128)(2,1)}, bf16[2,32,1024]{2,1,0:T(8,128)(2,1)S(1)}, u32[]{:S(2)}, u32[]{:S(2)}) %collective-permute-start.6) | collective-permute-done | bytes 131104 | tf_op jit(solution)/shard_map/mixed_exchange/ppermute | solution.py:404
  94.5 3.6 %collective-permute-start.13 = (bf16[2,32,1024]{2,1,0:T(8,128)(2,1)S(1)}, bf16[2,32,1024]{2,1,0:T(8,128)(2,1)S(1)}, u32[]{:S(2)}, u32[]{:S(2)}) collective-permute-start(bf16[2,32,1024]{2,1,0:T(8,128)(2,1)S(1)} %multiply_convert_fusion.refs_0_), channel_id=1, source_target_pairs={{0,7},{1,6},{2,5},{3,4},{4,3},{5,2},{6,1},{7,0},{8,15},{9,14},{10,... | collective-permute-start | bytes 393224 | tf_op jit(solution)/shard_map/slope_share/ppermute | solution.py:404
  99.7 2.9 %collective-permute-start.10 = (bf16[2,32,1024]{2,1,0:T(8,128)(2,1)S(1)}, bf16[2,32,1024]{2,1,0:T(8,128)(2,1)S(1)}, u32[]{:S(2)}, u32[]{:S(2)}) collective-permute-start(bf16[2,32,1024]{2,1,0:T(8,128)(2,1)S(1)} %multiply_convert_fusion.refs_0_), channel_id=1, source_target_pairs={{0,4},{1,5},{2,6},{3,7},{4,0},{5,1},{6,2},{7,3},{8,12},{9,13},{10,... | collective-permute-start | bytes 393224 | tf_op jit(solution)/shard_map/slope_share/ppermute | solution.py:404
  103.7 2.3 collective-permute-done.13.refs_7_
  105.9 4.7 %collective-permute-done.12.refs_6_ = bf16[2,32,1024]{2,1,0:T(8,128)(2,1)S(1)} collective-permute-done((bf16[2,32,1024]{2,1,0:T(8,128)(2,1)S(1)}, bf16[2,32,1024]{2,1,0:T(8,128)(2,1)S(1)}, u32[]{:S(2)}, u32[]{:S(2)}) %collective-permute-start.12) | collective-permute-done | bytes 131104 | tf_op jit(solution)/shard_map/slope_share/ppermute | solution.py:404
  112.3 2.8 %collective-permute-done.9.refs_3_ = bf16[2,32,1024]{2,1,0:T(8,128)(2,1)S(1)} collective-permute-done((bf16[2,32,1024]{2,1,0:T(8,128)(2,1)S(1)}, bf16[2,32,1024]{2,1,0:T(8,128)(2,1)S(1)}, u32[]{:S(2)}, u32[]{:S(2)}) %collective-permute-start.9) | collective-permute-done | bytes 131104 | tf_op jit(solution)/shard_map/slope_share/ppermute | solution.py:404
  115.1 2.0 collective-permute-done.7.refs_1_
  117.1 3.3 %derivatives.2 = bf16[32,2,32,512]{3,2,1,0:T(8,128)(2,1)} custom-call(f32[1]{0:T(128)S(6)} %div.4.scale_ref, bf16[2,256,1024]{2,1,0:T(8,128)(2,1)S(1)} %copy-done.2, f32[2,256,512]{2,1,0:T(8,128)S(1)} %copy-done.3, bf16[1024,512]{1,0:T(8,128)(2,1)S(1)} %copy-done, bf16[2,32,1024]{2,1,0:T(8,128)(2,1)S(1)} %multiply_convert_fusion.refs_0_, ...), custom_call_target="tpu_custom_call" | custom-call | tf_op jit(solution)/shard_map/derivatives/pallas_call | solution.py:163
  120.4 10.0 %all-to-all-start = ((bf16[32,2,32,512]{3,2,1,0:T(8,128)(2,1)}), bf16[32,2,32,512]{3,2,1,0:T(8,128)(2,1)S(1)}, u32[]{:S(2)}, u32[]{:S(2)}) async-start(bf16[32,2,32,512]{3,2,1,0:T(8,128)(2,1)} %derivatives.2), calls=%async_computation | async-start | bytes 4194304 | tf_op jit(solution)/shard_map/derivative_exchange/all_to_all | solution.py:464
  130.9 5.3 %gram.2 = (bf16[32,64,512]{2,1,0:T(8,128)(2,1)}, f32[4,2048,128]{2,1,0:T(8,128)}) custom-call(bf16[64,32,512]{2,1,0:T(8,128)(2,1)} %bitcast.6.code_ref), custom_call_target="tpu_custom_call" | custom-call | tf_op jit(solution)/shard_map/gram/pallas_call | solution.py:221
  136.2 44.3 %all-to-all-done = bf16[32,2,32,512]{3,2,1,0:T(8,128)(2,1)S(1)} async-done(((bf16[32,2,32,512]{3,2,1,0:T(8,128)(2,1)}), bf16[32,2,32,512]{3,2,1,0:T(8,128)(2,1)S(1)}, u32[]{:S(2)}, u32[]{:S(2)}) %all-to-all-start) | async-done | bytes 2097184 | tf_op jit(solution)/shard_map/derivative_exchange/all_to_all | solution.py:464
  180.5 1.6 copy-done.1
  182.1 4.9 %gram.3 = (f32[128,128]{1,0:T(8,128)S(1)}, f32[4,2048,128]{2,1,0:T(8,128)}) custom-call(f32[1,128]{1,0:T(1,128)S(1)} %broadcast_select_fusion.energy_ref, bf16[64,32,512]{2,1,0:T(8,128)(2,1)S(1)} %bitcast.10, bf16[32,64,512]{2,1,0:T(8,128)(2,1)S(1)} %copy-done.1), custom_call_target="tpu_custom_call" | custom-call | tf_op jit(solution)/shard_map/gram/pallas_call | solution.py:271
  187.0 10.6 %all_to_all.36 = f32[16,8,128]{2,1,0:T(8,128)S(1)} all-to-all(f32[16,8,128]{2,1,0:T(8,128)S(1)} %bitcast.11), channel_id=1, replica_groups=mesh['z'=8,'x_lo'=2,'core'=2,'y'=4,'x_hi'=2] {'x_lo','core','y'}, dimensions={0} | all-to-all | bytes 131072 | tf_op jit(solution)/shard_map/gram_sum/all_to_all | solution.py:472
  198.3 4.7 %all-to-all-start.5 = ((f32[16,8,128]{2,1,0:T(8,128)}), f32[16,8,128]{2,1,0:T(8,128)S(1)}, u32[]{:S(2)}, u32[]{:S(2)}) async-start(f32[16,8,128]{2,1,0:T(8,128)} %broadcast_in_dim.13), calls=%async_computation.5 | async-start | bytes 131072 | tf_op jit(solution)/shard_map/gram_sum/all_to_all | solution.py:38
  203.6 8.8 %all-to-all-done.5 = f32[16,8,128]{2,1,0:T(8,128)S(1)} async-done(((f32[16,8,128]{2,1,0:T(8,128)}), f32[16,8,128]{2,1,0:T(8,128)S(1)}, u32[]{:S(2)}, u32[]{:S(2)}) %all-to-all-start.5) | async-done | bytes 65568 | tf_op jit(solution)/shard_map/gram_sum/all_to_all | solution.py:38
  213.0 5.1 %all-to-all-start.6 = ((f32[16,8,128]{2,1,0:T(8,128)}), f32[16,8,128]{2,1,0:T(8,128)S(1)}, u32[]{:S(2)}, u32[]{:S(2)}) async-start(f32[16,8,128]{2,1,0:T(8,128)} %broadcast_in_dim.14), calls=%async_computation.6 | async-start | bytes 131072 | tf_op jit(solution)/shard_map/gram_sum/all_to_all | solution.py:38
  218.7 5.3 %all-to-all-done.6.shared_ref = f32[16,8,128]{2,1,0:T(8,128)S(1)} async-done(((f32[16,8,128]{2,1,0:T(8,128)}), f32[16,8,128]{2,1,0:T(8,128)S(1)}, u32[]{:S(2)}, u32[]{:S(2)}) %all-to-all-start.6) | async-done | bytes 65568 | tf_op jit(solution)/shard_map/gram_sum/all_to_all | solution.py:38
  224.6 5.7 %solve.1 = f32[32,512]{1,0:T(8,128)} custom-call(f32[2]{0:T(128)} %pad_maximum_fusion.scalar_ref, f32[16,8,128]{2,1,0:T(8,128)} %copy-done.10, f32[4,2048,128]{2,1,0:T(8,128)} %get-tuple-element.41.refs_0_, f32[4,2048,128]{2,1,0:T(8,128)} %get-tuple-element.42.refs_1_), custom_call_target="tpu_custom_call" | custom-call | tf_op jit(solution)/shard_map/solve/pallas_call | solution.py:365
  (56 shorter events, 15.2 us)
Async XLA Ops:
  6.1 23.9 %copy-start.8 = (f32[2,32,1024]{2,1,0:T(8,128)S(1)}, f32[2,32,1024]{2,1,0:T(8,128)}, u32[]{:S(2)}) copy-start(f32[2,32,1024]{2,1,0:T(8,128)} %get-tuple-element.38.own_ref) | copy-start | bytes 786436
  6.1 23.9 %copy-start.9 = (bf16[1024]{0:T(1024)(128)(2,1)S(1)}, bf16[1024]{0:T(1024)(128)(2,1)}, u32[]{:S(2)}) copy-start(bf16[1024]{0:T(1024)(128)(2,1)} %readout_ref.1) | copy-start | bytes 6148
  31.2 18.6 %all-to-all-start.2 = ((bf16[8,2,32,1024]{3,2,1,0:T(8,128)(2,1)}), bf16[8,2,32,1024]{3,2,1,0:T(8,128)(2,1)S(1)}, u32[]{:S(2)}, u32[]{:S(2)}) async-start(bf16[8,2,32,1024]{3,2,1,0:T(8,128)(2,1)} %slope.1), calls=%async_computation.2 | async-start | bytes 2097152 | tf_op jit(solution)/shard_map/slope_share/all_to_all | solution.py:455
  34.8 15.0 %copy-start = (bf16[1024,512]{1,0:T(8,128)(2,1)S(1)}, bf16[1024,512]{1,0:T(8,128)(2,1)}, u32[]{:S(2)}) copy-start(bf16[1024,512]{1,0:T(8,128)(2,1)} %down_ref.7) | copy-start | bytes 3145732
  34.8 15.0 %copy-start.4 = (bf16[2,256,1024]{2,1,0:T(8,128)(2,1)S(1)}, bf16[2,256,1024]{2,1,0:T(8,128)(2,1)}, u32[]{:S(2)}) copy-start(bf16[2,256,1024]{2,1,0:T(8,128)(2,1)} %get-tuple-element.35.normed_ref) | copy-start | bytes 3145732
  49.8 1.2 copy-start.5
  51.0 0.9 copy-start.6
  55.3 39.0 %copy-start.7 = (bf16[2,32,1024]{2,1,0:T(8,128)(2,1)S(1)}, bf16[2,32,1024]{2,1,0:T(8,128)(2,1)}, u32[]{:S(2)}) copy-start(bf16[2,32,1024]{2,1,0:T(8,128)(2,1)} %get-tuple-element.27.refs_1_) | copy-start | bytes 393220
  55.3 39.0 %copy-start.11 = (f32[2,32,1024]{2,1,0:T(8,128)S(1)}, f32[2,32,1024]{2,1,0:T(8,128)}, u32[]{:S(2)}) copy-start(f32[2,32,1024]{2,1,0:T(8,128)} %get-tuple-element.26) | copy-start | bytes 786436
  55.3 61.8 %copy-start.2 = (bf16[2,256,1024]{2,1,0:T(8,128)(2,1)S(1)}, bf16[2,256,1024]{2,1,0:T(8,128)(2,1)}, u32[]{:S(2)}) copy-start(bf16[2,256,1024]{2,1,0:T(8,128)(2,1)} %get-tuple-element.24.normed_ref) | copy-start | bytes 3145732
  55.3 61.8 %copy-start.3 = (f32[2,256,512]{2,1,0:T(8,128)S(1)}, f32[2,256,512]{2,1,0:T(8,128)}, u32[]{:S(2)}) copy-start(f32[2,256,512]{2,1,0:T(8,128)} %get-tuple-element.25.bend_ref) | copy-start | bytes 3145732
  55.3 65.1 %all-to-all-start.3 = ((bf16[32,2,32,512]{3,2,1,0:T(8,128)(2,1)}), bf16[32,2,32,512]{3,2,1,0:T(8,128)(2,1)}, u32[]{:S(2)}, u32[]{:S(2)}) async-start(bf16[32,2,32,512]{3,2,1,0:T(8,128)(2,1)} %derivatives.3), calls=%async_computation.3 | async-start | bytes 4194304 | tf_op jit(solution)/shard_map/derivative_exchange/all_to_all | solution.py:464
  67.3 10.6 %collective-permute-start = (bf16[2,32,1024]{2,1,0:T(8,128)(2,1)}, bf16[2,32,1024]{2,1,0:T(8,128)(2,1)S(1)}, u32[]{:S(2)}, u32[]{:S(2)}) collective-permute-start(bf16[2,32,1024]{2,1,0:T(8,128)(2,1)} %get-tuple-element.28), channel_id=1, source_target_pairs={{0,1},{1,0},{2,3},{3,2},{4,5},{5,4},{6,7},{7,6},{8,9},{9,8},{10,11... | collective-permute-start | bytes 393224 | tf_op jit(solution)/shard_map/mixed_exchange/ppermute | solution.py:404
  68.5 10.3 %collective-permute-start.1 = (bf16[2,32,1024]{2,1,0:T(8,128)(2,1)}, bf16[2,32,1024]{2,1,0:T(8,128)(2,1)S(1)}, u32[]{:S(2)}, u32[]{:S(2)}) collective-permute-start(bf16[2,32,1024]{2,1,0:T(8,128)(2,1)} %get-tuple-element.29), channel_id=1, source_target_pairs={{0,2},{1,3},{2,0},{3,1},{4,6},{5,7},{6,4},{7,5},{8,10},{9,11},{10,... | collective-permute-start | bytes 393224 | tf_op jit(solution)/shard_map/mixed_exchange/ppermute | solution.py:404
  68.8 16.7 %collective-permute-start.2 = (bf16[2,32,1024]{2,1,0:T(8,128)(2,1)}, bf16[2,32,1024]{2,1,0:T(8,128)(2,1)S(1)}, u32[]{:S(2)}, u32[]{:S(2)}) collective-permute-start(bf16[2,32,1024]{2,1,0:T(8,128)(2,1)} %get-tuple-element.30), channel_id=1, source_target_pairs={{0,3},{1,2},{2,1},{3,0},{4,7},{5,6},{6,5},{7,4},{8,11},{9,10},{10,... | collective-permute-start | bytes 393224 | tf_op jit(solution)/shard_map/mixed_exchange/ppermute | solution.py:404
  71.6 14.0 %collective-permute-start.3 = (bf16[2,32,1024]{2,1,0:T(8,128)(2,1)}, bf16[2,32,1024]{2,1,0:T(8,128)(2,1)S(1)}, u32[]{:S(2)}, u32[]{:S(2)}) collective-permute-start(bf16[2,32,1024]{2,1,0:T(8,128)(2,1)} %get-tuple-element.31), channel_id=1, source_target_pairs={{0,4},{1,5},{2,6},{3,7},{4,0},{5,1},{6,2},{7,3},{8,12},{9,13},{10,... | collective-permute-start | bytes 393224 | tf_op jit(solution)/shard_map/mixed_exchange/ppermute | solution.py:404
  72.1 18.6 %collective-permute-start.4 = (bf16[2,32,1024]{2,1,0:T(8,128)(2,1)}, bf16[2,32,1024]{2,1,0:T(8,128)(2,1)S(1)}, u32[]{:S(2)}, u32[]{:S(2)}) collective-permute-start(bf16[2,32,1024]{2,1,0:T(8,128)(2,1)} %get-tuple-element.32), channel_id=1, source_target_pairs={{0,5},{1,4},{2,7},{3,6},{4,1},{5,0},{6,3},{7,2},{8,13},{9,12},{10,... | collective-permute-start | bytes 393224 | tf_op jit(solution)/shard_map/mixed_exchange/ppermute | solution.py:404
  78.0 12.8 %collective-permute-start.5 = (bf16[2,32,1024]{2,1,0:T(8,128)(2,1)}, bf16[2,32,1024]{2,1,0:T(8,128)(2,1)S(1)}, u32[]{:S(2)}, u32[]{:S(2)}) collective-permute-start(bf16[2,32,1024]{2,1,0:T(8,128)(2,1)} %get-tuple-element.33), channel_id=1, source_target_pairs={{0,6},{1,7},{2,4},{3,5},{4,2},{5,3},{6,0},{7,1},{8,14},{9,15},{10,... | collective-permute-start | bytes 393224 | tf_op jit(solution)/shard_map/mixed_exchange/ppermute | solution.py:404
  78.9 15.4 %collective-permute-start.6 = (bf16[2,32,1024]{2,1,0:T(8,128)(2,1)}, bf16[2,32,1024]{2,1,0:T(8,128)(2,1)S(1)}, u32[]{:S(2)}, u32[]{:S(2)}) collective-permute-start(bf16[2,32,1024]{2,1,0:T(8,128)(2,1)} %get-tuple-element.34), channel_id=1, source_target_pairs={{0,7},{1,6},{2,5},{3,4},{4,3},{5,2},{6,1},{7,0},{8,15},{9,14},{10,... | collective-permute-start | bytes 393224 | tf_op jit(solution)/shard_map/mixed_exchange/ppermute | solution.py:404
  94.5 11.5 %collective-permute-start.13 = (bf16[2,32,1024]{2,1,0:T(8,128)(2,1)S(1)}, bf16[2,32,1024]{2,1,0:T(8,128)(2,1)S(1)}, u32[]{:S(2)}, u32[]{:S(2)}) collective-permute-start(bf16[2,32,1024]{2,1,0:T(8,128)(2,1)S(1)} %multiply_convert_fusion.refs_0_), channel_id=1, source_target_pairs={{0,7},{1,6},{2,5},{3,4},{4,3},{5,2},{6,1},{7,0},{8,15},{9,14},{10,... | collective-permute-start | bytes 393224 | tf_op jit(solution)/shard_map/slope_share/ppermute | solution.py:404
  98.0 12.7 %collective-permute-start.12 = (bf16[2,32,1024]{2,1,0:T(8,128)(2,1)S(1)}, bf16[2,32,1024]{2,1,0:T(8,128)(2,1)S(1)}, u32[]{:S(2)}, u32[]{:S(2)}) collective-permute-start(bf16[2,32,1024]{2,1,0:T(8,128)(2,1)S(1)} %multiply_convert_fusion.refs_0_), channel_id=1, source_target_pairs={{0,6},{1,7},{2,4},{3,5},{4,2},{5,3},{6,0},{7,1},{8,14},{9,15},{10,... | collective-permute-start | bytes 393224 | tf_op jit(solution)/shard_map/slope_share/ppermute | solution.py:404
  98.6 13.7 %collective-permute-start.11 = (bf16[2,32,1024]{2,1,0:T(8,128)(2,1)S(1)}, bf16[2,32,1024]{2,1,0:T(8,128)(2,1)S(1)}, u32[]{:S(2)}, u32[]{:S(2)}) collective-permute-start(bf16[2,32,1024]{2,1,0:T(8,128)(2,1)S(1)} %multiply_convert_fusion.refs_0_), channel_id=1, source_target_pairs={{0,5},{1,4},{2,7},{3,6},{4,1},{5,0},{6,3},{7,2},{8,13},{9,12},{10,... | collective-permute-start | bytes 393224 | tf_op jit(solution)/shard_map/slope_share/ppermute | solution.py:404
  99.7 12.6 %collective-permute-start.10 = (bf16[2,32,1024]{2,1,0:T(8,128)(2,1)S(1)}, bf16[2,32,1024]{2,1,0:T(8,128)(2,1)S(1)}, u32[]{:S(2)}, u32[]{:S(2)}) collective-permute-start(bf16[2,32,1024]{2,1,0:T(8,128)(2,1)S(1)} %multiply_convert_fusion.refs_0_), channel_id=1, source_target_pairs={{0,4},{1,5},{2,6},{3,7},{4,0},{5,1},{6,2},{7,3},{8,12},{9,13},{10,... | collective-permute-start | bytes 393224 | tf_op jit(solution)/shard_map/slope_share/ppermute | solution.py:404
  102.6 12.5 %collective-permute-start.9 = (bf16[2,32,1024]{2,1,0:T(8,128)(2,1)S(1)}, bf16[2,32,1024]{2,1,0:T(8,128)(2,1)S(1)}, u32[]{:S(2)}, u32[]{:S(2)}) collective-permute-start(bf16[2,32,1024]{2,1,0:T(8,128)(2,1)S(1)} %multiply_convert_fusion.refs_0_), channel_id=1, source_target_pairs={{0,3},{1,2},{2,1},{3,0},{4,7},{5,6},{6,5},{7,4},{8,11},{9,10},{10,... | collective-permute-start | bytes 393224 | tf_op jit(solution)/shard_map/slope_share/ppermute | solution.py:404
  105.9 9.1 %collective-permute-start.8 = (bf16[2,32,1024]{2,1,0:T(8,128)(2,1)S(1)}, bf16[2,32,1024]{2,1,0:T(8,128)(2,1)S(1)}, u32[]{:S(2)}, u32[]{:S(2)}) collective-permute-start(bf16[2,32,1024]{2,1,0:T(8,128)(2,1)S(1)} %multiply_convert_fusion.refs_0_), channel_id=1, source_target_pairs={{0,2},{1,3},{2,0},{3,1},{4,6},{5,7},{6,4},{7,5},{8,10},{9,11},{10,... | collective-permute-start | bytes 393224 | tf_op jit(solution)/shard_map/slope_share/ppermute | solution.py:404
  110.7 6.4 %collective-permute-start.7 = (bf16[2,32,1024]{2,1,0:T(8,128)(2,1)S(1)}, bf16[2,32,1024]{2,1,0:T(8,128)(2,1)S(1)}, u32[]{:S(2)}, u32[]{:S(2)}) collective-permute-start(bf16[2,32,1024]{2,1,0:T(8,128)(2,1)S(1)} %multiply_convert_fusion.refs_0_), channel_id=1, source_target_pairs={{0,1},{1,0},{2,3},{3,2},{4,5},{5,4},{6,7},{7,6},{8,9},{9,8},{10,11... | collective-permute-start | bytes 393224 | tf_op jit(solution)/shard_map/slope_share/ppermute | solution.py:404
  120.4 10.0 %copy-start.12 = (f32[4]{0:T(128)S(1)}, f32[4]{0:T(128)}, u32[]{:S(2)}) copy-start(f32[4]{0:T(128)} %param.16) | copy-start | bytes 52
  120.4 60.1 %all-to-all-start = ((bf16[32,2,32,512]{3,2,1,0:T(8,128)(2,1)}), bf16[32,2,32,512]{3,2,1,0:T(8,128)(2,1)S(1)}, u32[]{:S(2)}, u32[]{:S(2)}) async-start(bf16[32,2,32,512]{3,2,1,0:T(8,128)(2,1)} %derivatives.2), calls=%async_computation | async-start | bytes 4194304 | tf_op jit(solution)/shard_map/derivative_exchange/all_to_all | solution.py:464
  180.5 1.6 copy-start.1
  198.3 14.1 %all-to-all-start.5 = ((f32[16,8,128]{2,1,0:T(8,128)}), f32[16,8,128]{2,1,0:T(8,128)S(1)}, u32[]{:S(2)}, u32[]{:S(2)}) async-start(f32[16,8,128]{2,1,0:T(8,128)} %broadcast_in_dim.13), calls=%async_computation.5 | async-start | bytes 131072 | tf_op jit(solution)/shard_map/gram_sum/all_to_all | solution.py:38
  213.0 11.0 %all-to-all-start.6 = ((f32[16,8,128]{2,1,0:T(8,128)}), f32[16,8,128]{2,1,0:T(8,128)S(1)}, u32[]{:S(2)}, u32[]{:S(2)}) async-start(f32[16,8,128]{2,1,0:T(8,128)} %broadcast_in_dim.14), calls=%async_computation.6 | async-start | bytes 131072 | tf_op jit(solution)/shard_map/gram_sum/all_to_all | solution.py:38
  224.0 0.6 copy-start.10

commit v4 on v3

--- a/solution.py
+++ b/solution.py
@@ -75,25 +75,24 @@
     ).astype(jnp.bfloat16)
     for k in range(blocks):
         part = mixed[k * rows : (k + 1) * rows]
-        if len(part_refs) == 1:
-            part_refs[0][k, 0] = part
-        else:
-            part_refs[k][0] = part
-
-
-def forward(order, own, spins, features, embed, gain, up, down, first, samples, apart):
+        per_ref = part_refs[0].shape[0]
+        part_refs[k // per_ref][k % per_ref, 0] = part
+
+
+def forward(order, own, spins, features, embed, gain, up, down, first, samples, pairs):
     _, blocks, rows, width = features.shape
     hidden = up.shape[1]
     tokens = blocks * rows
     whole = lambda array: pl.BlockSpec(array.shape, lambda s: (0,) * array.ndim)
     block = lambda *shape: pl.BlockSpec((1,) + shape, lambda s: (s,) + (0,) * len(shape))
     result = lambda dtype, *shape: jax.ShapeDtypeStruct((samples,) + shape, dtype)
-    if not apart:
-        part_specs = [pl.BlockSpec((blocks, 1, rows, width), lambda s: (0, s, 0, 0))]
-        part_shapes = [jax.ShapeDtypeStruct((blocks, samples, rows, width), jnp.bfloat16)]
-    else:
-        part_specs = [block(rows, width)] * blocks
-        part_shapes = [result(jnp.bfloat16, rows, width)] * blocks
+    together = 2 if pairs else blocks
+    part_specs = [pl.BlockSpec((together, 1, rows, width), lambda s: (0, s, 0, 0))] * (
+        blocks // together
+    )
+    part_shapes = [jax.ShapeDtypeStruct((together, samples, rows, width), jnp.bfloat16)] * (
+        blocks // together
+    )
     scalars = jnp.stack([order, own, jnp.int32(first)])
     return pl.pallas_call(
         forward_kernel,
@@ -143,10 +142,7 @@
 def derivative_kernel(slope_count, scale_ref, normed_ref, bend_ref, down_ref, *refs):
     slope_refs, coded_ref = refs[:slope_count], refs[-1]
     tokens, width = normed_ref.shape[1:]
-    if len(slope_refs) == 1:
-        slope = slope_refs[0][:, 0].reshape(tokens, width)
-    else:
-        slope = jnp.concatenate([r[0] for r in slope_refs], axis=0)
+    slope = jnp.concatenate([r[:, 0].reshape(-1, width) for r in slope_refs], axis=0)
     back_proj = jnp.dot(slope, down_ref[...], preferred_element_type=jnp.float32)
     pullback = (bend_ref[0] * back_proj).astype(jnp.bfloat16)
     deriv = lax.dot_general(
@@ -170,12 +166,10 @@
             pl.BlockSpec(down.shape, lambda s: (0, 0)),
         ]
         + [
-            block(*a.shape[1:])
-            if a.ndim == 3
-            else pl.BlockSpec((a.shape[0], 1) + a.shape[2:], lambda s: (0, s, 0, 0))
+            pl.BlockSpec((a.shape[0], 1) + a.shape[2:], lambda s: (0, s, 0, 0))
             for a in slopes
         ]
-        + [pl.BlockSpec((1, 16, 128), lambda s: (0, 0, 0))] * len(after),
+        + [pl.BlockSpec((1, 1, 16, 128), lambda s: (0, 0, 0, 0))] * len(after),
         out_specs=pl.BlockSpec((parts, 1, width // parts, hidden), lambda s: (0, s, 0, 0)),
         out_shape=jax.ShapeDtypeStruct((parts, samples, width // parts, hidden), jnp.bfloat16),
         compiler_params=pltpu.CompilerParams(vmem_limit_bytes=VMEM_SMALL),
@@ -441,20 +435,25 @@
             if n == 0:
                 mixed_parts = lax.all_to_all(parts[0], MP, 0, 0)
             else:
-                mixed_parts = parts[:1] + [partner(parts[k], k) for k in range(1, mp_size)]
+                pairs = parts[:1] + [partner(pair, 2 * j) for j, pair in enumerate(parts) if j]
+                mixed_own = own_inputs
+                mixed_other = 0.0
+                for pair in pairs:
+                    mixed_own = mixed_own + pair[0].astype(jnp.float32)
+                    mixed_other = mixed_other + pair[1].astype(jnp.float32)
+                mixed_other = partner(mixed_other.astype(jnp.bfloat16), 1)
         with jax.named_scope("slope"):
             if n == 0:
                 slope = own_slope(mixed_parts, own_inputs, readout)
             else:
-                outputs = own_inputs
-                for part in mixed_parts:
-                    outputs = outputs + part.astype(jnp.float32)
+                outputs = mixed_own + mixed_other.astype(jnp.float32)
                 slope = (readout_wide * jnp.tanh(outputs)).astype(jnp.bfloat16)
         with jax.named_scope("slope_share"):
             if n == 0:
                 slopes = [lax.all_to_all(slope, MP, 0, 0)]
             else:
-                slopes = [slope] + [partner(slope, k) for k in range(1, mp_size)]
+                pair = jnp.stack([slope, partner(slope, 1)])
+                slopes = [pair] + [partner(pair, 2 * j) for j in range(1, mp_size // 2)]
         with jax.named_scope("derivatives"):
             after = [state[3] for state in states[n + 1 : n + 2]]
             coded_chunks.append(

time: 231 us -> 226 us (0.978)
  starting transfers between devices: 56.9 us -> 45.2 us
  waiting for transfers between devices: 94.2 us -> 102 us
    ppermute x14 -> x8, starting transfers between devices: 21.6 us -> 11.1 us  [partner(): return lax.ppermute(array, MP, [(i, i ^ k) for i in range(mp_size)])]
    ppermute x14 -> x8, waiting for transfers between devices: 27.9 us -> 34.7 us  [partner(): return lax.ppermute(array, MP, [(i, i ^ k) for i in range(mp_size)])]
  transfers between devices with their start and end apart: 19 -> 13, of which waited for: 13 -> 11; matrix products, arithmetic and copies ran while one was open for 1% -> 1% of each run, Pallas kernels for 6% -> 6%
where the time goes in v4:
time: 226 us; the launch traced here: 225 us
  waiting for transfers between devices  102 us (45%)
  starting transfers between devices  45.2 us (20%)
  Pallas kernels  34.9 us (15%)
  blocking collectives  33.5 us (15%)
  local copies, waits for them, and re-layouts  6.2 us (3%)
    all_to_all x2, waiting for transfers between devices, body(): chunks = [lax.all_to_all(c, SAMPLES, 0, 0) for c in coded_chunks]  44.7 us
    ppermute x8, waiting for transfers between devices, partner(): return lax.ppermute(array, MP, [(i, i ^ k) for i in range(mp_size)])  34.7 us
    all_to_all x1, blocking collectives, body(): mixed_parts = lax.all_to_all(parts[0], MP, 0, 0)  23.9 us
    all_to_all x2, starting transfers between devices, body(): chunks = [lax.all_to_all(c, SAMPLES, 0, 0) for c in coded_chunks]  20 us
    all_to_all x2, waiting for transfers between devices, share(): lax.all_to_all(jnp.broadcast_to(array, (size,) + array.shape), axis, 0, 0)  14 us
    ppermute x8, starting transfers between devices, partner(): return lax.ppermute(array, MP, [(i, i ^ k) for i in range(mp_size)])  11.1 us
    pallas_call x2, Pallas kernels, forward(): pl.pallas_call(forward_kernel, grid=(samples,), in_specs=[SMEM, whole(spi...  11.1 us
    all_to_all x2, starting transfers between devices, share(): lax.all_to_all(jnp.broadcast_to(array, (size,) + array.shape), axis, 0, 0)  10.6 us
  transfers between devices with their start and end apart: 13, of which 11 were waited for; matrix products, arithmetic and copies ran while one was open for 1% of the time, Pallas kernels for 6%

profile of v4, /device:TPU:1, one launch (start us, length us, event | category | flops | bytes accessed | tf_op | source)
XLA Modules:
  0.0 225.1 jit_solution(12450355409356820490)
XLA Ops:
  0.6 5.4 %forward.3 = (bf16[2,256,1024]{2,1,0:T(8,128)(2,1)}, f32[2,32,1024]{2,1,0:T(8,128)}, f32[2,256,512]{2,1,0:T(8,128)}, bf16[8,2,32,1024]{3,2,1,0:T(8,128)(2,1)}) custom-call(s32[3]{0:T(128)} %get-tuple-element.38.scalar_ref, s32[4,256]{1,0:T(4,128)} %spin_ref.3, bf16[4,8,32,1024]{3,2,1,0:T(8,128)(2,1)} %bitcast.34, bf16[1024]{0:T(1024)(128)(2,1)} %embed_ref.3, ...), custom_call_target="tpu_custom_call" | custom-call | tf_op jit(solution)/shard_map/forward/pallas_call | solution.py:97
  6.1 23.9 %all_to_all.35.part_ref = bf16[8,2,32,1024]{3,2,1,0:T(8,128)(2,1)S(1)} all-to-all(bf16[8,2,32,1024]{3,2,1,0:T(8,128)(2,1)} %get-tuple-element.29), channel_id=1, replica_groups=mesh['z'=8,'x_lo'=2,'core'=2,'y'=4,'x_hi'=2] {'y','x_hi'}, dimensions={0} | all-to-all | bytes 2097152 | tf_op jit(solution)/shard_map/mixed_exchange/all_to_all | solution.py:436
  30.0 1.2 slope.1
  31.2 3.6 %all-to-all-start.2 = ((bf16[8,2,32,1024]{3,2,1,0:T(8,128)(2,1)}), bf16[8,2,32,1024]{3,2,1,0:T(8,128)(2,1)S(1)}, u32[]{:S(2)}, u32[]{:S(2)}) async-start(bf16[8,2,32,1024]{3,2,1,0:T(8,128)(2,1)} %slope.1), calls=%async_computation.2 | async-start | bytes 2097152 | tf_op jit(solution)/shard_map/slope_share/all_to_all | solution.py:453
  34.8 5.6 %forward.2 = (bf16[2,256,1024]{2,1,0:T(8,128)(2,1)}, f32[2,32,1024]{2,1,0:T(8,128)}, f32[2,256,512]{2,1,0:T(8,128)}, bf16[2,2,32,1024]{3,2,1,0:T(8,128)(2,1)}, b...) custom-call(s32[3]{0:T(128)} %get-tuple-element.37.scalar_ref, ...), custom_call_target="tpu_custom_call" | custom-call | tf_op jit(solution)/shard_map/forward/pallas_call | solution.py:97
  41.7 8.1 %all-to-all-done.2.refs_0_ = bf16[8,2,32,1024]{3,2,1,0:T(8,128)(2,1)S(1)} async-done(((bf16[8,2,32,1024]{3,2,1,0:T(8,128)(2,1)}), bf16[8,2,32,1024]{3,2,1,0:T(8,128)(2,1)S(1)}, u32[]{:S(2)}, u32[]{:S(2)}) %all-to-all-start.2) | async-done | bytes 1048608 | tf_op jit(solution)/shard_map/slope_share/all_to_all | solution.py:453
  49.7 1.2 copy-done.5
  51.9 3.3 %derivatives.3 = bf16[32,2,32,512]{3,2,1,0:T(8,128)(2,1)} custom-call(f32[1]{0:T(128)S(6)} %div.4.scale_ref, bf16[2,256,1024]{2,1,0:T(8,128)(2,1)S(1)} %copy-done.4, f32[2,256,512]{2,1,0:T(8,128)S(1)} %copy-done.5, bf16[1024,512]{1,0:T(8,128)(2,1)S(1)} %copy-done, bf16[8,2,32,1024]{3,2,1,0:T(8,128)(2,1)S(1)} %all-to-all-done.2.refs_0_, ...), custom_call_target="tpu_custom_call" | custom-call | tf_op jit(solution)/shard_map/derivatives/pallas_call | solution.py:159
  55.3 12.0 %all-to-all-start.3 = ((bf16[32,2,32,512]{3,2,1,0:T(8,128)(2,1)}), bf16[32,2,32,512]{3,2,1,0:T(8,128)(2,1)}, u32[]{:S(2)}, u32[]{:S(2)}) async-start(bf16[32,2,32,512]{3,2,1,0:T(8,128)(2,1)} %derivatives.3), calls=%async_computation.3 | async-start | bytes 4194304 | tf_op jit(solution)/shard_map/derivative_exchange/all_to_all | solution.py:463
  67.5 1.7 collective-permute-start.1
  69.2 2.1 collective-permute-start.2
  71.3 3.8 %collective-permute-done = bf16[2,2,32,1024]{3,2,1,0:T(8,128)(2,1)S(1)} collective-permute-done((bf16[2,2,32,1024]{3,2,1,0:T(8,128)(2,1)S(1)}, bf16[2,2,32,1024]{3,2,1,0:T(8,128)(2,1)S(1)}, u32[]{:S(2)}, u32[]{:S(2)}) %collective-permute-start) | collective-permute-done | bytes 262176 | tf_op jit(solution)/shard_map/mixed_exchange/ppermute | solution.py:398
  75.1 5.8 %collective-permute-done.1 = bf16[2,2,32,1024]{3,2,1,0:T(8,128)(2,1)S(1)} collective-permute-done((bf16[2,2,32,1024]{3,2,1,0:T(8,128)(2,1)S(1)}, bf16[2,2,32,1024]{3,2,1,0:T(8,128)(2,1)S(1)}, u32[]{:S(2)}, u32[]{:S(2)}) %collective-permute-start.1) | collective-permute-done | bytes 262176 | tf_op jit(solution)/shard_map/mixed_exchange/ppermute | solution.py:398
  81.0 2.1 collective-permute-done.2
  83.1 1.5 collective-permute-start.3
  84.7 7.1 %collective-permute-done.3 = bf16[2,32,1024]{2,1,0:T(8,128)(2,1)S(1)} collective-permute-done((bf16[2,32,1024]{2,1,0:T(8,128)(2,1)S(1)}, bf16[2,32,1024]{2,1,0:T(8,128)(2,1)S(1)}, u32[]{:S(2)}, u32[]{:S(2)}) %collective-permute-start.3) | collective-permute-done | bytes 131104 | tf_op jit(solution)/shard_map/mixed_exchange/ppermute | solution.py:398
  91.9 1.5 collective-permute-start.4
  93.4 5.4 %collective-permute-done.4 = bf16[2,32,1024]{2,1,0:T(8,128)(2,1)S(1)} collective-permute-done((bf16[2,32,1024]{2,1,0:T(8,128)(2,1)S(1)}, bf16[2,32,1024]{2,1,0:T(8,128)(2,1)S(1)}, u32[]{:S(2)}, u32[]{:S(2)}) %collective-permute-start.4) | collective-permute-done | bytes 131104 | tf_op jit(solution)/shard_map/slope_share/ppermute | solution.py:398
  98.8 3.5 %collective-permute-start.7 = (bf16[2,2,32,1024]{3,2,1,0:T(8,128)(2,1)S(1)}, bf16[2,2,32,1024]{3,2,1,0:T(8,128)(2,1)S(1)}, u32[]{:S(2)}, u32[]{:S(2)}) collective-permute-start(bf16[2,2,32,1024]{3,2,1,0:T(8,128)(2,1)S(1)} %pad_maximum_fusion.refs_0_), channel_id=1, source_target_pairs={{0,6},{1,7},{2,4},{3,5},{4,2},{5,3},{6,0},{7,1},{8,14},{9,15},{10,... | collective-permute-start | bytes 786440 | tf_op jit(solution)/shard_map/slope_share/ppermute | solution.py:398
  103.0 10.5 %collective-permute-done.7.refs_3_ = bf16[2,2,32,1024]{3,2,1,0:T(8,128)(2,1)S(1)} collective-permute-done((bf16[2,2,32,1024]{3,2,1,0:T(8,128)(2,1)S(1)}, bf16[2,2,32,1024]{3,2,1,0:T(8,128)(2,1)S(1)}, u32[]{:S(2)}, u32[]{:S(2)}) %collective-permute-start.7) | collective-permute-done | bytes 262176 | tf_op jit(solution)/shard_map/slope_share/ppermute | solution.py:398
  113.5 3.4 %derivatives.2 = bf16[32,2,32,512]{3,2,1,0:T(8,128)(2,1)} custom-call(f32[1]{0:T(128)S(6)} %div.4.scale_ref, bf16[2,256,1024]{2,1,0:T(8,128)(2,1)S(1)} %copy-done.2, f32[2,256,512]{2,1,0:T(8,128)S(1)} %copy-done.3, bf16[1024,512]{1,0:T(8,128)(2,1)S(1)} %copy-done, bf16[2,2,32,1024]{3,2,1,0:T(8,128)(2,1)S(1)} %pad_maximum_fusion.refs_0_, ...), custom_call_target="tpu_custom_call" | custom-call | tf_op jit(solution)/shard_map/derivatives/pallas_call | solution.py:159
  117.4 7.9 %all-to-all-start = ((bf16[32,2,32,512]{3,2,1,0:T(8,128)(2,1)}), bf16[32,2,32,512]{3,2,1,0:T(8,128)(2,1)S(1)}, u32[]{:S(2)}, u32[]{:S(2)}) async-start(bf16[32,2,32,512]{3,2,1,0:T(8,128)(2,1)} %derivatives.2), calls=%async_computation | async-start | bytes 4194304 | tf_op jit(solution)/shard_map/derivative_exchange/all_to_all | solution.py:463
  125.9 5.3 %gram.2 = (bf16[32,64,512]{2,1,0:T(8,128)(2,1)}, f32[4,2048,128]{2,1,0:T(8,128)}) custom-call(bf16[64,32,512]{2,1,0:T(8,128)(2,1)} %bitcast.13.code_ref), custom_call_target="tpu_custom_call" | custom-call | tf_op jit(solution)/shard_map/gram/pallas_call | solution.py:215
  131.2 44.2 %all-to-all-done = bf16[32,2,32,512]{3,2,1,0:T(8,128)(2,1)S(1)} async-done(((bf16[32,2,32,512]{3,2,1,0:T(8,128)(2,1)}), bf16[32,2,32,512]{3,2,1,0:T(8,128)(2,1)S(1)}, u32[]{:S(2)}, u32[]{:S(2)}) %all-to-all-start) | async-done | bytes 2097184 | tf_op jit(solution)/shard_map/derivative_exchange/all_to_all | solution.py:463
  175.4 1.6 copy-done.1
  177.0 4.9 %gram.3 = (f32[128,128]{1,0:T(8,128)S(1)}, f32[4,2048,128]{2,1,0:T(8,128)}) custom-call(f32[1,128]{1,0:T(1,128)S(1)} %broadcast_select_fusion.energy_ref, bf16[64,32,512]{2,1,0:T(8,128)(2,1)S(1)} %bitcast.32, bf16[32,64,512]{2,1,0:T(8,128)(2,1)S(1)} %copy-done.1), custom_call_target="tpu_custom_call" | custom-call | tf_op jit(solution)/shard_map/gram/pallas_call | solution.py:265
  181.9 9.6 %all_to_all.36 = f32[16,8,128]{2,1,0:T(8,128)S(1)} all-to-all(f32[16,8,128]{2,1,0:T(8,128)S(1)} %bitcast.33), channel_id=1, replica_groups=mesh['z'=8,'x_lo'=2,'core'=2,'y'=4,'x_hi'=2] {'x_lo','core','y'}, dimensions={0} | all-to-all | bytes 131072 | tf_op jit(solution)/shard_map/gram_sum/all_to_all | solution.py:471
  192.2 5.4 %all-to-all-start.5 = ((f32[16,8,128]{2,1,0:T(8,128)}), f32[16,8,128]{2,1,0:T(8,128)S(1)}, u32[]{:S(2)}, u32[]{:S(2)}) async-start(f32[16,8,128]{2,1,0:T(8,128)} %broadcast_in_dim.13), calls=%async_computation.5 | async-start | bytes 131072 | tf_op jit(solution)/shard_map/gram_sum/all_to_all | solution.py:38
  198.2 8.8 %all-to-all-done.5 = f32[16,8,128]{2,1,0:T(8,128)S(1)} async-done(((f32[16,8,128]{2,1,0:T(8,128)}), f32[16,8,128]{2,1,0:T(8,128)S(1)}, u32[]{:S(2)}, u32[]{:S(2)}) %all-to-all-start.5) | async-done | bytes 65568 | tf_op jit(solution)/shard_map/gram_sum/all_to_all | solution.py:38
  207.7 5.1 %all-to-all-start.6 = ((f32[16,8,128]{2,1,0:T(8,128)}), f32[16,8,128]{2,1,0:T(8,128)S(1)}, u32[]{:S(2)}, u32[]{:S(2)}) async-start(f32[16,8,128]{2,1,0:T(8,128)} %broadcast_in_dim.14), calls=%async_computation.6 | async-start | bytes 131072 | tf_op jit(solution)/shard_map/gram_sum/all_to_all | solution.py:38
  213.4 5.3 %all-to-all-done.6.shared_ref = f32[16,8,128]{2,1,0:T(8,128)S(1)} async-done(((f32[16,8,128]{2,1,0:T(8,128)}), f32[16,8,128]{2,1,0:T(8,128)S(1)}, u32[]{:S(2)}, u32[]{:S(2)}) %all-to-all-start.6) | async-done | bytes 65568 | tf_op jit(solution)/shard_map/gram_sum/all_to_all | solution.py:38
  219.3 5.7 %solve.1 = f32[32,512]{1,0:T(8,128)} custom-call(f32[2]{0:T(128)} %pad_maximum_fusion.1.scalar_ref, f32[16,8,128]{2,1,0:T(8,128)} %copy-done.10, f32[4,2048,128]{2,1,0:T(8,128)} %get-tuple-element.33.refs_0_, f32[4,2048,128]{2,1,0:T(8,128)} %get-tuple-element.34.refs_1_), custom_call_target="tpu_custom_call" | custom-call | tf_op jit(solution)/shard_map/solve/pallas_call | solution.py:359
  (52 shorter events, 6.7 us)
Async XLA Ops:
  6.1 23.9 %copy-start.8 = (f32[2,32,1024]{2,1,0:T(8,128)S(1)}, f32[2,32,1024]{2,1,0:T(8,128)}, u32[]{:S(2)}) copy-start(f32[2,32,1024]{2,1,0:T(8,128)} %get-tuple-element.30.own_ref) | copy-start | bytes 786436
  6.1 23.9 %copy-start.9 = (bf16[1024]{0:T(1024)(128)(2,1)S(1)}, bf16[1024]{0:T(1024)(128)(2,1)}, u32[]{:S(2)}) copy-start(bf16[1024]{0:T(1024)(128)(2,1)} %readout_ref.1) | copy-start | bytes 6148
  31.2 18.6 %all-to-all-start.2 = ((bf16[8,2,32,1024]{3,2,1,0:T(8,128)(2,1)}), bf16[8,2,32,1024]{3,2,1,0:T(8,128)(2,1)S(1)}, u32[]{:S(2)}, u32[]{:S(2)}) async-start(bf16[8,2,32,1024]{3,2,1,0:T(8,128)(2,1)} %slope.1), calls=%async_computation.2 | async-start | bytes 2097152 | tf_op jit(solution)/shard_map/slope_share/all_to_all | solution.py:453
  34.7 15.0 %copy-start = (bf16[1024,512]{1,0:T(8,128)(2,1)S(1)}, bf16[1024,512]{1,0:T(8,128)(2,1)}, u32[]{:S(2)}) copy-start(bf16[1024,512]{1,0:T(8,128)(2,1)} %down_ref.7) | copy-start | bytes 3145732
  34.7 15.0 %copy-start.4 = (bf16[2,256,1024]{2,1,0:T(8,128)(2,1)S(1)}, bf16[2,256,1024]{2,1,0:T(8,128)(2,1)}, u32[]{:S(2)}) copy-start(bf16[2,256,1024]{2,1,0:T(8,128)(2,1)} %get-tuple-element.27.normed_ref) | copy-start | bytes 3145732
  49.7 1.2 copy-start.5
  51.0 0.9 copy-start.6
  55.3 12.1 %copy-start.15 = (bf16[2,2,32,1024]{3,2,1,0:T(8,128)(2,1)S(1)}, bf16[2,2,32,1024]{3,2,1,0:T(8,128)(2,1)}, u32[]{:S(2)}) copy-start(bf16[2,2,32,1024]{3,2,1,0:T(8,128)(2,1)} %get-tuple-element.24) | copy-start | bytes 786436
  55.3 12.2 %copy-start.14 = (bf16[2,2,32,1024]{3,2,1,0:T(8,128)(2,1)S(1)}, bf16[2,2,32,1024]{3,2,1,0:T(8,128)(2,1)}, u32[]{:S(2)}) copy-start(bf16[2,2,32,1024]{3,2,1,0:T(8,128)(2,1)} %get-tuple-element.25) | copy-start | bytes 786436
  55.3 13.9 %copy-start.13 = (bf16[2,2,32,1024]{3,2,1,0:T(8,128)(2,1)S(1)}, bf16[2,2,32,1024]{3,2,1,0:T(8,128)(2,1)}, u32[]{:S(2)}) copy-start(bf16[2,2,32,1024]{3,2,1,0:T(8,128)(2,1)} %get-tuple-element.26) | copy-start | bytes 786436
  55.3 27.8 %copy-start.7 = (bf16[2,2,32,1024]{3,2,1,0:T(8,128)(2,1)S(1)}, bf16[2,2,32,1024]{3,2,1,0:T(8,128)(2,1)}, u32[]{:S(2)}) copy-start(bf16[2,2,32,1024]{3,2,1,0:T(8,128)(2,1)} %get-tuple-element.23.refs_1_) | copy-start | bytes 786436
  55.3 36.5 %copy-start.11 = (f32[2,32,1024]{2,1,0:T(8,128)S(1)}, f32[2,32,1024]{2,1,0:T(8,128)}, u32[]{:S(2)}) copy-start(f32[2,32,1024]{2,1,0:T(8,128)} %get-tuple-element.22) | copy-start | bytes 786436
  55.3 62.2 %all-to-all-start.3 = ((bf16[32,2,32,512]{3,2,1,0:T(8,128)(2,1)}), bf16[32,2,32,512]{3,2,1,0:T(8,128)(2,1)}, u32[]{:S(2)}, u32[]{:S(2)}) async-start(bf16[32,2,32,512]{3,2,1,0:T(8,128)(2,1)} %derivatives.3), calls=%async_computation.3 | async-start | bytes 4194304 | tf_op jit(solution)/shard_map/derivative_exchange/all_to_all | solution.py:463
  67.3 46.2 %copy-start.2 = (bf16[2,256,1024]{2,1,0:T(8,128)(2,1)S(1)}, bf16[2,256,1024]{2,1,0:T(8,128)(2,1)}, u32[]{:S(2)}) copy-start(bf16[2,256,1024]{2,1,0:T(8,128)(2,1)} %get-tuple-element.20.normed_ref) | copy-start | bytes 3145732
  67.3 46.2 %copy-start.3 = (f32[2,256,512]{2,1,0:T(8,128)S(1)}, f32[2,256,512]{2,1,0:T(8,128)}, u32[]{:S(2)}) copy-start(f32[2,256,512]{2,1,0:T(8,128)} %get-tuple-element.21.bend_ref) | copy-start | bytes 3145732
  67.3 7.8 %collective-permute-start = (bf16[2,2,32,1024]{3,2,1,0:T(8,128)(2,1)S(1)}, bf16[2,2,32,1024]{3,2,1,0:T(8,128)(2,1)S(1)}, u32[]{:S(2)}, u32[]{:S(2)}) collective-permute-start(bf16[2,2,32,1024]{3,2,1,0:T(8,128)(2,1)S(1)} %copy-done.15), channel_id=1, source_target_pairs={{0,2},{1,3},{2,0},{3,1},{4,6},{5,7},{6,4},{7,5},{8,10},{9,11},{10,... | collective-permute-start | bytes 786440 | tf_op jit(solution)/shard_map/mixed_exchange/ppermute | solution.py:398
  67.5 13.5 %collective-permute-start.1 = (bf16[2,2,32,1024]{3,2,1,0:T(8,128)(2,1)S(1)}, bf16[2,2,32,1024]{3,2,1,0:T(8,128)(2,1)S(1)}, u32[]{:S(2)}, u32[]{:S(2)}) collective-permute-start(bf16[2,2,32,1024]{3,2,1,0:T(8,128)(2,1)S(1)} %copy-done.14), channel_id=1, source_target_pairs={{0,4},{1,5},{2,6},{3,7},{4,0},{5,1},{6,2},{7,3},{8,12},{9,13},{10,... | collective-permute-start | bytes 786440 | tf_op jit(solution)/shard_map/mixed_exchange/ppermute | solution.py:398
  69.2 13.9 %collective-permute-start.2 = (bf16[2,2,32,1024]{3,2,1,0:T(8,128)(2,1)S(1)}, bf16[2,2,32,1024]{3,2,1,0:T(8,128)(2,1)S(1)}, u32[]{:S(2)}, u32[]{:S(2)}) collective-permute-start(bf16[2,2,32,1024]{3,2,1,0:T(8,128)(2,1)S(1)} %copy-done.13), channel_id=1, source_target_pairs={{0,6},{1,7},{2,4},{3,5},{4,2},{5,3},{6,0},{7,1},{8,14},{9,15},{10,... | collective-permute-start | bytes 786440 | tf_op jit(solution)/shard_map/mixed_exchange/ppermute | solution.py:398
  83.1 8.6 %collective-permute-start.3 = (bf16[2,32,1024]{2,1,0:T(8,128)(2,1)S(1)}, bf16[2,32,1024]{2,1,0:T(8,128)(2,1)S(1)}, u32[]{:S(2)}, u32[]{:S(2)}) collective-permute-start(bf16[2,32,1024]{2,1,0:T(8,128)(2,1)S(1)} %fusion.4), channel_id=1, source_target_pairs={{0,1},{1,0},{2,3},{3,2},{4,5},{5,4},{6,7},{7,6},{8,9},{9,8},{10,11... | collective-permute-start | bytes 393224 | tf_op jit(solution)/shard_map/mixed_exchange/ppermute | solution.py:398
  91.9 6.9 %collective-permute-start.4 = (bf16[2,32,1024]{2,1,0:T(8,128)(2,1)S(1)}, bf16[2,32,1024]{2,1,0:T(8,128)(2,1)S(1)}, u32[]{:S(2)}, u32[]{:S(2)}) collective-permute-start(bf16[2,32,1024]{2,1,0:T(8,128)(2,1)S(1)} %fusion.3), channel_id=1, source_target_pairs={{0,1},{1,0},{2,3},{3,2},{4,5},{5,4},{6,7},{7,6},{8,9},{9,8},{10,11... | collective-permute-start | bytes 393224 | tf_op jit(solution)/shard_map/slope_share/ppermute | solution.py:398
  98.8 14.7 %collective-permute-start.7 = (bf16[2,2,32,1024]{3,2,1,0:T(8,128)(2,1)S(1)}, bf16[2,2,32,1024]{3,2,1,0:T(8,128)(2,1)S(1)}, u32[]{:S(2)}, u32[]{:S(2)}) collective-permute-start(bf16[2,2,32,1024]{3,2,1,0:T(8,128)(2,1)S(1)} %pad_maximum_fusion.refs_0_), channel_id=1, source_target_pairs={{0,6},{1,7},{2,4},{3,5},{4,2},{5,3},{6,0},{7,1},{8,14},{9,15},{10,... | collective-permute-start | bytes 786440 | tf_op jit(solution)/shard_map/slope_share/ppermute | solution.py:398
  102.3 11.2 %collective-permute-start.6 = (bf16[2,2,32,1024]{3,2,1,0:T(8,128)(2,1)S(1)}, bf16[2,2,32,1024]{3,2,1,0:T(8,128)(2,1)S(1)}, u32[]{:S(2)}, u32[]{:S(2)}) collective-permute-start(bf16[2,2,32,1024]{3,2,1,0:T(8,128)(2,1)S(1)} %pad_maximum_fusion.refs_0_), channel_id=1, source_target_pairs={{0,4},{1,5},{2,6},{3,7},{4,0},{5,1},{6,2},{7,3},{8,12},{9,13},{10,... | collective-permute-start | bytes 786440 | tf_op jit(solution)/shard_map/slope_share/ppermute | solution.py:398
  102.3 11.2 %collective-permute-start.5 = (bf16[2,2,32,1024]{3,2,1,0:T(8,128)(2,1)S(1)}, bf16[2,2,32,1024]{3,2,1,0:T(8,128)(2,1)S(1)}, u32[]{:S(2)}, u32[]{:S(2)}) collective-permute-start(bf16[2,2,32,1024]{3,2,1,0:T(8,128)(2,1)S(1)} %pad_maximum_fusion.refs_0_), channel_id=1, source_target_pairs={{0,2},{1,3},{2,0},{3,1},{4,6},{5,7},{6,4},{7,5},{8,10},{9,11},{10,... | collective-permute-start | bytes 786440 | tf_op jit(solution)/shard_map/slope_share/ppermute | solution.py:398
  116.9 8.5 %copy-start.12 = (f32[4]{0:T(128)S(1)}, f32[4]{0:T(128)}, u32[]{:S(2)}) copy-start(f32[4]{0:T(128)} %param.16) | copy-start | bytes 52
  117.4 57.9 %all-to-all-start = ((bf16[32,2,32,512]{3,2,1,0:T(8,128)(2,1)}), bf16[32,2,32,512]{3,2,1,0:T(8,128)(2,1)S(1)}, u32[]{:S(2)}, u32[]{:S(2)}) async-start(bf16[32,2,32,512]{3,2,1,0:T(8,128)(2,1)} %derivatives.2), calls=%async_computation | async-start | bytes 4194304 | tf_op jit(solution)/shard_map/derivative_exchange/all_to_all | solution.py:463
  175.4 1.6 copy-start.1
  192.2 14.9 %all-to-all-start.5 = ((f32[16,8,128]{2,1,0:T(8,128)}), f32[16,8,128]{2,1,0:T(8,128)S(1)}, u32[]{:S(2)}, u32[]{:S(2)}) async-start(f32[16,8,128]{2,1,0:T(8,128)} %broadcast_in_dim.13), calls=%async_computation.5 | async-start | bytes 131072 | tf_op jit(solution)/shard_map/gram_sum/all_to_all | solution.py:38
  207.7 11.0 %all-to-all-start.6 = ((f32[16,8,128]{2,1,0:T(8,128)}), f32[16,8,128]{2,1,0:T(8,128)S(1)}, u32[]{:S(2)}, u32[]{:S(2)}) async-start(f32[16,8,128]{2,1,0:T(8,128)} %broadcast_in_dim.14), calls=%async_computation.6 | async-start | bytes 131072 | tf_op jit(solution)/shard_map/gram_sum/all_to_all | solution.py:38
  218.7 0.6 copy-start.10

commit v5 on v4

--- a/solution.py
+++ b/solution.py
@@ -13,8 +13,8 @@
 VMEM_SMALL = 32 * 1024 * 1024
 SAMPLES = ("z", "x_lo", "core")
 MP = ("y", "x_hi")
-NEAR = ("x_lo", "core", "y")
-FAR = ("z", "x_hi")
+NEAR = ("z", "core")
+FAR = ("x_lo", "y", "x_hi")
 
 
 gelu_coef = 0.7978845608028654
@@ -42,12 +42,13 @@
 SMEM = pl.BlockSpec(memory_space=pltpu.SMEM)
 
 
-def forward_kernel(scalar_ref, spin_ref, feature_ref, embed_ref, gain_ref, up_ref, down_ref, *refs):
-    normed_ref, own_ref, bend_ref, *part_refs = refs
+def forward_kernel(first, pairs, *refs):
+    if pairs:
+        order_ref, *refs = refs
+        order = order_ref[0]
+    spin_ref, feature_ref, embed_ref, gain_ref, up_ref, down_ref, normed_ref, bend_ref, *refs = refs
     blocks, rows, width = feature_ref.shape[1:]
-    order = scalar_ref[0]
-    own_block = jnp.bitwise_xor(order, scalar_ref[1])
-    spin_row = spin_ref[pl.ds(scalar_ref[2] + pl.program_id(0), 1)].astype(jnp.float32)
+    spin_row = spin_ref[pl.ds(first + pl.program_id(0), 1)].astype(jnp.float32)
     offset = lax.broadcasted_iota(jnp.int32, (rows, blocks * rows), 1) - lax.broadcasted_iota(
         jnp.int32, (rows, blocks * rows), 0
     )
@@ -58,9 +59,13 @@
         spin_col = jnp.sum(jnp.where(offset == block * rows, spin_row, 0.0), axis=1, keepdims=True)
         return feature_ref[0, block].astype(jnp.float32) + spin_col * embed
 
-    own_ref[0] = block_inputs(scalar_ref[1])
+    part_refs = refs
+    if pairs:
+        own_ref, mark_ref, *part_refs = refs
+        own_ref[0] = block_inputs(order)
+        mark_ref[...] = jnp.zeros_like(mark_ref)
     for k in range(blocks):
-        inputs = block_inputs(jnp.bitwise_xor(order, k))
+        inputs = block_inputs(jnp.bitwise_xor(order, k) if pairs else k)
         inv_scale = lax.rsqrt(jnp.mean(inputs * inputs, axis=1, keepdims=True) + 1e-05)
         normed_ref[0, k * rows : (k + 1) * rows] = (inputs * inv_scale * gain).astype(jnp.bfloat16)
     hidden_pre = jnp.dot(normed_ref[0], up_ref[...], preferred_element_type=jnp.float32)
@@ -79,26 +84,31 @@
         part_refs[k // per_ref][k % per_ref, 0] = part
 
 
-def forward(order, own, spins, features, embed, gain, up, down, first, samples, pairs):
+def forward(order, spins, features, embed, gain, up, down, first, samples, pairs):
     _, blocks, rows, width = features.shape
     hidden = up.shape[1]
     tokens = blocks * rows
     whole = lambda array: pl.BlockSpec(array.shape, lambda s: (0,) * array.ndim)
     block = lambda *shape: pl.BlockSpec((1,) + shape, lambda s: (s,) + (0,) * len(shape))
     result = lambda dtype, *shape: jax.ShapeDtypeStruct((samples,) + shape, dtype)
-    together = 2 if pairs else blocks
+    together = 1 if pairs else blocks
     part_specs = [pl.BlockSpec((together, 1, rows, width), lambda s: (0, s, 0, 0))] * (
         blocks // together
     )
     part_shapes = [jax.ShapeDtypeStruct((together, samples, rows, width), jnp.bfloat16)] * (
         blocks // together
     )
-    scalars = jnp.stack([order, own, jnp.int32(first)])
+    if pairs:
+        part_specs = [block(rows, width), pl.BlockSpec((8, 128), lambda s: (0, 0))] + part_specs
+        part_shapes = [
+            result(jnp.float32, rows, width),
+            jax.ShapeDtypeStruct((8, 128), jnp.float32),
+        ] + part_shapes
     return pl.pallas_call(
-        forward_kernel,
+        functools.partial(forward_kernel, first, pairs),
         grid=(samples,),
-        in_specs=[
-            SMEM,
+        in_specs=[SMEM] * pairs
+        + [
             whole(spins),
             pl.BlockSpec((1, blocks, rows, width), lambda s: (s + first, 0, 0, 0)),
             whole(embed),
@@ -106,22 +116,28 @@
             whole(up),
             whole(down),
         ],
-        out_specs=[block(tokens, width), block(rows, width), block(tokens, hidden)] + part_specs,
+        out_specs=[block(tokens, width), block(tokens, hidden)] + part_specs,
         out_shape=[
             result(jnp.bfloat16, tokens, width),
-            result(jnp.float32, rows, width),
             result(jnp.float32, tokens, hidden),
         ]
         + part_shapes,
         compiler_params=pltpu.CompilerParams(vmem_limit_bytes=VMEM_LIMIT),
-    )(scalars, spins, features, embed, gain, up, down)
-
-
-def slope_kernel(part_ref, own_ref, readout_ref, slope_ref):
+    )(*[order] * pairs, spins, features, embed, gain, up, down)
+
+
+def slope_kernel(own_ref, part_ref, spin_ref, feature_ref, embed_ref, readout_ref, slope_ref):
     blocks, samples, rows, width = part_ref.shape
+    own = own_ref[0]
+    offset = lax.broadcasted_iota(jnp.int32, (rows, blocks * rows), 1) - lax.broadcasted_iota(
+        jnp.int32, (rows, blocks * rows), 0
+    )
+    embed = embed_ref[...].astype(jnp.float32).reshape(1, width)
     readout = readout_ref[...].astype(jnp.float32).reshape(1, width)
     for s in range(samples):
-        outputs = own_ref[s]
+        spin_row = spin_ref[s : s + 1].astype(jnp.float32)
+        spin_col = jnp.sum(jnp.where(offset == own * rows, spin_row, 0.0), axis=1, keepdims=True)
+        outputs = feature_ref[s, own].astype(jnp.float32) + spin_col * embed
         for k in range(blocks):
             outputs = outputs + part_ref[k, s].astype(jnp.float32)
         slope = (readout * jnp.tanh(outputs)).astype(jnp.bfloat16)
@@ -129,14 +145,23 @@
             slope_ref[k, s] = slope
 
 
-def own_slope(parts, own, readout):
+def own_slope(own, parts, spins, features, embed, readout):
+    whole = lambda array: pl.BlockSpec(array.shape, lambda s: (0,) * array.ndim)
     return pl.pallas_call(
         slope_kernel,
-        out_shape=jax.ShapeDtypeStruct(parts.shape, parts.dtype),
-        in_specs=[VMEM] * 3,
-        out_specs=VMEM,
+        grid=(1,),
+        out_shape=pltpu.HBM(parts.shape, parts.dtype),
+        in_specs=[
+            SMEM,
+            whole(parts),
+            whole(spins),
+            pl.BlockSpec((parts.shape[1],) + features.shape[1:], lambda s: (0, 0, 0, 0)),
+            whole(embed),
+            whole(readout),
+        ],
+        out_specs=whole(parts),
         compiler_params=pltpu.CompilerParams(vmem_limit_bytes=VMEM_SMALL),
-    )(parts, own, readout)
+    )(own, parts, spins, features, embed, readout)
 
 
 def derivative_kernel(slope_count, scale_ref, normed_ref, bend_ref, down_ref, *refs):
@@ -169,36 +194,42 @@
             pl.BlockSpec((a.shape[0], 1) + a.shape[2:], lambda s: (0, s, 0, 0))
             for a in slopes
         ]
-        + [pl.BlockSpec((1, 1, 16, 128), lambda s: (0, 0, 0, 0))] * len(after),
+        + [pl.BlockSpec(memory_space=pl.ANY)] * len(after),
         out_specs=pl.BlockSpec((parts, 1, width // parts, hidden), lambda s: (0, s, 0, 0)),
-        out_shape=jax.ShapeDtypeStruct((parts, samples, width // parts, hidden), jnp.bfloat16),
+        out_shape=pltpu.HBM((parts, samples, width // parts, hidden), jnp.bfloat16),
         compiler_params=pltpu.CompilerParams(vmem_limit_bytes=VMEM_SMALL),
     )(scale, normed, bend, down, *slopes, *after)
 
 
 LANES = 128
+
+
+STEP = 16
 
 
 def widen(code_ref, wide_ref, apart_ref):
     count, rows, _ = code_ref.shape
     for n in range(count):
         values = decode(code_ref[n])
-        wide_ref[0, n * rows : (n + 1) * rows] = values
-        apart_ref[n * (rows + 1) : n * (rows + 1) + rows] = values
+        for f in range(wide_ref.shape[1]):
+            group = values[:, f * LANES : (f + 1) * LANES]
+            wide_ref[0, f, n * rows : (n + 1) * rows] = group
+            apart_ref[f, n * (rows + 1) : n * (rows + 1) + rows] = group
 
 
 def row_of_all(apart_ref, row, count, rows):
-    return apart_ref[pl.ds(row, count, stride=rows + 1)].astype(jnp.bfloat16)
-
-
-def apart_scratch(count, rows):
-    return pltpu.VMEM((-(-count * (rows + 1) // 8) * 8, LANES), jnp.float32)
+    groups = [apart_ref[f, pl.ds(row, count, stride=rows + 1)] for f in range(apart_ref.shape[0])]
+    return jnp.concatenate(groups, axis=1).astype(jnp.bfloat16)
+
+
+def apart_scratch(count, width):
+    return pltpu.VMEM((width // LANES, -(-count * (STEP + 1) // 8) * 8, LANES), jnp.float32)
 
 
 def wide_out(count, rows, width):
     return (
-        pl.BlockSpec((1, count * rows, LANES), lambda f: (f, 0, 0)),
-        pltpu.HBM((width // LANES, count * rows, LANES), jnp.float32),
+        pl.BlockSpec((1, width // LANES, count * STEP, LANES), lambda r: (r, 0, 0, 0)),
+        pltpu.HBM((rows // STEP, width // LANES, count * STEP, LANES), jnp.float32),
     )
 
 
@@ -214,12 +245,12 @@
     wide_spec, wide_shape = wide_out(count, rows, width)
     return pl.pallas_call(
         rows_first_kernel,
-        grid=(width // LANES,),
-        in_specs=[pl.BlockSpec((count, rows, LANES), lambda f: (0, 0, f))],
-        out_specs=[pl.BlockSpec((rows, count, LANES), lambda f: (0, 0, f)), wide_spec],
+        grid=(rows // STEP,),
+        in_specs=[pl.BlockSpec((count, STEP, width), lambda r: (0, r, 0))],
+        out_specs=[pl.BlockSpec((STEP, count, width), lambda r: (r, 0, 0)), wide_spec],
         out_shape=[jax.ShapeDtypeStruct((rows, count, width), jnp.bfloat16), wide_shape],
-        scratch_shapes=[apart_scratch(count, rows)],
-        compiler_params=pltpu.CompilerParams(vmem_limit_bytes=VMEM_LIMIT),
+        scratch_shapes=[apart_scratch(count, width)],
+        compiler_params=pltpu.CompilerParams(vmem_limit_bytes=VMEM_SMALL),
     )(code)
 
 
@@ -228,13 +259,9 @@
     count, rows, _ = code_ref.shape
     widen(code_ref, wide_ref, apart_ref)
     gram = jnp.zeros(gram_ref.shape, jnp.float32)
-    for r in range(0, rows, 4):
+    for r in range(rows):
         half = jnp.concatenate(
-            [
-                jnp.concatenate([h[q] for h in half_refs] + [row_of_all(apart_ref, q, count, rows)], axis=0)
-                for q in range(r, r + 4)
-            ],
-            axis=1,
+            [h[r] for h in half_refs] + [row_of_all(apart_ref, r, count, rows)], axis=0
         )
         gram += lax.dot_general(half, half, (((1,), (1,)), ((), ())), preferred_element_type=jnp.float32)
 
@@ -264,16 +291,16 @@
     wide_spec, wide_shape = wide_out(count, rows, width)
     return pl.pallas_call(
         gram_kernel,
-        grid=(width // LANES,),
+        grid=(rows // STEP,),
         in_specs=[
             pl.BlockSpec(energy.shape, lambda f: (0, 0)),
-            pl.BlockSpec((count, rows, LANES), lambda f: (0, 0, f)),
+            pl.BlockSpec((count, STEP, width), lambda r: (0, r, 0)),
         ]
-        + [pl.BlockSpec(h.shape[:2] + (LANES,), lambda f: (0, 0, f)) for h in halves],
+        + [pl.BlockSpec((STEP,) + h.shape[1:], lambda r: (r, 0, 0)) for h in halves],
         out_specs=[pl.BlockSpec((size, size), lambda f: (0, 0)), wide_spec],
         out_shape=[jax.ShapeDtypeStruct((size, size), jnp.float32), wide_shape],
-        scratch_shapes=[apart_scratch(count, rows)],
-        compiler_params=pltpu.CompilerParams(vmem_limit_bytes=VMEM_SMALL),
+        scratch_shapes=[apart_scratch(count, width)],
+        compiler_params=pltpu.CompilerParams(vmem_limit_bytes=VMEM_LIMIT),
     )(energy, code, *halves)
 
 
@@ -332,33 +359,34 @@
             direction = tuple(r + ratio * d for r, d in zip(residual, direction))
             norm_now = norm_next
     spread_ref[...] = jnp.broadcast_to(coef * unit, spread_ref.shape)
-    for copy in copies:
-        copy.wait()
-    rows, width = out_ref.shape
     lanes = spread_ref.shape[1]
-    groups = 2
-    for f in range(0, width // lanes, groups):
-        total = (jnp.zeros((rows, lanes), jnp.float32),) * groups
-        first = 0
-        for chunk_ref in chunk_refs:
-            samples = chunk_ref.shape[1] // rows
+    first = 0
+    for n, chunk_ref in enumerate(chunk_refs):
+        copies[n].wait()
+        steps, groups, depth, _ = chunk_ref.shape
+        for r in range(steps):
+            here = slice(r * STEP, (r + 1) * STEP)
 
             def add(s, total):
-                start = pl.multiple_of(s * rows, rows)
+                start = pl.multiple_of(s * STEP, STEP)
                 spread = spread_ref[pl.ds(first + s, 1)]
-                return tuple(t + spread * chunk_ref[f + g, pl.ds(start, rows)] for g, t in enumerate(total))
-
-            total = lax.fori_loop(0, samples, add, total, unroll=8)
-            first += samples
-        for g in range(groups):
-            out_ref[:, (f + g) * lanes : (f + g + 1) * lanes] = total[g]
+                return tuple(t + spread * chunk_ref[r, f, pl.ds(start, STEP)] for f, t in enumerate(total))
+
+            total = tuple(
+                out_ref[here, f * lanes : (f + 1) * lanes] if n else jnp.zeros((STEP, lanes), jnp.float32)
+                for f in range(groups)
+            )
+            total = lax.fori_loop(0, depth // STEP, add, total, unroll=8)
+            for f, t in enumerate(total):
+                out_ref[here, f * lanes : (f + 1) * lanes] = t
+        first += depth // STEP
 
 
 def solve(scalars, shared, chunks, rows):
     count = shared.shape[2]
     return pl.pallas_call(
         solve_kernel,
-        out_shape=jax.ShapeDtypeStruct((rows, chunks[0].shape[0] * chunks[0].shape[2]), jnp.float32),
+        out_shape=jax.ShapeDtypeStruct((rows, chunks[0].shape[1] * chunks[0].shape[3]), jnp.float32),
         in_specs=[SMEM, VMEM] + [pl.BlockSpec(memory_space=pltpu.HBM)] * len(chunks),
         out_specs=VMEM,
         scratch_shapes=[
@@ -415,8 +443,7 @@
         with jax.named_scope("forward"):
             states.append(
                 forward(
-                    place if n else jnp.int32(0),
-                    place,
+                    place.reshape(1),
                     spin_values,
                     feature_blocks,
                     spin_embed,
@@ -430,21 +457,25 @@
             )
         first += samples
     coded_chunks = []
-    for n, (normed, own_inputs, bend, *parts) in enumerate(states):
+    for n, (normed, bend, *parts) in enumerate(states):
+        if n > 0:
+            own_inputs, _, *parts = parts
         with jax.named_scope("mixed_exchange"):
             if n == 0:
                 mixed_parts = lax.all_to_all(parts[0], MP, 0, 0)
             else:
-                pairs = parts[:1] + [partner(pair, 2 * j) for j, pair in enumerate(parts) if j]
-                mixed_own = own_inputs
-                mixed_other = 0.0
-                for pair in pairs:
-                    mixed_own = mixed_own + pair[0].astype(jnp.float32)
-                    mixed_other = mixed_other + pair[1].astype(jnp.float32)
+                mixed_other = parts[1].astype(jnp.float32)
+                for k in range(3, mp_size, 2):
+                    mixed_other = mixed_other + partner(parts[k], k - 1).astype(jnp.float32)
                 mixed_other = partner(mixed_other.astype(jnp.bfloat16), 1)
+                mixed_own = own_inputs + parts[0].astype(jnp.float32)
+                for k in range(2, mp_size, 2):
+                    mixed_own = mixed_own + partner(parts[k], k).astype(jnp.float32)
         with jax.named_scope("slope"):
             if n == 0:
-                slope = own_slope(mixed_parts, own_inputs, readout)
+                slope = own_slope(
+                    place.reshape(1), mixed_parts, spin_values, feature_blocks, spin_embed, readout
+                )
             else:
                 outputs = mixed_own + mixed_other.astype(jnp.float32)
                 slope = (readout_wide * jnp.tanh(outputs)).astype(jnp.bfloat16)
@@ -452,8 +483,10 @@
             if n == 0:
                 slopes = [lax.all_to_all(slope, MP, 0, 0)]
             else:
-                pair = jnp.stack([slope, partner(slope, 1)])
-                slopes = [pair] + [partner(pair, 2 * j) for j in range(1, mp_size // 2)]
+                other = partner(slope, 1)
+                slopes = [slope, other]
+                for k in range(2, mp_size, 2):
+                    slopes += [partner(slope, k), partner(other, k)]
         with jax.named_scope("derivatives"):
             after = [state[3] for state in states[n + 1 : n + 2]]
             coded_chunks.append(

time: 226 us -> 219 us (0.969)
  blocking collectives: 33.5 us -> 21.6 us
  starting transfers between devices: 45.2 us -> 49.3 us
  Pallas kernels: 34.9 us -> 32.6 us
    ppermute x8 -> x14, waiting for transfers between devices: 34.7 us -> 18 us  [partner(): return lax.ppermute(array, MP, [(i, i ^ k) for i in range(mp_size)])]
    all_to_all x0 -> x1, waiting for transfers between devices: none -> 16 us  [body(): mixed_parts = lax.all_to_all(parts[0], MP, 0, 0)]
    all_to_all x1, blocking collectives: 23.9 us -> 9.66 us  [share(): lax.all_to_all(jnp.broadcast_to(array, (size,) + array.shape), axis, 0, 0)]
    all_to_all x2, waiting for transfers between devices: 44.7 us -> 54.8 us  [body(): chunks = [lax.all_to_all(c, SAMPLES, 0, 0) for c in coded_chunks]]
    all_to_all x0 -> x1, starting transfers between devices: none -> 7.63 us  [body(): mixed_parts = lax.all_to_all(parts[0], MP, 0, 0)]
    all_to_all x2 -> x1, waiting for transfers between devices: 14 us -> 6.52 us  [share(): lax.all_to_all(jnp.broadcast_to(array, (size,) + array.shape), axis, 0, 0)]
    all_to_all x2 -> x1, starting transfers between devices: 10.6 us -> 4.88 us  [share(): lax.all_to_all(jnp.broadcast_to(array, (size,) + array.shape), axis, 0, 0)]
    ppermute x8 -> x14, starting transfers between devices: 11.1 us -> 16.2 us  [partner(): return lax.ppermute(array, MP, [(i, i ^ k) for i in range(mp_size)])]
  transfers between devices with their start and end apart: 13 -> 19, of which waited for: 11 -> 15; matrix products, arithmetic and copies ran while one was open for 1% -> 2% of each run, Pallas kernels for 6% -> 5%
where the time goes in v5:
time: 219 us; the launch traced here: 218 us
  waiting for transfers between devices  104 us (47%)
  starting transfers between devices  49.3 us (23%)
  Pallas kernels  32.6 us (15%)
  blocking collectives  21.6 us (10%)
  local copies, waits for them, and re-layouts  6.3 us (3%)
  other arithmetic  3.07 us (1%)
    all_to_all x2, waiting for transfers between devices, body(): chunks = [lax.all_to_all(c, SAMPLES, 0, 0) for c in coded_chunks]  54.8 us
    ppermute x14, waiting for transfers between devices, partner(): return lax.ppermute(array, MP, [(i, i ^ k) for i in range(mp_size)])  18 us
    all_to_all x2, starting transfers between devices, body(): chunks = [lax.all_to_all(c, SAMPLES, 0, 0) for c in coded_chunks]  16.4 us
    ppermute x14, starting transfers between devices, partner(): return lax.ppermute(array, MP, [(i, i ^ k) for i in range(mp_size)])  16.2 us
    all_to_all x1, waiting for transfers between devices, body(): mixed_parts = lax.all_to_all(parts[0], MP, 0, 0)  16 us
    all_to_all x1, blocking collectives, body(): lax.all_to_all(gram_part.reshape(near_size, sample_count // near_size, sa...  11.9 us
    pallas_call x2, Pallas kernels, forward(): pl.pallas_call(functools.partial(forward_kernel, first, pairs), grid=(sam...  10.6 us
    all_to_all x1, blocking collectives, share(): lax.all_to_all(jnp.broadcast_to(array, (size,) + array.shape), axis, 0, 0)  9.66 us
  transfers between devices with their start and end apart: 19, of which 15 were waited for; matrix products, arithmetic and copies ran while one was open for 2% of the time, Pallas kernels for 5%

profile of v5, /device:TPU:1, one launch (start us, length us, event | category | flops | bytes accessed | tf_op | source)
XLA Modules:
  0.0 218.5 jit_solution(4240391153384827775)
XLA Ops:
  0.0 5.2 %forward.3 = (bf16[2,256,1024]{2,1,0:T(8,128)(2,1)}, f32[2,256,512]{2,1,0:T(8,128)}, bf16[8,2,32,1024]{3,2,1,0:T(8,128)(2,1)}) custom-call(s32[4,256]{1,0:T(4,128)} %spin_ref.1, bf16[4,8,32,1024]{3,2,1,0:T(8,128)(2,1)} %bitcast.26, bf16[1024]{0:T(1024)(128)(2,1)} %embed_ref.1, bf16[1024]{0:T(1024)(128)(2,1)} %refs_3_.3, bf16[1024,512]{1,0:T(8,128)(2,1)} %refs_4_.3, ...), custom_call_target="tpu_custom_call" | custom-call | tf_op jit(solution)/shard_map/forward/pallas_call | solution.py:107
  5.2 7.6 %all-to-all-start.1 = ((bf16[8,2,32,1024]{3,2,1,0:T(8,128)(2,1)}), bf16[8,2,32,1024]{3,2,1,0:T(8,128)(2,1)S(1)}, u32[]{:S(2)}, u32[]{:S(2)}) async-start(bf16[8,2,32,1024]{3,2,1,0:T(8,128)(2,1)} %get-tuple-element.37), calls=%async_computation.1 | async-start | bytes 2097152 | tf_op jit(solution)/shard_map/mixed_exchange/all_to_all | solution.py:465
  12.9 16.0 %all-to-all-done.1.part_ref = bf16[8,2,32,1024]{3,2,1,0:T(8,128)(2,1)S(1)} async-done(((bf16[8,2,32,1024]{3,2,1,0:T(8,128)(2,1)}), bf16[8,2,32,1024]{3,2,1,0:T(8,128)(2,1)S(1)}, u32[]{:S(2)}, u32[]{:S(2)}) %all-to-all-start.1) | async-done | bytes 1048608 | tf_op jit(solution)/shard_map/mixed_exchange/all_to_all | solution.py:465
  30.2 4.1 %all-to-all-start.2 = ((bf16[8,2,32,1024]{3,2,1,0:T(8,128)(2,1)}), bf16[8,2,32,1024]{3,2,1,0:T(8,128)(2,1)S(1)}, u32[]{:S(2)}, u32[]{:S(2)}) async-start(bf16[8,2,32,1024]{3,2,1,0:T(8,128)(2,1)} %slope.1), calls=%async_computation.2 | async-start | bytes 2097152 | tf_op jit(solution)/shard_map/slope_share/all_to_all | solution.py:484
  34.4 5.4 %forward.2 = (bf16[2,256,1024]{2,1,0:T(8,128)(2,1)}, f32[2,256,512]{2,1,0:T(8,128)}, f32[2,32,1024]{2,1,0:T(8,128)}, f32[8,128]{1,0:T(8,128)}, bf16[1,2,32,1024]...) custom-call(s32[1]{0:T(128)} %bitcast.3.refs_0_.own_ref, ...), custom_call_target="tpu_custom_call" | custom-call | tf_op jit(solution)/shard_map/forward/pallas_call | solution.py:107
  41.1 8.6 %all-to-all-done.2.refs_0_ = bf16[8,2,32,1024]{3,2,1,0:T(8,128)(2,1)S(1)} async-done(((bf16[8,2,32,1024]{3,2,1,0:T(8,128)(2,1)}), bf16[8,2,32,1024]{3,2,1,0:T(8,128)(2,1)S(1)}, u32[]{:S(2)}, u32[]{:S(2)}) %all-to-all-start.2) | async-done | bytes 1048608 | tf_op jit(solution)/shard_map/slope_share/all_to_all | solution.py:484
  51.7 3.3 %derivatives.3 = bf16[32,2,32,512]{3,2,1,0:T(8,128)(2,1)} custom-call(f32[1]{0:T(128)S(6)} %div.4.scale_ref, bf16[2,256,1024]{2,1,0:T(8,128)(2,1)S(1)} %copy-done.5, f32[2,256,512]{2,1,0:T(8,128)S(1)} %copy-done.6, bf16[1024,512]{1,0:T(8,128)(2,1)S(1)} %copy-done.1, bf16[8,2,32,1024]{3,2,1,0:T(8,128)(2,1)S(1)} %all-to-all-done.2.refs_0_, f32[8,128]{1,0:T(8,128)S(1)} %copy-done.10), custom_call_target="tpu_custom_call" | custom-call | tf_op jit(solution)/shard_map/derivatives/pallas_call | solution.py:184
  55.0 11.5 %all-to-all-start.3 = ((bf16[32,2,32,512]{3,2,1,0:T(8,128)(2,1)}), bf16[32,2,32,512]{3,2,1,0:T(8,128)(2,1)S(1)}, u32[]{:S(2)}, u32[]{:S(2)}) async-start(bf16[32,2,32,512]{3,2,1,0:T(8,128)(2,1)} %derivatives.3), calls=%async_computation.3 | async-start | bytes 4194304 | tf_op jit(solution)/shard_map/derivative_exchange/all_to_all | solution.py:496
  66.7 1.7 collective-permute-start.4
  68.4 2.1 collective-permute-start.5
  70.5 1.8 collective-permute-start.1
  72.3 2.1 collective-permute-start.2
  74.9 2.5 %collective-permute-done.5 = bf16[1,2,32,1024]{3,2,1,0:T(8,128)(2,1)S(1)} collective-permute-done((bf16[1,2,32,1024]{3,2,1,0:T(8,128)(2,1)}, bf16[1,2,32,1024]{3,2,1,0:T(8,128)(2,1)S(1)}, u32[]{:S(2)}, u32[]{:S(2)}) %collective-permute-start.5) | collective-permute-done | bytes 131104 | tf_op jit(solution)/shard_map/mixed_exchange/ppermute | solution.py:426
  77.5 1.6 collective-permute-start.6
  79.1 1.5 collective-permute-done.1
  80.6 2.5 %collective-permute-done.2 = bf16[1,2,32,1024]{3,2,1,0:T(8,128)(2,1)S(1)} collective-permute-done((bf16[1,2,32,1024]{3,2,1,0:T(8,128)(2,1)}, bf16[1,2,32,1024]{3,2,1,0:T(8,128)(2,1)S(1)}, u32[]{:S(2)}, u32[]{:S(2)}) %collective-permute-start.2) | collective-permute-done | bytes 131104 | tf_op jit(solution)/shard_map/mixed_exchange/ppermute | solution.py:426
  83.0 2.0 collective-permute-done.6
  86.1 2.0 collective-permute-start.7
  88.2 3.1 %collective-permute-start.8 = (bf16[1,2,32,1024]{3,2,1,0:T(8,128)(2,1)S(1)}, bf16[1,2,32,1024]{3,2,1,0:T(8,128)(2,1)S(1)}, u32[]{:S(2)}, u32[]{:S(2)}) collective-permute-start(bf16[1,2,32,1024]{3,2,1,0:T(8,128)(2,1)S(1)} %fusion.6.refs_0_), channel_id=1, source_target_pairs={{0,2},{1,3},{2,0},{3,1},{4,6},{5,7},{6,4},{7,5},{8,10},{9,11},{10,... | collective-permute-start | bytes 393224 | tf_op jit(solution)/shard_map/slope_share/ppermute | solution.py:426
  93.4 2.1 collective-permute-done.12.refs_6_
  95.7 5.6 %collective-permute-done.13.refs_7_ = bf16[1,2,32,1024]{3,2,1,0:T(8,128)(2,1)S(1)} collective-permute-done((bf16[1,2,32,1024]{3,2,1,0:T(8,128)(2,1)S(1)}, bf16[1,2,32,1024]{3,2,1,0:T(8,128)(2,1)S(1)}, u32[]{:S(2)}, u32[]{:S(2)}) %collective-permute-start.13) | collective-permute-done | bytes 131104 | tf_op jit(solution)/shard_map/slope_share/ppermute | solution.py:426
  103.2 3.3 %derivatives.2 = bf16[32,2,32,512]{3,2,1,0:T(8,128)(2,1)} custom-call(f32[1]{0:T(128)S(6)} %div.4.scale_ref, bf16[2,256,1024]{2,1,0:T(8,128)(2,1)S(1)} %copy-done.3, f32[2,256,512]{2,1,0:T(8,128)S(1)} %copy-done.4, bf16[1024,512]{1,0:T(8,128)(2,1)S(1)} %copy-done.1, bf16[1,2,32,1024]{3,2,1,0:T(8,128)(2,1)S(1)} %fusion.6.refs_0_, ...), custom_call_target="tpu_custom_call" | custom-call | tf_op jit(solution)/shard_map/derivatives/pallas_call | solution.py:184
  106.5 10.2 %all-to-all-done.3 = bf16[32,2,32,512]{3,2,1,0:T(8,128)(2,1)S(1)} async-done(((bf16[32,2,32,512]{3,2,1,0:T(8,128)(2,1)}), bf16[32,2,32,512]{3,2,1,0:T(8,128)(2,1)S(1)}, u32[]{:S(2)}, u32[]{:S(2)}) %all-to-all-start.3) | async-done | bytes 2097184 | tf_op jit(solution)/shard_map/derivative_exchange/all_to_all | solution.py:496
  116.6 4.9 %all-to-all-start = ((bf16[32,2,32,512]{3,2,1,0:T(8,128)(2,1)}), bf16[32,2,32,512]{3,2,1,0:T(8,128)(2,1)}, u32[]{:S(2)}, u32[]{:S(2)}) async-start(bf16[32,2,32,512]{3,2,1,0:T(8,128)(2,1)} %derivatives.2), calls=%async_computation | async-start | bytes 4194304 | tf_op jit(solution)/shard_map/derivative_exchange/all_to_all | solution.py:496
  122.7 2.9 %gram.2 = (bf16[32,64,512]{2,1,0:T(8,128)(2,1)S(1)}, f32[2,4,1024,128]{3,2,1,0:T(8,128)}) custom-call(bf16[64,32,512]{2,1,0:T(8,128)(2,1)S(1)} %bitcast.29), custom_call_target="tpu_custom_call" | custom-call | tf_op jit(solution)/shard_map/gram/pallas_call | solution.py:246
  127.0 44.7 %all-to-all-done = bf16[32,2,32,512]{3,2,1,0:T(8,128)(2,1)} async-done(((bf16[32,2,32,512]{3,2,1,0:T(8,128)(2,1)}), bf16[32,2,32,512]{3,2,1,0:T(8,128)(2,1)}, u32[]{:S(2)}, u32[]{:S(2)}) %all-to-all-start) | async-done | bytes 2097184 | tf_op jit(solution)/shard_map/derivative_exchange/all_to_all | solution.py:496
  171.6 5.7 %gram.3 = (f32[128,128]{1,0:T(8,128)}, f32[2,4,1024,128]{3,2,1,0:T(8,128)}) custom-call(f32[1,128]{1,0:T(1,128)} %broadcast_select_fusion.energy_ref, bf16[64,32,512]{2,1,0:T(8,128)(2,1)} %bitcast.6.code_ref, bf16[32,64,512]{2,1,0:T(8,128)(2,1)} %copy-done.2), custom_call_target="tpu_custom_call" | custom-call | tf_op jit(solution)/shard_map/gram/pallas_call | solution.py:292
  177.4 11.9 %all_to_all.35 = f32[16,8,128]{2,1,0:T(8,128)S(1)} all-to-all(f32[16,8,128]{2,1,0:T(8,128)} %bitcast.30), channel_id=1, replica_groups=mesh['z'=8,'x_lo'=2,'core'=2,'y'=4,'x_hi'=2] {'z','core'}, dimensions={0} | all-to-all | bytes 131072 | tf_op jit(solution)/shard_map/gram_sum/all_to_all | solution.py:504
  189.3 9.7 %all_to_all.36 = f32[16,8,128]{2,1,0:T(8,128)S(1)} all-to-all(f32[16,8,128]{2,1,0:T(8,128)S(1)} %broadcast_in_dim.17), channel_id=1, replica_groups=mesh['z'=8,'x_lo'=2,'core'=2,'y'=4,'x_hi'=2] {'x_lo','y','x_hi'}, dimensions={0} | all-to-all | bytes 131072 | tf_op jit(solution)/shard_map/gram_sum/all_to_all | solution.py:38
  199.6 4.9 %all-to-all-start.6 = ((f32[16,8,128]{2,1,0:T(8,128)}), f32[16,8,128]{2,1,0:T(8,128)S(1)}, u32[]{:S(2)}, u32[]{:S(2)}) async-start(f32[16,8,128]{2,1,0:T(8,128)} %broadcast_in_dim.18), calls=%async_computation.6 | async-start | bytes 131072 | tf_op jit(solution)/shard_map/gram_sum/all_to_all | solution.py:38
  205.8 6.5 %all-to-all-done.6.shared_ref = f32[16,8,128]{2,1,0:T(8,128)S(1)} async-done(((f32[16,8,128]{2,1,0:T(8,128)}), f32[16,8,128]{2,1,0:T(8,128)S(1)}, u32[]{:S(2)}, u32[]{:S(2)}) %all-to-all-start.6) | async-done | bytes 65568 | tf_op jit(solution)/shard_map/gram_sum/all_to_all | solution.py:38
  213.0 5.3 %solve.1 = f32[32,512]{1,0:T(8,128)} custom-call(f32[2]{0:T(128)} %pad_maximum_fusion.scalar_ref, f32[16,8,128]{2,1,0:T(8,128)} %copy-done.11, f32[2,4,1024,128]{3,2,1,0:T(8,128)} %get-tuple-element.41.refs_0_, f32[2,4,1024,128]{3,2,1,0:T(8,128)} %get-tuple-element.42.refs_1_), custom_call_target="tpu_custom_call" | custom-call | tf_op jit(solution)/shard_map/solve/pallas_call | solution.py:387
  (60 shorter events, 14.4 us)
Async XLA Ops:
  5.2 23.7 %copy-start = (bf16[4,256,1024]{2,1,0:T(8,128)(2,1)S(1)}, bf16[4,256,1024]{2,1,0:T(8,128)(2,1)}, u32[]{:S(2)}) copy-start(bf16[4,256,1024]{2,1,0:T(8,128)(2,1)} %param.10) | copy-start | bytes 6291460
  5.2 23.7 %copy-start.7 = (s32[4,256]{1,0:T(4,128)S(1)}, s32[4,256]{1,0:T(4,128)}, u32[]{:S(2)}) copy-start(s32[4,256]{1,0:T(4,128)} %spin_ref.1) | copy-start | bytes 12292
  5.2 23.7 %copy-start.8 = (bf16[1024]{0:T(1024)(128)(2,1)S(1)}, bf16[1024]{0:T(1024)(128)(2,1)}, u32[]{:S(2)}) copy-start(bf16[1024]{0:T(1024)(128)(2,1)} %embed_ref.1) | copy-start | bytes 6148
  5.2 23.6 %copy-start.9 = (bf16[1024]{0:T(1024)(128)(2,1)S(1)}, bf16[1024]{0:T(1024)(128)(2,1)}, u32[]{:S(2)}) copy-start(bf16[1024]{0:T(1024)(128)(2,1)} %readout_ref.1) | copy-start | bytes 6148
  5.2 23.6 %all-to-all-start.1 = ((bf16[8,2,32,1024]{3,2,1,0:T(8,128)(2,1)}), bf16[8,2,32,1024]{3,2,1,0:T(8,128)(2,1)S(1)}, u32[]{:S(2)}, u32[]{:S(2)}) async-start(bf16[8,2,32,1024]{3,2,1,0:T(8,128)(2,1)} %get-tuple-element.37), calls=%async_computation.1 | async-start | bytes 2097152 | tf_op jit(solution)/shard_map/mixed_exchange/all_to_all | solution.py:465
  30.2 19.5 %all-to-all-start.2 = ((bf16[8,2,32,1024]{3,2,1,0:T(8,128)(2,1)}), bf16[8,2,32,1024]{3,2,1,0:T(8,128)(2,1)S(1)}, u32[]{:S(2)}, u32[]{:S(2)}) async-start(bf16[8,2,32,1024]{3,2,1,0:T(8,128)(2,1)} %slope.1), calls=%async_computation.2 | async-start | bytes 2097152 | tf_op jit(solution)/shard_map/slope_share/all_to_all | solution.py:484
  34.4 15.4 %copy-start.1 = (bf16[1024,512]{1,0:T(8,128)(2,1)S(1)}, bf16[1024,512]{1,0:T(8,128)(2,1)}, u32[]{:S(2)}) copy-start(bf16[1024,512]{1,0:T(8,128)(2,1)} %down_ref.3) | copy-start | bytes 3145732
  34.4 15.4 %copy-start.5 = (bf16[2,256,1024]{2,1,0:T(8,128)(2,1)S(1)}, bf16[2,256,1024]{2,1,0:T(8,128)(2,1)}, u32[]{:S(2)}) copy-start(bf16[2,256,1024]{2,1,0:T(8,128)(2,1)} %get-tuple-element.35.normed_ref) | copy-start | bytes 3145732
  49.8 1.2 copy-start.6
  55.0 22.4 %copy-start.13 = (bf16[1,2,32,1024]{3,2,1,0:T(8,128)(2,1)S(1)}, bf16[1,2,32,1024]{3,2,1,0:T(8,128)(2,1)}, u32[]{:S(2)}) copy-start(bf16[1,2,32,1024]{3,2,1,0:T(8,128)(2,1)} %get-tuple-element.31) | copy-start | bytes 393220
  55.0 30.0 %copy-start.12 = (f32[2,32,1024]{2,1,0:T(8,128)S(1)}, f32[2,32,1024]{2,1,0:T(8,128)}, u32[]{:S(2)}) copy-start(f32[2,32,1024]{2,1,0:T(8,128)} %get-tuple-element.26) | copy-start | bytes 786436
  55.0 61.6 %all-to-all-start.3 = ((bf16[32,2,32,512]{3,2,1,0:T(8,128)(2,1)}), bf16[32,2,32,512]{3,2,1,0:T(8,128)(2,1)S(1)}, u32[]{:S(2)}, u32[]{:S(2)}) async-start(bf16[32,2,32,512]{3,2,1,0:T(8,128)(2,1)} %derivatives.3), calls=%async_computation.3 | async-start | bytes 4194304 | tf_op jit(solution)/shard_map/derivative_exchange/all_to_all | solution.py:496
  66.6 35.4 %copy-start.3 = (bf16[2,256,1024]{2,1,0:T(8,128)(2,1)S(1)}, bf16[2,256,1024]{2,1,0:T(8,128)(2,1)}, u32[]{:S(2)}) copy-start(bf16[2,256,1024]{2,1,0:T(8,128)(2,1)} %get-tuple-element.24.normed_ref) | copy-start | bytes 3145732
  66.6 5.7 %collective-permute-start.3 = (bf16[1,2,32,1024]{3,2,1,0:T(8,128)(2,1)}, bf16[1,2,32,1024]{3,2,1,0:T(8,128)(2,1)S(1)}, u32[]{:S(2)}, u32[]{:S(2)}) collective-permute-start(bf16[1,2,32,1024]{3,2,1,0:T(8,128)(2,1)} %get-tuple-element.32), channel_id=1, source_target_pairs={{0,2},{1,3},{2,0},{3,1},{4,6},{5,7},{6,4},{7,5},{8,10},{9,11},{10,... | collective-permute-start | bytes 393224 | tf_op jit(solution)/shard_map/mixed_exchange/ppermute | solution.py:426
  66.7 8.2 %collective-permute-start.4 = (bf16[1,2,32,1024]{3,2,1,0:T(8,128)(2,1)}, bf16[1,2,32,1024]{3,2,1,0:T(8,128)(2,1)S(1)}, u32[]{:S(2)}, u32[]{:S(2)}) collective-permute-start(bf16[1,2,32,1024]{3,2,1,0:T(8,128)(2,1)} %get-tuple-element.33), channel_id=1, source_target_pairs={{0,4},{1,5},{2,6},{3,7},{4,0},{5,1},{6,2},{7,3},{8,12},{9,13},{10,... | collective-permute-start | bytes 393224 | tf_op jit(solution)/shard_map/mixed_exchange/ppermute | solution.py:426
  68.4 9.0 %collective-permute-start.5 = (bf16[1,2,32,1024]{3,2,1,0:T(8,128)(2,1)}, bf16[1,2,32,1024]{3,2,1,0:T(8,128)(2,1)S(1)}, u32[]{:S(2)}, u32[]{:S(2)}) collective-permute-start(bf16[1,2,32,1024]{3,2,1,0:T(8,128)(2,1)} %get-tuple-element.34), channel_id=1, source_target_pairs={{0,6},{1,7},{2,4},{3,5},{4,2},{5,3},{6,0},{7,1},{8,14},{9,15},{10,... | collective-permute-start | bytes 393224 | tf_op jit(solution)/shard_map/mixed_exchange/ppermute | solution.py:426
  70.5 8.5 %collective-permute-start = (bf16[1,2,32,1024]{3,2,1,0:T(8,128)(2,1)}, bf16[1,2,32,1024]{3,2,1,0:T(8,128)(2,1)S(1)}, u32[]{:S(2)}, u32[]{:S(2)}) collective-permute-start(bf16[1,2,32,1024]{3,2,1,0:T(8,128)(2,1)} %get-tuple-element.28), channel_id=1, source_target_pairs={{0,2},{1,3},{2,0},{3,1},{4,6},{5,7},{6,4},{7,5},{8,10},{9,11},{10,... | collective-permute-start | bytes 393224 | tf_op jit(solution)/shard_map/mixed_exchange/ppermute | solution.py:426
  70.5 10.0 %collective-permute-start.1 = (bf16[1,2,32,1024]{3,2,1,0:T(8,128)(2,1)}, bf16[1,2,32,1024]{3,2,1,0:T(8,128)(2,1)S(1)}, u32[]{:S(2)}, u32[]{:S(2)}) collective-permute-start(bf16[1,2,32,1024]{3,2,1,0:T(8,128)(2,1)} %get-tuple-element.29), channel_id=1, source_target_pairs={{0,4},{1,5},{2,6},{3,7},{4,0},{5,1},{6,2},{7,3},{8,12},{9,13},{10,... | collective-permute-start | bytes 393224 | tf_op jit(solution)/shard_map/mixed_exchange/ppermute | solution.py:426
  72.3 10.7 %collective-permute-start.2 = (bf16[1,2,32,1024]{3,2,1,0:T(8,128)(2,1)}, bf16[1,2,32,1024]{3,2,1,0:T(8,128)(2,1)S(1)}, u32[]{:S(2)}, u32[]{:S(2)}) collective-permute-start(bf16[1,2,32,1024]{3,2,1,0:T(8,128)(2,1)} %get-tuple-element.30), channel_id=1, source_target_pairs={{0,6},{1,7},{2,4},{3,5},{4,2},{5,3},{6,0},{7,1},{8,14},{9,15},{10,... | collective-permute-start | bytes 393224 | tf_op jit(solution)/shard_map/mixed_exchange/ppermute | solution.py:426
  77.5 7.6 %collective-permute-start.6 = (bf16[1,2,32,1024]{3,2,1,0:T(8,128)(2,1)S(1)}, bf16[1,2,32,1024]{3,2,1,0:T(8,128)(2,1)S(1)}, u32[]{:S(2)}, u32[]{:S(2)}) collective-permute-start(bf16[1,2,32,1024]{3,2,1,0:T(8,128)(2,1)S(1)} %add_convert_fusion), channel_id=1, source_target_pairs={{0,1},{1,0},{2,3},{3,2},{4,5},{5,4},{6,7},{7,6},{8,9},{9,8},{10,11... | collective-permute-start | bytes 393224 | tf_op jit(solution)/shard_map/mixed_exchange/ppermute | solution.py:426
  86.1 5.7 %collective-permute-start.7 = (bf16[1,2,32,1024]{3,2,1,0:T(8,128)(2,1)S(1)}, bf16[1,2,32,1024]{3,2,1,0:T(8,128)(2,1)S(1)}, u32[]{:S(2)}, u32[]{:S(2)}) collective-permute-start(bf16[1,2,32,1024]{3,2,1,0:T(8,128)(2,1)S(1)} %fusion.6.refs_0_), channel_id=1, source_target_pairs={{0,1},{1,0},{2,3},{3,2},{4,5},{5,4},{6,7},{7,6},{8,9},{9,8},{10,11... | collective-permute-start | bytes 393224 | tf_op jit(solution)/shard_map/slope_share/ppermute | solution.py:426
  88.0 7.4 %collective-permute-start.12 = (bf16[1,2,32,1024]{3,2,1,0:T(8,128)(2,1)S(1)}, bf16[1,2,32,1024]{3,2,1,0:T(8,128)(2,1)S(1)}, u32[]{:S(2)}, u32[]{:S(2)}) collective-permute-start(bf16[1,2,32,1024]{3,2,1,0:T(8,128)(2,1)S(1)} %fusion.6.refs_0_), channel_id=1, source_target_pairs={{0,6},{1,7},{2,4},{3,5},{4,2},{5,3},{6,0},{7,1},{8,14},{9,15},{10,... | collective-permute-start | bytes 393224 | tf_op jit(solution)/shard_map/slope_share/ppermute | solution.py:426
  88.2 7.2 %collective-permute-start.10 = (bf16[1,2,32,1024]{3,2,1,0:T(8,128)(2,1)S(1)}, bf16[1,2,32,1024]{3,2,1,0:T(8,128)(2,1)S(1)}, u32[]{:S(2)}, u32[]{:S(2)}) collective-permute-start(bf16[1,2,32,1024]{3,2,1,0:T(8,128)(2,1)S(1)} %fusion.6.refs_0_), channel_id=1, source_target_pairs={{0,4},{1,5},{2,6},{3,7},{4,0},{5,1},{6,2},{7,3},{8,12},{9,13},{10,... | collective-permute-start | bytes 393224 | tf_op jit(solution)/shard_map/slope_share/ppermute | solution.py:426
  88.2 7.5 %collective-permute-start.8 = (bf16[1,2,32,1024]{3,2,1,0:T(8,128)(2,1)S(1)}, bf16[1,2,32,1024]{3,2,1,0:T(8,128)(2,1)S(1)}, u32[]{:S(2)}, u32[]{:S(2)}) collective-permute-start(bf16[1,2,32,1024]{3,2,1,0:T(8,128)(2,1)S(1)} %fusion.6.refs_0_), channel_id=1, source_target_pairs={{0,2},{1,3},{2,0},{3,1},{4,6},{5,7},{6,4},{7,5},{8,10},{9,11},{10,... | collective-permute-start | bytes 393224 | tf_op jit(solution)/shard_map/slope_share/ppermute | solution.py:426
  91.8 9.6 %collective-permute-start.13 = (bf16[1,2,32,1024]{3,2,1,0:T(8,128)(2,1)S(1)}, bf16[1,2,32,1024]{3,2,1,0:T(8,128)(2,1)S(1)}, u32[]{:S(2)}, u32[]{:S(2)}) collective-permute-start(bf16[1,2,32,1024]{3,2,1,0:T(8,128)(2,1)S(1)} %collective-permute-done.7.refs_1_), channel_id=1, source_target_pairs={{0,6},{1,7},{2,4},{3,5},{4,2},{5,3},{6,0},{7,1},{8,14},{9,15},{10,... | collective-permute-start | bytes 393224 | tf_op jit(solution)/shard_map/slope_share/ppermute | solution.py:426
  92.5 8.8 %collective-permute-start.11 = (bf16[1,2,32,1024]{3,2,1,0:T(8,128)(2,1)S(1)}, bf16[1,2,32,1024]{3,2,1,0:T(8,128)(2,1)S(1)}, u32[]{:S(2)}, u32[]{:S(2)}) collective-permute-start(bf16[1,2,32,1024]{3,2,1,0:T(8,128)(2,1)S(1)} %collective-permute-done.7.refs_1_), channel_id=1, source_target_pairs={{0,4},{1,5},{2,6},{3,7},{4,0},{5,1},{6,2},{7,3},{8,12},{9,13},{10,... | collective-permute-start | bytes 393224 | tf_op jit(solution)/shard_map/slope_share/ppermute | solution.py:426
  95.5 6.5 %collective-permute-start.9 = (bf16[1,2,32,1024]{3,2,1,0:T(8,128)(2,1)S(1)}, bf16[1,2,32,1024]{3,2,1,0:T(8,128)(2,1)S(1)}, u32[]{:S(2)}, u32[]{:S(2)}) collective-permute-start(bf16[1,2,32,1024]{3,2,1,0:T(8,128)(2,1)S(1)} %collective-permute-done.7.refs_1_), channel_id=1, source_target_pairs={{0,2},{1,3},{2,0},{3,1},{4,6},{5,7},{6,4},{7,5},{8,10},{9,11},{10,... | collective-permute-start | bytes 393224 | tf_op jit(solution)/shard_map/slope_share/ppermute | solution.py:426
  102.0 1.2 copy-start.4
  106.5 15.1 %copy-start.14 = (f32[4]{0:T(128)S(1)}, f32[4]{0:T(128)}, u32[]{:S(2)}) copy-start(f32[4]{0:T(128)} %param.16) | copy-start | bytes 52
  116.6 55.0 %all-to-all-start = ((bf16[32,2,32,512]{3,2,1,0:T(8,128)(2,1)}), bf16[32,2,32,512]{3,2,1,0:T(8,128)(2,1)}, u32[]{:S(2)}, u32[]{:S(2)}) async-start(bf16[32,2,32,512]{3,2,1,0:T(8,128)(2,1)} %derivatives.2), calls=%async_computation | async-start | bytes 4194304 | tf_op jit(solution)/shard_map/derivative_exchange/all_to_all | solution.py:496
  125.6 1.4 copy-start.2
  199.6 12.7 %all-to-all-start.6 = ((f32[16,8,128]{2,1,0:T(8,128)}), f32[16,8,128]{2,1,0:T(8,128)S(1)}, u32[]{:S(2)}, u32[]{:S(2)}) async-start(f32[16,8,128]{2,1,0:T(8,128)} %broadcast_in_dim.18), calls=%async_computation.6 | async-start | bytes 131072 | tf_op jit(solution)/shard_map/gram_sum/all_to_all | solution.py:38
  (2 other events, 1.3 us)

commit v6 on v5

--- a/solution.py
+++ b/solution.py
@@ -126,7 +126,8 @@
     )(*[order] * pairs, spins, features, embed, gain, up, down)
 
 
-def slope_kernel(own_ref, part_ref, spin_ref, feature_ref, embed_ref, readout_ref, slope_ref):
+def slope_kernel(own_ref, part_ref, spin_ref, feature_ref, embed_ref, readout_ref, *refs):
+    slope_ref = refs[-1]
     blocks, samples, rows, width = part_ref.shape
     own = own_ref[0]
     offset = lax.broadcasted_iota(jnp.int32, (rows, blocks * rows), 1) - lax.broadcasted_iota(
@@ -141,16 +142,15 @@
         for k in range(blocks):
             outputs = outputs + part_ref[k, s].astype(jnp.float32)
         slope = (readout * jnp.tanh(outputs)).astype(jnp.bfloat16)
-        for k in range(blocks):
-            slope_ref[k, s] = slope
-
-
-def own_slope(own, parts, spins, features, embed, readout):
+        slope_ref[0, s] = slope
+
+
+def own_slope(own, parts, spins, features, embed, readout, after):
     whole = lambda array: pl.BlockSpec(array.shape, lambda s: (0,) * array.ndim)
     return pl.pallas_call(
         slope_kernel,
         grid=(1,),
-        out_shape=pltpu.HBM(parts.shape, parts.dtype),
+        out_shape=pltpu.HBM((1,) + parts.shape[1:], parts.dtype),
         in_specs=[
             SMEM,
             whole(parts),
@@ -158,16 +158,21 @@
             pl.BlockSpec((parts.shape[1],) + features.shape[1:], lambda s: (0, 0, 0, 0)),
             whole(embed),
             whole(readout),
-        ],
-        out_specs=whole(parts),
+        ]
+        + [pl.BlockSpec(memory_space=pl.ANY)] * len(after),
+        out_specs=pl.BlockSpec((1,) + parts.shape[1:], lambda s: (0, 0, 0, 0)),
         compiler_params=pltpu.CompilerParams(vmem_limit_bytes=VMEM_SMALL),
-    )(own, parts, spins, features, embed, readout)
-
-
-def derivative_kernel(slope_count, scale_ref, normed_ref, bend_ref, down_ref, *refs):
-    slope_refs, coded_ref = refs[:slope_count], refs[-1]
+    )(own, parts, spins, features, embed, readout, *after)
+
+
+def derivative_kernel(order_ref, scale_ref, normed_ref, bend_ref, down_ref, *refs):
+    *slope_refs, coded_ref, slope_ref = refs
     tokens, width = normed_ref.shape[1:]
-    slope = jnp.concatenate([r[:, 0].reshape(-1, width) for r in slope_refs], axis=0)
+    rows = slope_refs[0].shape[2]
+    for k, received_ref in enumerate(slope_refs):
+        start = pl.multiple_of(jnp.bitwise_xor(order_ref[0], k) * rows, rows)
+        slope_ref[pl.ds(start, rows)] = received_ref[0, 0]
+    slope = slope_ref[...]
     back_proj = jnp.dot(slope, down_ref[...], preferred_element_type=jnp.float32)
     pullback = (bend_ref[0] * back_proj).astype(jnp.bfloat16)
     deriv = lax.dot_general(
@@ -177,14 +182,15 @@
     coded_ref[:, 0] = coded.reshape(coded_ref.shape[0], coded_ref.shape[2], coded_ref.shape[3])
 
 
-def derivative(scale, normed, bend, down, slopes, parts, after):
+def derivative(order, scale, normed, bend, down, slopes, parts, limit):
     samples, tokens, width = normed.shape
     hidden = down.shape[1]
     block = lambda *shape: pl.BlockSpec((1,) + shape, lambda s: (s,) + (0,) * len(shape))
     return pl.pallas_call(
-        functools.partial(derivative_kernel, len(slopes)),
+        derivative_kernel,
         grid=(samples,),
         in_specs=[
+            SMEM,
             SMEM,
             block(tokens, width),
             block(tokens, hidden),
@@ -193,12 +199,12 @@
         + [
             pl.BlockSpec((a.shape[0], 1) + a.shape[2:], lambda s: (0, s, 0, 0))
             for a in slopes
-        ]
-        + [pl.BlockSpec(memory_space=pl.ANY)] * len(after),
+        ],
         out_specs=pl.BlockSpec((parts, 1, width // parts, hidden), lambda s: (0, s, 0, 0)),
         out_shape=pltpu.HBM((parts, samples, width // parts, hidden), jnp.bfloat16),
-        compiler_params=pltpu.CompilerParams(vmem_limit_bytes=VMEM_SMALL),
-    )(scale, normed, bend, down, *slopes, *after)
+        scratch_shapes=[pltpu.VMEM((tokens, width), jnp.bfloat16)],
+        compiler_params=pltpu.CompilerParams(vmem_limit_bytes=limit),
+    )(order, scale, normed, bend, down, *slopes)
 
 
 LANES = 128
@@ -460,6 +466,7 @@
     for n, (normed, bend, *parts) in enumerate(states):
         if n > 0:
             own_inputs, _, *parts = parts
+            *parts, coded_chunks[-1] = lax.optimization_barrier((*parts, coded_chunks[-1]))
         with jax.named_scope("mixed_exchange"):
             if n == 0:
                 mixed_parts = lax.all_to_all(parts[0], MP, 0, 0)
@@ -474,23 +481,35 @@
         with jax.named_scope("slope"):
             if n == 0:
                 slope = own_slope(
-                    place.reshape(1), mixed_parts, spin_values, feature_blocks, spin_embed, readout
+                    place.reshape(1),
+                    mixed_parts,
+                    spin_values,
+                    feature_blocks,
+                    spin_embed,
+                    readout,
+                    [state[3] for state in states[1:2]],
                 )
             else:
                 outputs = mixed_own + mixed_other.astype(jnp.float32)
                 slope = (readout_wide * jnp.tanh(outputs)).astype(jnp.bfloat16)
         with jax.named_scope("slope_share"):
-            if n == 0:
-                slopes = [lax.all_to_all(slope, MP, 0, 0)]
-            else:
-                other = partner(slope, 1)
-                slopes = [slope, other]
-                for k in range(2, mp_size, 2):
-                    slopes += [partner(slope, k), partner(other, k)]
+            other = partner(slope, 1)
+            slopes = [slope, other]
+            for k in range(2, mp_size, 2):
+                slopes += [partner(slope, k), partner(other, k)]
         with jax.named_scope("derivatives"):
-            after = [state[3] for state in states[n + 1 : n + 2]]
+            order = jnp.zeros((1,), jnp.int32) if n else place.reshape(1)
             coded_chunks.append(
-                derivative(1.0 / unit, normed, bend, down_weight, slopes, samp_size, after)
+                derivative(
+                    order,
+                    1.0 / unit,
+                    normed,
+                    bend,
+                    down_weight,
+                    slopes,
+                    samp_size,
+                    VMEM_SMALL if n else VMEM_LIMIT,
+                )
             )
     with jax.named_scope("derivative_exchange"):
         chunks = [lax.all_to_all(c, SAMPLES, 0, 0) for c in coded_chunks]

time: 219 us -> 217 us (level)
  waiting for transfers between devices: 104 us -> 95.2 us
  starting transfers between devices: 49.3 us -> 54.8 us
    all_to_all x1 -> x0, waiting for transfers between devices: 8.62 us -> none  [body(): slopes = [lax.all_to_all(slope, MP, 0, 0)]]
    ppermute x14 -> x21, starting transfers between devices: 16.2 us -> 24.5 us  [partner(): return lax.ppermute(array, MP, [(i, i ^ k) for i in range(mp_size)])]
    all_to_all x1, waiting for transfers between devices: 16 us -> 10.5 us  [body(): mixed_parts = lax.all_to_all(parts[0], MP, 0, 0)]
    ppermute x14 -> x21, waiting for transfers between devices: 18 us -> 22.9 us  [partner(): return lax.ppermute(array, MP, [(i, i ^ k) for i in range(mp_size)])]
    all_to_all x1 -> x0, starting transfers between devices: 4.12 us -> none  [body(): slopes = [lax.all_to_all(slope, MP, 0, 0)]]
    unnamed x30 -> x40, local copies, waits for them, and re-layouts: 5.16 us -> 4.71 us
  transfers between devices with their start and end apart: 19 -> 25, of which waited for: 15 -> 15; matrix products, arithmetic and copies ran while one was open for 2% -> 2% of each run, Pallas kernels for 5% -> 5%
where the time goes in v6:
time: 217 us; the launch traced here: 216 us
  waiting for transfers between devices  95.2 us (44%)
  starting transfers between devices  54.8 us (25%)
  Pallas kernels  34.4 us (16%)
  blocking collectives  21.5 us (10%)
  local copies, waits for them, and re-layouts  5.85 us (3%)
  other arithmetic  3.01 us (1%)
    all_to_all x2, waiting for transfers between devices, body(): chunks = [lax.all_to_all(c, SAMPLES, 0, 0) for c in coded_chunks]  55.3 us
    ppermute x21, starting transfers between devices, partner(): return lax.ppermute(array, MP, [(i, i ^ k) for i in range(mp_size)])  24.5 us
    ppermute x21, waiting for transfers between devices, partner(): return lax.ppermute(array, MP, [(i, i ^ k) for i in range(mp_size)])  22.9 us
    all_to_all x2, starting transfers between devices, body(): chunks = [lax.all_to_all(c, SAMPLES, 0, 0) for c in coded_chunks]  17.9 us
    all_to_all x1, blocking collectives, body(): lax.all_to_all(gram_part.reshape(near_size, sample_count // near_size, sa...  11.9 us
    pallas_call x2, Pallas kernels, forward(): pl.pallas_call(functools.partial(forward_kernel, first, pairs), grid=(sam...  10.7 us
    all_to_all x1, waiting for transfers between devices, body(): mixed_parts = lax.all_to_all(parts[0], MP, 0, 0)  10.5 us
    all_to_all x1, blocking collectives, share(): lax.all_to_all(jnp.broadcast_to(array, (size,) + array.shape), axis, 0, 0)  9.53 us
  transfers between devices with their start and end apart: 25, of which 15 were waited for; matrix products, arithmetic and copies ran while one was open for 2% of the time, Pallas kernels for 5%

profile of v6, /device:TPU:1, one launch (start us, length us, event | category | flops | bytes accessed | tf_op | source)
XLA Modules:
  0.0 216.5 jit_solution(3184243718096444967)
XLA Ops:
  0.0 5.2 %forward.3 = (bf16[2,256,1024]{2,1,0:T(8,128)(2,1)}, f32[2,256,512]{2,1,0:T(8,128)}, bf16[8,2,32,1024]{3,2,1,0:T(8,128)(2,1)}) custom-call(s32[4,256]{1,0:T(4,128)} %spin_ref.1, bf16[4,8,32,1024]{3,2,1,0:T(8,128)(2,1)} %bitcast.26, bf16[1024]{0:T(1024)(128)(2,1)} %embed_ref.1, bf16[1024]{0:T(1024)(128)(2,1)} %refs_3_.3, bf16[1024,512]{1,0:T(8,128)(2,1)} %refs_4_.3, ...), custom_call_target="tpu_custom_call" | custom-call | tf_op jit(solution)/shard_map/forward/pallas_call | solution.py:107
  5.2 7.5 %all-to-all-start = ((bf16[8,2,32,1024]{3,2,1,0:T(8,128)(2,1)}), bf16[8,2,32,1024]{3,2,1,0:T(8,128)(2,1)S(1)}, u32[]{:S(2)}, u32[]{:S(2)}) async-start(bf16[8,2,32,1024]{3,2,1,0:T(8,128)(2,1)} %get-tuple-element.46), calls=%async_computation | async-start | bytes 2097152 | tf_op jit(solution)/shard_map/mixed_exchange/all_to_all | solution.py:472
  12.7 5.4 %forward.2 = (bf16[2,256,1024]{2,1,0:T(8,128)(2,1)}, f32[2,256,512]{2,1,0:T(8,128)}, f32[2,32,1024]{2,1,0:T(8,128)}, f32[8,128]{1,0:T(8,128)}, bf16[1,2,32,1024]...) custom-call(s32[1]{0:T(128)} %bitcast.3.refs_0_.own_ref.order_ref, ...), custom_call_target="tpu_custom_call" | custom-call | tf_op jit(solution)/shard_map/forward/pallas_call | solution.py:107
  18.2 10.5 %all-to-all-done.part_ref = bf16[8,2,32,1024]{3,2,1,0:T(8,128)(2,1)S(1)} async-done(((bf16[8,2,32,1024]{3,2,1,0:T(8,128)(2,1)}), bf16[8,2,32,1024]{3,2,1,0:T(8,128)(2,1)S(1)}, u32[]{:S(2)}, u32[]{:S(2)}) %all-to-all-start) | async-done | bytes 1048608 | tf_op jit(solution)/shard_map/mixed_exchange/all_to_all | solution.py:472
  31.1 2.4 %collective-permute-start.5 = (bf16[1,2,32,1024]{3,2,1,0:T(8,128)(2,1)}, bf16[1,2,32,1024]{3,2,1,0:T(8,128)(2,1)S(1)}, u32[]{:S(2)}, u32[]{:S(2)}) collective-permute-start(bf16[1,2,32,1024]{3,2,1,0:T(8,128)(2,1)} %slope.1.refs_0_), channel_id=1, source_target_pairs={{0,6},{1,7},{2,4},{3,5},{4,2},{5,3},{6,0},{7,1},{8,14},{9,15},{10,... | collective-permute-start | bytes 393224 | tf_op jit(solution)/shard_map/slope_share/ppermute | solution.py:432
  40.5 4.9 %collective-permute-done.6.refs_7_ = bf16[1,2,32,1024]{3,2,1,0:T(8,128)(2,1)S(1)} collective-permute-done((bf16[1,2,32,1024]{3,2,1,0:T(8,128)(2,1)S(1)}, bf16[1,2,32,1024]{3,2,1,0:T(8,128)(2,1)S(1)}, u32[]{:S(2)}, u32[]{:S(2)}) %collective-permute-start.6) | collective-permute-done | bytes 131104 | tf_op jit(solution)/shard_map/slope_share/ppermute | solution.py:432
  46.2 5.4 %derivatives.2 = bf16[32,2,32,512]{3,2,1,0:T(8,128)(2,1)} custom-call(s32[1]{0:T(128)} %bitcast.3.refs_0_.own_ref.order_ref, f32[1]{0:T(128)S(6)} %div.4.scale_ref, bf16[2,256,1024]{2,1,0:T(8,128)(2,1)} %get-tuple-element.44.normed_ref, f32[2,256,512]{2,1,0:T(8,128)} %get-tuple-element.45.bend_ref, bf16[1024,512]{1,0:T(8,128)(2,1)} %down_ref.3, ...), custom_call_target="tpu_custom_call" | custom-call | tf_op jit(solution)/shard_map/derivatives/pallas_call | solution.py:189
  51.7 13.0 %all-to-all-start.2 = ((bf16[32,2,32,512]{3,2,1,0:T(8,128)(2,1)}), bf16[32,2,32,512]{3,2,1,0:T(8,128)(2,1)S(1)}, u32[]{:S(2)}, u32[]{:S(2)}) async-start(bf16[32,2,32,512]{3,2,1,0:T(8,128)(2,1)} %derivatives.2), calls=%async_computation.2 | async-start | bytes 4194304 | tf_op jit(solution)/shard_map/derivative_exchange/all_to_all | solution.py:515
  64.8 1.8 collective-permute-start.11
  66.7 2.0 collective-permute-start.12
  68.7 1.8 collective-permute-start.8
  70.5 2.0 collective-permute-start.9
  73.1 2.5 %collective-permute-done.12 = bf16[1,2,32,1024]{3,2,1,0:T(8,128)(2,1)S(1)} collective-permute-done((bf16[1,2,32,1024]{3,2,1,0:T(8,128)(2,1)}, bf16[1,2,32,1024]{3,2,1,0:T(8,128)(2,1)S(1)}, u32[]{:S(2)}, u32[]{:S(2)}) %collective-permute-start.12) | collective-permute-done | bytes 131104 | tf_op jit(solution)/shard_map/mixed_exchange/ppermute | solution.py:432
  75.7 1.6 collective-permute-start.13
  77.3 1.5 collective-permute-done.8
  78.8 2.5 %collective-permute-done.9 = bf16[1,2,32,1024]{3,2,1,0:T(8,128)(2,1)S(1)} collective-permute-done((bf16[1,2,32,1024]{3,2,1,0:T(8,128)(2,1)}, bf16[1,2,32,1024]{3,2,1,0:T(8,128)(2,1)S(1)}, u32[]{:S(2)}, u32[]{:S(2)}) %collective-permute-start.9) | collective-permute-done | bytes 131104 | tf_op jit(solution)/shard_map/mixed_exchange/ppermute | solution.py:432
  83.6 2.6 %collective-permute-start.14 = (bf16[1,2,32,1024]{3,2,1,0:T(8,128)(2,1)S(1)}, bf16[1,2,32,1024]{3,2,1,0:T(8,128)(2,1)S(1)}, u32[]{:S(2)}, u32[]{:S(2)}) collective-permute-start(bf16[1,2,32,1024]{3,2,1,0:T(8,128)(2,1)S(1)} %fusion.6.refs_0_), channel_id=1, source_target_pairs={{0,1},{1,0},{2,3},{3,2},{4,5},{5,4},{6,7},{7,6},{8,9},{9,8},{10,11... | collective-permute-start | bytes 393224 | tf_op jit(solution)/shard_map/slope_share/ppermute | solution.py:432
  86.6 2.9 %collective-permute-start.15 = (bf16[1,2,32,1024]{3,2,1,0:T(8,128)(2,1)S(1)}, bf16[1,2,32,1024]{3,2,1,0:T(8,128)(2,1)S(1)}, u32[]{:S(2)}, u32[]{:S(2)}) collective-permute-start(bf16[1,2,32,1024]{3,2,1,0:T(8,128)(2,1)S(1)} %fusion.6.refs_0_), channel_id=1, source_target_pairs={{0,2},{1,3},{2,0},{3,1},{4,6},{5,7},{6,4},{7,5},{8,10},{9,11},{10,... | collective-permute-start | bytes 393224 | tf_op jit(solution)/shard_map/slope_share/ppermute | solution.py:432
  91.2 2.3 %collective-permute-done.19.refs_6_ = bf16[1,2,32,1024]{3,2,1,0:T(8,128)(2,1)S(1)} collective-permute-done((bf16[1,2,32,1024]{3,2,1,0:T(8,128)(2,1)S(1)}, bf16[1,2,32,1024]{3,2,1,0:T(8,128)(2,1)S(1)}, u32[]{:S(2)}, u32[]{:S(2)}) %collective-permute-start.19) | collective-permute-done | bytes 131104 | tf_op jit(solution)/shard_map/slope_share/ppermute | solution.py:432
  93.9 5.3 %collective-permute-done.20.refs_7_ = bf16[1,2,32,1024]{3,2,1,0:T(8,128)(2,1)S(1)} collective-permute-done((bf16[1,2,32,1024]{3,2,1,0:T(8,128)(2,1)S(1)}, bf16[1,2,32,1024]{3,2,1,0:T(8,128)(2,1)S(1)}, u32[]{:S(2)}, u32[]{:S(2)}) %collective-permute-start.20) | collective-permute-done | bytes 131104 | tf_op jit(solution)/shard_map/slope_share/ppermute | solution.py:432
  100.8 3.3 %derivatives.3 = bf16[32,2,32,512]{3,2,1,0:T(8,128)(2,1)} custom-call(s32[1]{0:T(128)} %constant.41.clone.1.order_ref, f32[1]{0:T(128)S(6)} %div.4.scale_ref, bf16[2,256,1024]{2,1,0:T(8,128)(2,1)S(1)} %copy-done.3, f32[2,256,512]{2,1,0:T(8,128)S(1)} %copy-done.4, bf16[1024,512]{1,0:T(8,128)(2,1)S(1)} %copy-done.1, ...), custom_call_target="tpu_custom_call" | custom-call | tf_op jit(solution)/shard_map/derivatives/pallas_call | solution.py:189
  104.1 10.7 %all-to-all-done.2 = bf16[32,2,32,512]{3,2,1,0:T(8,128)(2,1)S(1)} async-done(((bf16[32,2,32,512]{3,2,1,0:T(8,128)(2,1)}), bf16[32,2,32,512]{3,2,1,0:T(8,128)(2,1)S(1)}, u32[]{:S(2)}, u32[]{:S(2)}) %all-to-all-start.2) | async-done | bytes 2097184 | tf_op jit(solution)/shard_map/derivative_exchange/all_to_all | solution.py:515
  114.8 4.9 %all-to-all-start.1 = ((bf16[32,2,32,512]{3,2,1,0:T(8,128)(2,1)}), bf16[32,2,32,512]{3,2,1,0:T(8,128)(2,1)}, u32[]{:S(2)}, u32[]{:S(2)}) async-start(bf16[32,2,32,512]{3,2,1,0:T(8,128)(2,1)} %derivatives.3), calls=%async_computation.1 | async-start | bytes 4194304 | tf_op jit(solution)/shard_map/derivative_exchange/all_to_all | solution.py:515
  120.8 2.9 %gram.2 = (bf16[32,64,512]{2,1,0:T(8,128)(2,1)S(1)}, f32[2,4,1024,128]{3,2,1,0:T(8,128)}) custom-call(bf16[64,32,512]{2,1,0:T(8,128)(2,1)S(1)} %bitcast.29), custom_call_target="tpu_custom_call" | custom-call | tf_op jit(solution)/shard_map/gram/pallas_call | solution.py:252
  123.8 1.4 copy-done.2
  125.2 44.6 %all-to-all-done.1 = bf16[32,2,32,512]{3,2,1,0:T(8,128)(2,1)} async-done(((bf16[32,2,32,512]{3,2,1,0:T(8,128)(2,1)}), bf16[32,2,32,512]{3,2,1,0:T(8,128)(2,1)}, u32[]{:S(2)}, u32[]{:S(2)}) %all-to-all-start.1) | async-done | bytes 2097184 | tf_op jit(solution)/shard_map/derivative_exchange/all_to_all | solution.py:515
  169.8 5.7 %gram.3 = (f32[128,128]{1,0:T(8,128)}, f32[2,4,1024,128]{3,2,1,0:T(8,128)}) custom-call(f32[1,128]{1,0:T(1,128)} %broadcast_select_fusion.energy_ref, bf16[64,32,512]{2,1,0:T(8,128)(2,1)} %bitcast.6.code_ref, bf16[32,64,512]{2,1,0:T(8,128)(2,1)} %copy-done.2), custom_call_target="tpu_custom_call" | custom-call | tf_op jit(solution)/shard_map/gram/pallas_call | solution.py:298
  175.5 11.9 %all_to_all.30 = f32[16,8,128]{2,1,0:T(8,128)S(1)} all-to-all(f32[16,8,128]{2,1,0:T(8,128)} %bitcast.30), channel_id=1, replica_groups=mesh['z'=8,'x_lo'=2,'core'=2,'y'=4,'x_hi'=2] {'z','core'}, dimensions={0} | all-to-all | bytes 131072 | tf_op jit(solution)/shard_map/gram_sum/all_to_all | solution.py:523
  187.5 9.5 %all_to_all.31 = f32[16,8,128]{2,1,0:T(8,128)S(1)} all-to-all(f32[16,8,128]{2,1,0:T(8,128)S(1)} %broadcast_in_dim.17), channel_id=1, replica_groups=mesh['z'=8,'x_lo'=2,'core'=2,'y'=4,'x_hi'=2] {'x_lo','y','x_hi'}, dimensions={0} | all-to-all | bytes 131072 | tf_op jit(solution)/shard_map/gram_sum/all_to_all | solution.py:38
  197.7 4.9 %all-to-all-start.5 = ((f32[16,8,128]{2,1,0:T(8,128)}), f32[16,8,128]{2,1,0:T(8,128)S(1)}, u32[]{:S(2)}, u32[]{:S(2)}) async-start(f32[16,8,128]{2,1,0:T(8,128)} %broadcast_in_dim.18), calls=%async_computation.5 | async-start | bytes 131072 | tf_op jit(solution)/shard_map/gram_sum/all_to_all | solution.py:38
  203.9 6.5 %all-to-all-done.5.shared_ref = f32[16,8,128]{2,1,0:T(8,128)S(1)} async-done(((f32[16,8,128]{2,1,0:T(8,128)}), f32[16,8,128]{2,1,0:T(8,128)S(1)}, u32[]{:S(2)}, u32[]{:S(2)}) %all-to-all-start.5) | async-done | bytes 65568 | tf_op jit(solution)/shard_map/gram_sum/all_to_all | solution.py:38
  211.0 5.3 %solve.1 = f32[32,512]{1,0:T(8,128)} custom-call(f32[2]{0:T(128)} %pad_maximum_fusion.scalar_ref, f32[16,8,128]{2,1,0:T(8,128)} %copy-done.9, f32[2,4,1024,128]{3,2,1,0:T(8,128)} %get-tuple-element.59.refs_0_, f32[2,4,1024,128]{3,2,1,0:T(8,128)} %get-tuple-element.60.refs_1_), custom_call_target="tpu_custom_call" | custom-call | tf_op jit(solution)/shard_map/solve/pallas_call | solution.py:393
  (82 shorter events, 19.7 us)
Async XLA Ops:
  5.2 23.5 %all-to-all-start = ((bf16[8,2,32,1024]{3,2,1,0:T(8,128)(2,1)}), bf16[8,2,32,1024]{3,2,1,0:T(8,128)(2,1)S(1)}, u32[]{:S(2)}, u32[]{:S(2)}) async-start(bf16[8,2,32,1024]{3,2,1,0:T(8,128)(2,1)} %get-tuple-element.46), calls=%async_computation | async-start | bytes 2097152 | tf_op jit(solution)/shard_map/mixed_exchange/all_to_all | solution.py:472
  12.7 16.0 %copy-start = (bf16[4,256,1024]{2,1,0:T(8,128)(2,1)S(1)}, bf16[4,256,1024]{2,1,0:T(8,128)(2,1)}, u32[]{:S(2)}) copy-start(bf16[4,256,1024]{2,1,0:T(8,128)(2,1)} %param.10) | copy-start | bytes 6291460
  12.7 16.0 %copy-start.5 = (s32[4,256]{1,0:T(4,128)S(1)}, s32[4,256]{1,0:T(4,128)}, u32[]{:S(2)}) copy-start(s32[4,256]{1,0:T(4,128)} %spin_ref.1) | copy-start | bytes 12292
  12.7 16.0 %copy-start.6 = (bf16[1024]{0:T(1024)(128)(2,1)S(1)}, bf16[1024]{0:T(1024)(128)(2,1)}, u32[]{:S(2)}) copy-start(bf16[1024]{0:T(1024)(128)(2,1)} %embed_ref.1) | copy-start | bytes 6148
  30.4 5.5 %collective-permute-start = (bf16[1,2,32,1024]{3,2,1,0:T(8,128)(2,1)}, bf16[1,2,32,1024]{3,2,1,0:T(8,128)(2,1)S(1)}, u32[]{:S(2)}, u32[]{:S(2)}) collective-permute-start(bf16[1,2,32,1024]{3,2,1,0:T(8,128)(2,1)} %slope.1.refs_0_), channel_id=1, source_target_pairs={{0,1},{1,0},{2,3},{3,2},{4,5},{5,4},{6,7},{7,6},{8,9},{9,8},{10,11... | collective-permute-start | bytes 393224 | tf_op jit(solution)/shard_map/slope_share/ppermute | solution.py:432
  31.1 6.8 %collective-permute-start.5 = (bf16[1,2,32,1024]{3,2,1,0:T(8,128)(2,1)}, bf16[1,2,32,1024]{3,2,1,0:T(8,128)(2,1)S(1)}, u32[]{:S(2)}, u32[]{:S(2)}) collective-permute-start(bf16[1,2,32,1024]{3,2,1,0:T(8,128)(2,1)} %slope.1.refs_0_), channel_id=1, source_target_pairs={{0,6},{1,7},{2,4},{3,5},{4,2},{5,3},{6,0},{7,1},{8,14},{9,15},{10,... | collective-permute-start | bytes 393224 | tf_op jit(solution)/shard_map/slope_share/ppermute | solution.py:432
  33.5 7.0 %collective-permute-start.3 = (bf16[1,2,32,1024]{3,2,1,0:T(8,128)(2,1)}, bf16[1,2,32,1024]{3,2,1,0:T(8,128)(2,1)S(1)}, u32[]{:S(2)}, u32[]{:S(2)}) collective-permute-start(bf16[1,2,32,1024]{3,2,1,0:T(8,128)(2,1)} %slope.1.refs_0_), channel_id=1, source_target_pairs={{0,4},{1,5},{2,6},{3,7},{4,0},{5,1},{6,2},{7,3},{8,12},{9,13},{10,... | collective-permute-start | bytes 393224 | tf_op jit(solution)/shard_map/slope_share/ppermute | solution.py:432
  34.7 5.8 %collective-permute-start.1 = (bf16[1,2,32,1024]{3,2,1,0:T(8,128)(2,1)}, bf16[1,2,32,1024]{3,2,1,0:T(8,128)(2,1)S(1)}, u32[]{:S(2)}, u32[]{:S(2)}) collective-permute-start(bf16[1,2,32,1024]{3,2,1,0:T(8,128)(2,1)} %slope.1.refs_0_), channel_id=1, source_target_pairs={{0,2},{1,3},{2,0},{3,1},{4,6},{5,7},{6,4},{7,5},{8,10},{9,11},{10,... | collective-permute-start | bytes 393224 | tf_op jit(solution)/shard_map/slope_share/ppermute | solution.py:432
  35.9 9.5 %collective-permute-start.6 = (bf16[1,2,32,1024]{3,2,1,0:T(8,128)(2,1)S(1)}, bf16[1,2,32,1024]{3,2,1,0:T(8,128)(2,1)S(1)}, u32[]{:S(2)}, u32[]{:S(2)}) collective-permute-start(bf16[1,2,32,1024]{3,2,1,0:T(8,128)(2,1)S(1)} %collective-permute-done.refs_1_), channel_id=1, source_target_pairs={{0,6},{1,7},{2,4},{3,5},{4,2},{5,3},{6,0},{7,1},{8,14},{9,15},{10,... | collective-permute-start | bytes 393224 | tf_op jit(solution)/shard_map/slope_share/ppermute | solution.py:432
  36.7 8.7 %collective-permute-start.4 = (bf16[1,2,32,1024]{3,2,1,0:T(8,128)(2,1)S(1)}, bf16[1,2,32,1024]{3,2,1,0:T(8,128)(2,1)S(1)}, u32[]{:S(2)}, u32[]{:S(2)}) collective-permute-start(bf16[1,2,32,1024]{3,2,1,0:T(8,128)(2,1)S(1)} %collective-permute-done.refs_1_), channel_id=1, source_target_pairs={{0,4},{1,5},{2,6},{3,7},{4,0},{5,1},{6,2},{7,3},{8,12},{9,13},{10,... | collective-permute-start | bytes 393224 | tf_op jit(solution)/shard_map/slope_share/ppermute | solution.py:432
  37.9 7.5 %collective-permute-start.2 = (bf16[1,2,32,1024]{3,2,1,0:T(8,128)(2,1)S(1)}, bf16[1,2,32,1024]{3,2,1,0:T(8,128)(2,1)S(1)}, u32[]{:S(2)}, u32[]{:S(2)}) collective-permute-start(bf16[1,2,32,1024]{3,2,1,0:T(8,128)(2,1)S(1)} %collective-permute-done.refs_1_), channel_id=1, source_target_pairs={{0,2},{1,3},{2,0},{3,1},{4,6},{5,7},{6,4},{7,5},{8,10},{9,11},{10,... | collective-permute-start | bytes 393224 | tf_op jit(solution)/shard_map/slope_share/ppermute | solution.py:432
  51.7 24.0 %copy-start.11 = (bf16[1,2,32,1024]{3,2,1,0:T(8,128)(2,1)S(1)}, bf16[1,2,32,1024]{3,2,1,0:T(8,128)(2,1)}, u32[]{:S(2)}) copy-start(bf16[1,2,32,1024]{3,2,1,0:T(8,128)(2,1)} %get-tuple-element.52) | copy-start | bytes 393220
  51.7 30.9 %copy-start.10 = (f32[2,32,1024]{2,1,0:T(8,128)S(1)}, f32[2,32,1024]{2,1,0:T(8,128)}, u32[]{:S(2)}) copy-start(f32[2,32,1024]{2,1,0:T(8,128)} %get-tuple-element.35) | copy-start | bytes 786436
  51.7 47.9 %copy-start.1 = (bf16[1024,512]{1,0:T(8,128)(2,1)S(1)}, bf16[1024,512]{1,0:T(8,128)(2,1)}, u32[]{:S(2)}) copy-start(bf16[1024,512]{1,0:T(8,128)(2,1)} %down_ref.3) | copy-start | bytes 3145732
  51.7 63.1 %all-to-all-start.2 = ((bf16[32,2,32,512]{3,2,1,0:T(8,128)(2,1)}), bf16[32,2,32,512]{3,2,1,0:T(8,128)(2,1)S(1)}, u32[]{:S(2)}, u32[]{:S(2)}) async-start(bf16[32,2,32,512]{3,2,1,0:T(8,128)(2,1)} %derivatives.2), calls=%async_computation.2 | async-start | bytes 4194304 | tf_op jit(solution)/shard_map/derivative_exchange/all_to_all | solution.py:515
  64.7 34.8 %copy-start.3 = (bf16[2,256,1024]{2,1,0:T(8,128)(2,1)S(1)}, bf16[2,256,1024]{2,1,0:T(8,128)(2,1)}, u32[]{:S(2)}) copy-start(bf16[2,256,1024]{2,1,0:T(8,128)(2,1)} %get-tuple-element.33.normed_ref) | copy-start | bytes 3145732
  64.7 5.8 %collective-permute-start.10 = (bf16[1,2,32,1024]{3,2,1,0:T(8,128)(2,1)}, bf16[1,2,32,1024]{3,2,1,0:T(8,128)(2,1)S(1)}, u32[]{:S(2)}, u32[]{:S(2)}) collective-permute-start(bf16[1,2,32,1024]{3,2,1,0:T(8,128)(2,1)} %get-tuple-element.53), channel_id=1, source_target_pairs={{0,2},{1,3},{2,0},{3,1},{4,6},{5,7},{6,4},{7,5},{8,10},{9,11},{10,... | collective-permute-start | bytes 393224 | tf_op jit(solution)/shard_map/mixed_exchange/ppermute | solution.py:432
  64.8 8.3 %collective-permute-start.11 = (bf16[1,2,32,1024]{3,2,1,0:T(8,128)(2,1)}, bf16[1,2,32,1024]{3,2,1,0:T(8,128)(2,1)S(1)}, u32[]{:S(2)}, u32[]{:S(2)}) collective-permute-start(bf16[1,2,32,1024]{3,2,1,0:T(8,128)(2,1)} %get-tuple-element.54), channel_id=1, source_target_pairs={{0,4},{1,5},{2,6},{3,7},{4,0},{5,1},{6,2},{7,3},{8,12},{9,13},{10,... | collective-permute-start | bytes 393224 | tf_op jit(solution)/shard_map/mixed_exchange/ppermute | solution.py:432
  66.7 9.0 %collective-permute-start.12 = (bf16[1,2,32,1024]{3,2,1,0:T(8,128)(2,1)}, bf16[1,2,32,1024]{3,2,1,0:T(8,128)(2,1)S(1)}, u32[]{:S(2)}, u32[]{:S(2)}) collective-permute-start(bf16[1,2,32,1024]{3,2,1,0:T(8,128)(2,1)} %get-tuple-element.55), channel_id=1, source_target_pairs={{0,6},{1,7},{2,4},{3,5},{4,2},{5,3},{6,0},{7,1},{8,14},{9,15},{10,... | collective-permute-start | bytes 393224 | tf_op jit(solution)/shard_map/mixed_exchange/ppermute | solution.py:432
  68.7 8.6 %collective-permute-start.7 = (bf16[1,2,32,1024]{3,2,1,0:T(8,128)(2,1)}, bf16[1,2,32,1024]{3,2,1,0:T(8,128)(2,1)S(1)}, u32[]{:S(2)}, u32[]{:S(2)}) collective-permute-start(bf16[1,2,32,1024]{3,2,1,0:T(8,128)(2,1)} %get-tuple-element.49), channel_id=1, source_target_pairs={{0,2},{1,3},{2,0},{3,1},{4,6},{5,7},{6,4},{7,5},{8,10},{9,11},{10,... | collective-permute-start | bytes 393224 | tf_op jit(solution)/shard_map/mixed_exchange/ppermute | solution.py:432
  68.7 10.1 %collective-permute-start.8 = (bf16[1,2,32,1024]{3,2,1,0:T(8,128)(2,1)}, bf16[1,2,32,1024]{3,2,1,0:T(8,128)(2,1)S(1)}, u32[]{:S(2)}, u32[]{:S(2)}) collective-permute-start(bf16[1,2,32,1024]{3,2,1,0:T(8,128)(2,1)} %get-tuple-element.50), channel_id=1, source_target_pairs={{0,4},{1,5},{2,6},{3,7},{4,0},{5,1},{6,2},{7,3},{8,12},{9,13},{10,... | collective-permute-start | bytes 393224 | tf_op jit(solution)/shard_map/mixed_exchange/ppermute | solution.py:432
  70.5 10.7 %collective-permute-start.9 = (bf16[1,2,32,1024]{3,2,1,0:T(8,128)(2,1)}, bf16[1,2,32,1024]{3,2,1,0:T(8,128)(2,1)S(1)}, u32[]{:S(2)}, u32[]{:S(2)}) collective-permute-start(bf16[1,2,32,1024]{3,2,1,0:T(8,128)(2,1)} %get-tuple-element.51), channel_id=1, source_target_pairs={{0,6},{1,7},{2,4},{3,5},{4,2},{5,3},{6,0},{7,1},{8,14},{9,15},{10,... | collective-permute-start | bytes 393224 | tf_op jit(solution)/shard_map/mixed_exchange/ppermute | solution.py:432
  75.7 6.9 %collective-permute-start.13 = (bf16[1,2,32,1024]{3,2,1,0:T(8,128)(2,1)S(1)}, bf16[1,2,32,1024]{3,2,1,0:T(8,128)(2,1)S(1)}, u32[]{:S(2)}, u32[]{:S(2)}) collective-permute-start(bf16[1,2,32,1024]{3,2,1,0:T(8,128)(2,1)S(1)} %add_convert_fusion), channel_id=1, source_target_pairs={{0,1},{1,0},{2,3},{3,2},{4,5},{5,4},{6,7},{7,6},{8,9},{9,8},{10,11... | collective-permute-start | bytes 393224 | tf_op jit(solution)/shard_map/mixed_exchange/ppermute | solution.py:432
  83.6 5.8 %collective-permute-start.14 = (bf16[1,2,32,1024]{3,2,1,0:T(8,128)(2,1)S(1)}, bf16[1,2,32,1024]{3,2,1,0:T(8,128)(2,1)S(1)}, u32[]{:S(2)}, u32[]{:S(2)}) collective-permute-start(bf16[1,2,32,1024]{3,2,1,0:T(8,128)(2,1)S(1)} %fusion.6.refs_0_), channel_id=1, source_target_pairs={{0,1},{1,0},{2,3},{3,2},{4,5},{5,4},{6,7},{7,6},{8,9},{9,8},{10,11... | collective-permute-start | bytes 393224 | tf_op jit(solution)/shard_map/slope_share/ppermute | solution.py:432
  86.2 7.4 %collective-permute-start.19 = (bf16[1,2,32,1024]{3,2,1,0:T(8,128)(2,1)S(1)}, bf16[1,2,32,1024]{3,2,1,0:T(8,128)(2,1)S(1)}, u32[]{:S(2)}, u32[]{:S(2)}) collective-permute-start(bf16[1,2,32,1024]{3,2,1,0:T(8,128)(2,1)S(1)} %fusion.6.refs_0_), channel_id=1, source_target_pairs={{0,6},{1,7},{2,4},{3,5},{4,2},{5,3},{6,0},{7,1},{8,14},{9,15},{10,... | collective-permute-start | bytes 393224 | tf_op jit(solution)/shard_map/slope_share/ppermute | solution.py:432
  86.5 7.1 %collective-permute-start.17 = (bf16[1,2,32,1024]{3,2,1,0:T(8,128)(2,1)S(1)}, bf16[1,2,32,1024]{3,2,1,0:T(8,128)(2,1)S(1)}, u32[]{:S(2)}, u32[]{:S(2)}) collective-permute-start(bf16[1,2,32,1024]{3,2,1,0:T(8,128)(2,1)S(1)} %fusion.6.refs_0_), channel_id=1, source_target_pairs={{0,4},{1,5},{2,6},{3,7},{4,0},{5,1},{6,2},{7,3},{8,12},{9,13},{10,... | collective-permute-start | bytes 393224 | tf_op jit(solution)/shard_map/slope_share/ppermute | solution.py:432
  86.6 7.3 %collective-permute-start.15 = (bf16[1,2,32,1024]{3,2,1,0:T(8,128)(2,1)S(1)}, bf16[1,2,32,1024]{3,2,1,0:T(8,128)(2,1)S(1)}, u32[]{:S(2)}, u32[]{:S(2)}) collective-permute-start(bf16[1,2,32,1024]{3,2,1,0:T(8,128)(2,1)S(1)} %fusion.6.refs_0_), channel_id=1, source_target_pairs={{0,2},{1,3},{2,0},{3,1},{4,6},{5,7},{6,4},{7,5},{8,10},{9,11},{10,... | collective-permute-start | bytes 393224 | tf_op jit(solution)/shard_map/slope_share/ppermute | solution.py:432
  89.5 9.7 %collective-permute-start.20 = (bf16[1,2,32,1024]{3,2,1,0:T(8,128)(2,1)S(1)}, bf16[1,2,32,1024]{3,2,1,0:T(8,128)(2,1)S(1)}, u32[]{:S(2)}, u32[]{:S(2)}) collective-permute-start(bf16[1,2,32,1024]{3,2,1,0:T(8,128)(2,1)S(1)} %collective-permute-done.14.refs_1_), channel_id=1, source_target_pairs={{0,6},{1,7},{2,4},{3,5},{4,2},{5,3},{6,0},{7,1},{8,14},{9,15},{10,... | collective-permute-start | bytes 393224 | tf_op jit(solution)/shard_map/slope_share/ppermute | solution.py:432
  90.7 8.5 %collective-permute-start.18 = (bf16[1,2,32,1024]{3,2,1,0:T(8,128)(2,1)S(1)}, bf16[1,2,32,1024]{3,2,1,0:T(8,128)(2,1)S(1)}, u32[]{:S(2)}, u32[]{:S(2)}) collective-permute-start(bf16[1,2,32,1024]{3,2,1,0:T(8,128)(2,1)S(1)} %collective-permute-done.14.refs_1_), channel_id=1, source_target_pairs={{0,4},{1,5},{2,6},{3,7},{4,0},{5,1},{6,2},{7,3},{8,12},{9,13},{10,... | collective-permute-start | bytes 393224 | tf_op jit(solution)/shard_map/slope_share/ppermute | solution.py:432
  93.6 6.0 %collective-permute-start.16 = (bf16[1,2,32,1024]{3,2,1,0:T(8,128)(2,1)S(1)}, bf16[1,2,32,1024]{3,2,1,0:T(8,128)(2,1)S(1)}, u32[]{:S(2)}, u32[]{:S(2)}) collective-permute-start(bf16[1,2,32,1024]{3,2,1,0:T(8,128)(2,1)S(1)} %collective-permute-done.14.refs_1_), channel_id=1, source_target_pairs={{0,2},{1,3},{2,0},{3,1},{4,6},{5,7},{6,4},{7,5},{8,10},{9,11},{10,... | collective-permute-start | bytes 393224 | tf_op jit(solution)/shard_map/slope_share/ppermute | solution.py:432
  114.8 55.0 %all-to-all-start.1 = ((bf16[32,2,32,512]{3,2,1,0:T(8,128)(2,1)}), bf16[32,2,32,512]{3,2,1,0:T(8,128)(2,1)}, u32[]{:S(2)}, u32[]{:S(2)}) async-start(bf16[32,2,32,512]{3,2,1,0:T(8,128)(2,1)} %derivatives.3), calls=%async_computation.1 | async-start | bytes 4194304 | tf_op jit(solution)/shard_map/derivative_exchange/all_to_all | solution.py:515
  197.7 12.7 %all-to-all-start.5 = ((f32[16,8,128]{2,1,0:T(8,128)}), f32[16,8,128]{2,1,0:T(8,128)S(1)}, u32[]{:S(2)}, u32[]{:S(2)}) async-start(f32[16,8,128]{2,1,0:T(8,128)} %broadcast_in_dim.18), calls=%async_computation.5 | async-start | bytes 131072 | tf_op jit(solution)/shard_map/gram_sum/all_to_all | solution.py:38
  (13 other events, 64.8 us)

commit v7 on v6

--- a/solution.py
+++ b/solution.py
@@ -314,11 +314,13 @@
     chunk_count = (len(refs) - 4) // 2
     far_refs, out_ref, gram_ref, spread_ref = refs[:chunk_count], *refs[chunk_count : chunk_count + 3]
     chunk_refs, sems = refs[chunk_count + 3 : -1], refs[-1]
-    copies = [
-        pltpu.make_async_copy(far, near, sems.at[n])
+    copies = {
+        (n, r, f): pltpu.make_async_copy(far.at[r, f], near.at[r, f], sems.at[n, r, f])
         for n, (far, near) in enumerate(zip(far_refs, chunk_refs))
-    ]
-    for copy in copies:
+        for r in range(near.shape[0])
+        for f in range(near.shape[1])
+    }
+    for copy in copies.values():
         copy.start()
     count = gram_ref.shape[0]
     gram_rows = shared_ref.shape[1]
@@ -368,9 +370,10 @@
     lanes = spread_ref.shape[1]
     first = 0
     for n, chunk_ref in enumerate(chunk_refs):
-        copies[n].wait()
         steps, groups, depth, _ = chunk_ref.shape
         for r in range(steps):
+            for f in range(groups):
+                copies[n, r, f].wait()
             here = slice(r * STEP, (r + 1) * STEP)
 
             def add(s, total):
@@ -400,7 +403,7 @@
             pltpu.VMEM((count, LANES), jnp.float32),
         ]
         + [pltpu.VMEM(c.shape, c.dtype) for c in chunks]
-        + [pltpu.SemaphoreType.DMA((len(chunks),))],
+        + [pltpu.SemaphoreType.DMA((len(chunks),) + chunks[0].shape[:2])],
         compiler_params=pltpu.CompilerParams(vmem_limit_bytes=VMEM_LIMIT),
     )(scalars, shared, *chunks)
 

time: 217 us -> 217 us (level)
  no operation moved by 1% of the time
where the time goes in v7:
time: 217 us; the launch traced here: 216 us
  waiting for transfers between devices  95.2 us (44%)
  starting transfers between devices  54.8 us (25%)
  Pallas kernels  34.3 us (16%)
  blocking collectives  21.5 us (10%)
  local copies, waits for them, and re-layouts  5.85 us (3%)
  other arithmetic  3.01 us (1%)
    all_to_all x2, waiting for transfers between devices, body(): chunks = [lax.all_to_all(c, SAMPLES, 0, 0) for c in coded_chunks]  55.3 us
    ppermute x21, starting transfers between devices, partner(): return lax.ppermute(array, MP, [(i, i ^ k) for i in range(mp_size)])  24.5 us
    ppermute x21, waiting for transfers between devices, partner(): return lax.ppermute(array, MP, [(i, i ^ k) for i in range(mp_size)])  22.9 us
    all_to_all x2, starting transfers between devices, body(): chunks = [lax.all_to_all(c, SAMPLES, 0, 0) for c in coded_chunks]  17.9 us
    all_to_all x1, blocking collectives, body(): lax.all_to_all(gram_part.reshape(near_size, sample_count // near_size, sa...  11.9 us
    pallas_call x2, Pallas kernels, forward(): pl.pallas_call(functools.partial(forward_kernel, first, pairs), grid=(sam...  10.7 us
    all_to_all x1, waiting for transfers between devices, body(): mixed_parts = lax.all_to_all(parts[0], MP, 0, 0)  10.5 us
    all_to_all x1, blocking collectives, share(): lax.all_to_all(jnp.broadcast_to(array, (size,) + array.shape), axis, 0, 0)  9.53 us
  transfers between devices with their start and end apart: 25, of which 15 were waited for; matrix products, arithmetic and copies ran while one was open for 2% of the time, Pallas kernels for 5%

profile of v7, /device:TPU:1, one launch (start us, length us, event | category | flops | bytes accessed | tf_op | source)
XLA Modules:
  0.0 216.4 jit_solution(11370268575817014385)
XLA Ops:
  0.0 5.2 %forward.3 = (bf16[2,256,1024]{2,1,0:T(8,128)(2,1)}, f32[2,256,512]{2,1,0:T(8,128)}, bf16[8,2,32,1024]{3,2,1,0:T(8,128)(2,1)}) custom-call(s32[4,256]{1,0:T(4,128)} %spin_ref.1, bf16[4,8,32,1024]{3,2,1,0:T(8,128)(2,1)} %bitcast.26, bf16[1024]{0:T(1024)(128)(2,1)} %embed_ref.1, bf16[1024]{0:T(1024)(128)(2,1)} %refs_3_.3, bf16[1024,512]{1,0:T(8,128)(2,1)} %refs_4_.3, ...), custom_call_target="tpu_custom_call" | custom-call | tf_op jit(solution)/shard_map/forward/pallas_call | solution.py:107
  5.2 7.5 %all-to-all-start = ((bf16[8,2,32,1024]{3,2,1,0:T(8,128)(2,1)}), bf16[8,2,32,1024]{3,2,1,0:T(8,128)(2,1)S(1)}, u32[]{:S(2)}, u32[]{:S(2)}) async-start(bf16[8,2,32,1024]{3,2,1,0:T(8,128)(2,1)} %get-tuple-element.46), calls=%async_computation | async-start | bytes 2097152 | tf_op jit(solution)/shard_map/mixed_exchange/all_to_all | solution.py:475
  12.7 5.4 %forward.2 = (bf16[2,256,1024]{2,1,0:T(8,128)(2,1)}, f32[2,256,512]{2,1,0:T(8,128)}, f32[2,32,1024]{2,1,0:T(8,128)}, f32[8,128]{1,0:T(8,128)}, bf16[1,2,32,1024]...) custom-call(s32[1]{0:T(128)} %bitcast.3.refs_0_.own_ref.order_ref, ...), custom_call_target="tpu_custom_call" | custom-call | tf_op jit(solution)/shard_map/forward/pallas_call | solution.py:107
  18.2 10.5 %all-to-all-done.part_ref = bf16[8,2,32,1024]{3,2,1,0:T(8,128)(2,1)S(1)} async-done(((bf16[8,2,32,1024]{3,2,1,0:T(8,128)(2,1)}), bf16[8,2,32,1024]{3,2,1,0:T(8,128)(2,1)S(1)}, u32[]{:S(2)}, u32[]{:S(2)}) %all-to-all-start) | async-done | bytes 1048608 | tf_op jit(solution)/shard_map/mixed_exchange/all_to_all | solution.py:475
  31.1 2.4 %collective-permute-start.5 = (bf16[1,2,32,1024]{3,2,1,0:T(8,128)(2,1)}, bf16[1,2,32,1024]{3,2,1,0:T(8,128)(2,1)S(1)}, u32[]{:S(2)}, u32[]{:S(2)}) collective-permute-start(bf16[1,2,32,1024]{3,2,1,0:T(8,128)(2,1)} %slope.1.refs_0_), channel_id=1, source_target_pairs={{0,6},{1,7},{2,4},{3,5},{4,2},{5,3},{6,0},{7,1},{8,14},{9,15},{10,... | collective-permute-start | bytes 393224 | tf_op jit(solution)/shard_map/slope_share/ppermute | solution.py:435
  40.5 4.9 %collective-permute-done.6.refs_7_ = bf16[1,2,32,1024]{3,2,1,0:T(8,128)(2,1)S(1)} collective-permute-done((bf16[1,2,32,1024]{3,2,1,0:T(8,128)(2,1)S(1)}, bf16[1,2,32,1024]{3,2,1,0:T(8,128)(2,1)S(1)}, u32[]{:S(2)}, u32[]{:S(2)}) %collective-permute-start.6) | collective-permute-done | bytes 131104 | tf_op jit(solution)/shard_map/slope_share/ppermute | solution.py:435
  46.2 5.4 %derivatives.2 = bf16[32,2,32,512]{3,2,1,0:T(8,128)(2,1)} custom-call(s32[1]{0:T(128)} %bitcast.3.refs_0_.own_ref.order_ref, f32[1]{0:T(128)S(6)} %div.4.scale_ref, bf16[2,256,1024]{2,1,0:T(8,128)(2,1)} %get-tuple-element.44.normed_ref, f32[2,256,512]{2,1,0:T(8,128)} %get-tuple-element.45.bend_ref, bf16[1024,512]{1,0:T(8,128)(2,1)} %down_ref.3, ...), custom_call_target="tpu_custom_call" | custom-call | tf_op jit(solution)/shard_map/derivatives/pallas_call | solution.py:189
  51.7 13.0 %all-to-all-start.2 = ((bf16[32,2,32,512]{3,2,1,0:T(8,128)(2,1)}), bf16[32,2,32,512]{3,2,1,0:T(8,128)(2,1)S(1)}, u32[]{:S(2)}, u32[]{:S(2)}) async-start(bf16[32,2,32,512]{3,2,1,0:T(8,128)(2,1)} %derivatives.2), calls=%async_computation.2 | async-start | bytes 4194304 | tf_op jit(solution)/shard_map/derivative_exchange/all_to_all | solution.py:518
  64.8 1.8 collective-permute-start.11
  66.7 2.0 collective-permute-start.12
  68.7 1.8 collective-permute-start.8
  70.5 2.0 collective-permute-start.9
  73.1 2.5 %collective-permute-done.12 = bf16[1,2,32,1024]{3,2,1,0:T(8,128)(2,1)S(1)} collective-permute-done((bf16[1,2,32,1024]{3,2,1,0:T(8,128)(2,1)}, bf16[1,2,32,1024]{3,2,1,0:T(8,128)(2,1)S(1)}, u32[]{:S(2)}, u32[]{:S(2)}) %collective-permute-start.12) | collective-permute-done | bytes 131104 | tf_op jit(solution)/shard_map/mixed_exchange/ppermute | solution.py:435
  75.7 1.6 collective-permute-start.13
  77.3 1.5 collective-permute-done.8
  78.8 2.5 %collective-permute-done.9 = bf16[1,2,32,1024]{3,2,1,0:T(8,128)(2,1)S(1)} collective-permute-done((bf16[1,2,32,1024]{3,2,1,0:T(8,128)(2,1)}, bf16[1,2,32,1024]{3,2,1,0:T(8,128)(2,1)S(1)}, u32[]{:S(2)}, u32[]{:S(2)}) %collective-permute-start.9) | collective-permute-done | bytes 131104 | tf_op jit(solution)/shard_map/mixed_exchange/ppermute | solution.py:435
  83.6 2.6 %collective-permute-start.14 = (bf16[1,2,32,1024]{3,2,1,0:T(8,128)(2,1)S(1)}, bf16[1,2,32,1024]{3,2,1,0:T(8,128)(2,1)S(1)}, u32[]{:S(2)}, u32[]{:S(2)}) collective-permute-start(bf16[1,2,32,1024]{3,2,1,0:T(8,128)(2,1)S(1)} %fusion.6.refs_0_), channel_id=1, source_target_pairs={{0,1},{1,0},{2,3},{3,2},{4,5},{5,4},{6,7},{7,6},{8,9},{9,8},{10,11... | collective-permute-start | bytes 393224 | tf_op jit(solution)/shard_map/slope_share/ppermute | solution.py:435
  86.6 2.9 %collective-permute-start.15 = (bf16[1,2,32,1024]{3,2,1,0:T(8,128)(2,1)S(1)}, bf16[1,2,32,1024]{3,2,1,0:T(8,128)(2,1)S(1)}, u32[]{:S(2)}, u32[]{:S(2)}) collective-permute-start(bf16[1,2,32,1024]{3,2,1,0:T(8,128)(2,1)S(1)} %fusion.6.refs_0_), channel_id=1, source_target_pairs={{0,2},{1,3},{2,0},{3,1},{4,6},{5,7},{6,4},{7,5},{8,10},{9,11},{10,... | collective-permute-start | bytes 393224 | tf_op jit(solution)/shard_map/slope_share/ppermute | solution.py:435
  91.2 2.3 %collective-permute-done.19.refs_6_ = bf16[1,2,32,1024]{3,2,1,0:T(8,128)(2,1)S(1)} collective-permute-done((bf16[1,2,32,1024]{3,2,1,0:T(8,128)(2,1)S(1)}, bf16[1,2,32,1024]{3,2,1,0:T(8,128)(2,1)S(1)}, u32[]{:S(2)}, u32[]{:S(2)}) %collective-permute-start.19) | collective-permute-done | bytes 131104 | tf_op jit(solution)/shard_map/slope_share/ppermute | solution.py:435
  93.9 5.3 %collective-permute-done.20.refs_7_ = bf16[1,2,32,1024]{3,2,1,0:T(8,128)(2,1)S(1)} collective-permute-done((bf16[1,2,32,1024]{3,2,1,0:T(8,128)(2,1)S(1)}, bf16[1,2,32,1024]{3,2,1,0:T(8,128)(2,1)S(1)}, u32[]{:S(2)}, u32[]{:S(2)}) %collective-permute-start.20) | collective-permute-done | bytes 131104 | tf_op jit(solution)/shard_map/slope_share/ppermute | solution.py:435
  100.8 3.3 %derivatives.3 = bf16[32,2,32,512]{3,2,1,0:T(8,128)(2,1)} custom-call(s32[1]{0:T(128)} %constant.41.clone.1.order_ref, f32[1]{0:T(128)S(6)} %div.4.scale_ref, bf16[2,256,1024]{2,1,0:T(8,128)(2,1)S(1)} %copy-done.3, f32[2,256,512]{2,1,0:T(8,128)S(1)} %copy-done.4, bf16[1024,512]{1,0:T(8,128)(2,1)S(1)} %copy-done.1, ...), custom_call_target="tpu_custom_call" | custom-call | tf_op jit(solution)/shard_map/derivatives/pallas_call | solution.py:189
  104.1 10.7 %all-to-all-done.2 = bf16[32,2,32,512]{3,2,1,0:T(8,128)(2,1)S(1)} async-done(((bf16[32,2,32,512]{3,2,1,0:T(8,128)(2,1)}), bf16[32,2,32,512]{3,2,1,0:T(8,128)(2,1)S(1)}, u32[]{:S(2)}, u32[]{:S(2)}) %all-to-all-start.2) | async-done | bytes 2097184 | tf_op jit(solution)/shard_map/derivative_exchange/all_to_all | solution.py:518
  114.8 4.9 %all-to-all-start.1 = ((bf16[32,2,32,512]{3,2,1,0:T(8,128)(2,1)}), bf16[32,2,32,512]{3,2,1,0:T(8,128)(2,1)}, u32[]{:S(2)}, u32[]{:S(2)}) async-start(bf16[32,2,32,512]{3,2,1,0:T(8,128)(2,1)} %derivatives.3), calls=%async_computation.1 | async-start | bytes 4194304 | tf_op jit(solution)/shard_map/derivative_exchange/all_to_all | solution.py:518
  120.8 2.9 %gram.2 = (bf16[32,64,512]{2,1,0:T(8,128)(2,1)S(1)}, f32[2,4,1024,128]{3,2,1,0:T(8,128)}) custom-call(bf16[64,32,512]{2,1,0:T(8,128)(2,1)S(1)} %bitcast.29), custom_call_target="tpu_custom_call" | custom-call | tf_op jit(solution)/shard_map/gram/pallas_call | solution.py:252
  123.8 1.4 copy-done.2
  125.2 44.6 %all-to-all-done.1 = bf16[32,2,32,512]{3,2,1,0:T(8,128)(2,1)} async-done(((bf16[32,2,32,512]{3,2,1,0:T(8,128)(2,1)}), bf16[32,2,32,512]{3,2,1,0:T(8,128)(2,1)}, u32[]{:S(2)}, u32[]{:S(2)}) %all-to-all-start.1) | async-done | bytes 2097184 | tf_op jit(solution)/shard_map/derivative_exchange/all_to_all | solution.py:518
  169.8 5.7 %gram.3 = (f32[128,128]{1,0:T(8,128)}, f32[2,4,1024,128]{3,2,1,0:T(8,128)}) custom-call(f32[1,128]{1,0:T(1,128)} %broadcast_select_fusion.energy_ref, bf16[64,32,512]{2,1,0:T(8,128)(2,1)} %bitcast.6.code_ref, bf16[32,64,512]{2,1,0:T(8,128)(2,1)} %copy-done.2), custom_call_target="tpu_custom_call" | custom-call | tf_op jit(solution)/shard_map/gram/pallas_call | solution.py:298
  175.5 11.9 %all_to_all.30 = f32[16,8,128]{2,1,0:T(8,128)S(1)} all-to-all(f32[16,8,128]{2,1,0:T(8,128)} %bitcast.30), channel_id=1, replica_groups=mesh['z'=8,'x_lo'=2,'core'=2,'y'=4,'x_hi'=2] {'z','core'}, dimensions={0} | all-to-all | bytes 131072 | tf_op jit(solution)/shard_map/gram_sum/all_to_all | solution.py:526
  187.5 9.5 %all_to_all.31 = f32[16,8,128]{2,1,0:T(8,128)S(1)} all-to-all(f32[16,8,128]{2,1,0:T(8,128)S(1)} %broadcast_in_dim.17), channel_id=1, replica_groups=mesh['z'=8,'x_lo'=2,'core'=2,'y'=4,'x_hi'=2] {'x_lo','y','x_hi'}, dimensions={0} | all-to-all | bytes 131072 | tf_op jit(solution)/shard_map/gram_sum/all_to_all | solution.py:38
  197.7 4.9 %all-to-all-start.5 = ((f32[16,8,128]{2,1,0:T(8,128)}), f32[16,8,128]{2,1,0:T(8,128)S(1)}, u32[]{:S(2)}, u32[]{:S(2)}) async-start(f32[16,8,128]{2,1,0:T(8,128)} %broadcast_in_dim.18), calls=%async_computation.5 | async-start | bytes 131072 | tf_op jit(solution)/shard_map/gram_sum/all_to_all | solution.py:38
  203.9 6.5 %all-to-all-done.5.shared_ref = f32[16,8,128]{2,1,0:T(8,128)S(1)} async-done(((f32[16,8,128]{2,1,0:T(8,128)}), f32[16,8,128]{2,1,0:T(8,128)S(1)}, u32[]{:S(2)}, u32[]{:S(2)}) %all-to-all-start.5) | async-done | bytes 65568 | tf_op jit(solution)/shard_map/gram_sum/all_to_all | solution.py:38
  211.0 5.2 %solve.1 = f32[32,512]{1,0:T(8,128)} custom-call(f32[2]{0:T(128)} %pad_maximum_fusion.scalar_ref, f32[16,8,128]{2,1,0:T(8,128)} %copy-done.9, f32[2,4,1024,128]{3,2,1,0:T(8,128)} %get-tuple-element.59.refs_0_, f32[2,4,1024,128]{3,2,1,0:T(8,128)} %get-tuple-element.60.refs_1_), custom_call_target="tpu_custom_call" | custom-call | tf_op jit(solution)/shard_map/solve/pallas_call | solution.py:396
  (82 shorter events, 19.7 us)
Async XLA Ops:
  5.2 23.5 %all-to-all-start = ((bf16[8,2,32,1024]{3,2,1,0:T(8,128)(2,1)}), bf16[8,2,32,1024]{3,2,1,0:T(8,128)(2,1)S(1)}, u32[]{:S(2)}, u32[]{:S(2)}) async-start(bf16[8,2,32,1024]{3,2,1,0:T(8,128)(2,1)} %get-tuple-element.46), calls=%async_computation | async-start | bytes 2097152 | tf_op jit(solution)/shard_map/mixed_exchange/all_to_all | solution.py:475
  12.7 16.0 %copy-start = (bf16[4,256,1024]{2,1,0:T(8,128)(2,1)S(1)}, bf16[4,256,1024]{2,1,0:T(8,128)(2,1)}, u32[]{:S(2)}) copy-start(bf16[4,256,1024]{2,1,0:T(8,128)(2,1)} %param.10) | copy-start | bytes 6291460
  12.7 16.0 %copy-start.5 = (s32[4,256]{1,0:T(4,128)S(1)}, s32[4,256]{1,0:T(4,128)}, u32[]{:S(2)}) copy-start(s32[4,256]{1,0:T(4,128)} %spin_ref.1) | copy-start | bytes 12292
  12.7 16.0 %copy-start.6 = (bf16[1024]{0:T(1024)(128)(2,1)S(1)}, bf16[1024]{0:T(1024)(128)(2,1)}, u32[]{:S(2)}) copy-start(bf16[1024]{0:T(1024)(128)(2,1)} %embed_ref.1) | copy-start | bytes 6148
  30.4 5.5 %collective-permute-start = (bf16[1,2,32,1024]{3,2,1,0:T(8,128)(2,1)}, bf16[1,2,32,1024]{3,2,1,0:T(8,128)(2,1)S(1)}, u32[]{:S(2)}, u32[]{:S(2)}) collective-permute-start(bf16[1,2,32,1024]{3,2,1,0:T(8,128)(2,1)} %slope.1.refs_0_), channel_id=1, source_target_pairs={{0,1},{1,0},{2,3},{3,2},{4,5},{5,4},{6,7},{7,6},{8,9},{9,8},{10,11... | collective-permute-start | bytes 393224 | tf_op jit(solution)/shard_map/slope_share/ppermute | solution.py:435
  31.1 6.8 %collective-permute-start.5 = (bf16[1,2,32,1024]{3,2,1,0:T(8,128)(2,1)}, bf16[1,2,32,1024]{3,2,1,0:T(8,128)(2,1)S(1)}, u32[]{:S(2)}, u32[]{:S(2)}) collective-permute-start(bf16[1,2,32,1024]{3,2,1,0:T(8,128)(2,1)} %slope.1.refs_0_), channel_id=1, source_target_pairs={{0,6},{1,7},{2,4},{3,5},{4,2},{5,3},{6,0},{7,1},{8,14},{9,15},{10,... | collective-permute-start | bytes 393224 | tf_op jit(solution)/shard_map/slope_share/ppermute | solution.py:435
  33.5 7.0 %collective-permute-start.3 = (bf16[1,2,32,1024]{3,2,1,0:T(8,128)(2,1)}, bf16[1,2,32,1024]{3,2,1,0:T(8,128)(2,1)S(1)}, u32[]{:S(2)}, u32[]{:S(2)}) collective-permute-start(bf16[1,2,32,1024]{3,2,1,0:T(8,128)(2,1)} %slope.1.refs_0_), channel_id=1, source_target_pairs={{0,4},{1,5},{2,6},{3,7},{4,0},{5,1},{6,2},{7,3},{8,12},{9,13},{10,... | collective-permute-start | bytes 393224 | tf_op jit(solution)/shard_map/slope_share/ppermute | solution.py:435
  34.7 5.8 %collective-permute-start.1 = (bf16[1,2,32,1024]{3,2,1,0:T(8,128)(2,1)}, bf16[1,2,32,1024]{3,2,1,0:T(8,128)(2,1)S(1)}, u32[]{:S(2)}, u32[]{:S(2)}) collective-permute-start(bf16[1,2,32,1024]{3,2,1,0:T(8,128)(2,1)} %slope.1.refs_0_), channel_id=1, source_target_pairs={{0,2},{1,3},{2,0},{3,1},{4,6},{5,7},{6,4},{7,5},{8,10},{9,11},{10,... | collective-permute-start | bytes 393224 | tf_op jit(solution)/shard_map/slope_share/ppermute | solution.py:435
  35.9 9.5 %collective-permute-start.6 = (bf16[1,2,32,1024]{3,2,1,0:T(8,128)(2,1)S(1)}, bf16[1,2,32,1024]{3,2,1,0:T(8,128)(2,1)S(1)}, u32[]{:S(2)}, u32[]{:S(2)}) collective-permute-start(bf16[1,2,32,1024]{3,2,1,0:T(8,128)(2,1)S(1)} %collective-permute-done.refs_1_), channel_id=1, source_target_pairs={{0,6},{1,7},{2,4},{3,5},{4,2},{5,3},{6,0},{7,1},{8,14},{9,15},{10,... | collective-permute-start | bytes 393224 | tf_op jit(solution)/shard_map/slope_share/ppermute | solution.py:435
  36.7 8.7 %collective-permute-start.4 = (bf16[1,2,32,1024]{3,2,1,0:T(8,128)(2,1)S(1)}, bf16[1,2,32,1024]{3,2,1,0:T(8,128)(2,1)S(1)}, u32[]{:S(2)}, u32[]{:S(2)}) collective-permute-start(bf16[1,2,32,1024]{3,2,1,0:T(8,128)(2,1)S(1)} %collective-permute-done.refs_1_), channel_id=1, source_target_pairs={{0,4},{1,5},{2,6},{3,7},{4,0},{5,1},{6,2},{7,3},{8,12},{9,13},{10,... | collective-permute-start | bytes 393224 | tf_op jit(solution)/shard_map/slope_share/ppermute | solution.py:435
  37.9 7.5 %collective-permute-start.2 = (bf16[1,2,32,1024]{3,2,1,0:T(8,128)(2,1)S(1)}, bf16[1,2,32,1024]{3,2,1,0:T(8,128)(2,1)S(1)}, u32[]{:S(2)}, u32[]{:S(2)}) collective-permute-start(bf16[1,2,32,1024]{3,2,1,0:T(8,128)(2,1)S(1)} %collective-permute-done.refs_1_), channel_id=1, source_target_pairs={{0,2},{1,3},{2,0},{3,1},{4,6},{5,7},{6,4},{7,5},{8,10},{9,11},{10,... | collective-permute-start | bytes 393224 | tf_op jit(solution)/shard_map/slope_share/ppermute | solution.py:435
  51.7 24.0 %copy-start.11 = (bf16[1,2,32,1024]{3,2,1,0:T(8,128)(2,1)S(1)}, bf16[1,2,32,1024]{3,2,1,0:T(8,128)(2,1)}, u32[]{:S(2)}) copy-start(bf16[1,2,32,1024]{3,2,1,0:T(8,128)(2,1)} %get-tuple-element.52) | copy-start | bytes 393220
  51.7 30.9 %copy-start.10 = (f32[2,32,1024]{2,1,0:T(8,128)S(1)}, f32[2,32,1024]{2,1,0:T(8,128)}, u32[]{:S(2)}) copy-start(f32[2,32,1024]{2,1,0:T(8,128)} %get-tuple-element.35) | copy-start | bytes 786436
  51.7 47.9 %copy-start.1 = (bf16[1024,512]{1,0:T(8,128)(2,1)S(1)}, bf16[1024,512]{1,0:T(8,128)(2,1)}, u32[]{:S(2)}) copy-start(bf16[1024,512]{1,0:T(8,128)(2,1)} %down_ref.3) | copy-start | bytes 3145732
  51.7 63.1 %all-to-all-start.2 = ((bf16[32,2,32,512]{3,2,1,0:T(8,128)(2,1)}), bf16[32,2,32,512]{3,2,1,0:T(8,128)(2,1)S(1)}, u32[]{:S(2)}, u32[]{:S(2)}) async-start(bf16[32,2,32,512]{3,2,1,0:T(8,128)(2,1)} %derivatives.2), calls=%async_computation.2 | async-start | bytes 4194304 | tf_op jit(solution)/shard_map/derivative_exchange/all_to_all | solution.py:518
  64.7 34.8 %copy-start.3 = (bf16[2,256,1024]{2,1,0:T(8,128)(2,1)S(1)}, bf16[2,256,1024]{2,1,0:T(8,128)(2,1)}, u32[]{:S(2)}) copy-start(bf16[2,256,1024]{2,1,0:T(8,128)(2,1)} %get-tuple-element.33.normed_ref) | copy-start | bytes 3145732
  64.7 5.8 %collective-permute-start.10 = (bf16[1,2,32,1024]{3,2,1,0:T(8,128)(2,1)}, bf16[1,2,32,1024]{3,2,1,0:T(8,128)(2,1)S(1)}, u32[]{:S(2)}, u32[]{:S(2)}) collective-permute-start(bf16[1,2,32,1024]{3,2,1,0:T(8,128)(2,1)} %get-tuple-element.53), channel_id=1, source_target_pairs={{0,2},{1,3},{2,0},{3,1},{4,6},{5,7},{6,4},{7,5},{8,10},{9,11},{10,... | collective-permute-start | bytes 393224 | tf_op jit(solution)/shard_map/mixed_exchange/ppermute | solution.py:435
  64.8 8.3 %collective-permute-start.11 = (bf16[1,2,32,1024]{3,2,1,0:T(8,128)(2,1)}, bf16[1,2,32,1024]{3,2,1,0:T(8,128)(2,1)S(1)}, u32[]{:S(2)}, u32[]{:S(2)}) collective-permute-start(bf16[1,2,32,1024]{3,2,1,0:T(8,128)(2,1)} %get-tuple-element.54), channel_id=1, source_target_pairs={{0,4},{1,5},{2,6},{3,7},{4,0},{5,1},{6,2},{7,3},{8,12},{9,13},{10,... | collective-permute-start | bytes 393224 | tf_op jit(solution)/shard_map/mixed_exchange/ppermute | solution.py:435
  66.7 9.0 %collective-permute-start.12 = (bf16[1,2,32,1024]{3,2,1,0:T(8,128)(2,1)}, bf16[1,2,32,1024]{3,2,1,0:T(8,128)(2,1)S(1)}, u32[]{:S(2)}, u32[]{:S(2)}) collective-permute-start(bf16[1,2,32,1024]{3,2,1,0:T(8,128)(2,1)} %get-tuple-element.55), channel_id=1, source_target_pairs={{0,6},{1,7},{2,4},{3,5},{4,2},{5,3},{6,0},{7,1},{8,14},{9,15},{10,... | collective-permute-start | bytes 393224 | tf_op jit(solution)/shard_map/mixed_exchange/ppermute | solution.py:435
  68.7 8.6 %collective-permute-start.7 = (bf16[1,2,32,1024]{3,2,1,0:T(8,128)(2,1)}, bf16[1,2,32,1024]{3,2,1,0:T(8,128)(2,1)S(1)}, u32[]{:S(2)}, u32[]{:S(2)}) collective-permute-start(bf16[1,2,32,1024]{3,2,1,0:T(8,128)(2,1)} %get-tuple-element.49), channel_id=1, source_target_pairs={{0,2},{1,3},{2,0},{3,1},{4,6},{5,7},{6,4},{7,5},{8,10},{9,11},{10,... | collective-permute-start | bytes 393224 | tf_op jit(solution)/shard_map/mixed_exchange/ppermute | solution.py:435
  68.7 10.1 %collective-permute-start.8 = (bf16[1,2,32,1024]{3,2,1,0:T(8,128)(2,1)}, bf16[1,2,32,1024]{3,2,1,0:T(8,128)(2,1)S(1)}, u32[]{:S(2)}, u32[]{:S(2)}) collective-permute-start(bf16[1,2,32,1024]{3,2,1,0:T(8,128)(2,1)} %get-tuple-element.50), channel_id=1, source_target_pairs={{0,4},{1,5},{2,6},{3,7},{4,0},{5,1},{6,2},{7,3},{8,12},{9,13},{10,... | collective-permute-start | bytes 393224 | tf_op jit(solution)/shard_map/mixed_exchange/ppermute | solution.py:435
  70.5 10.7 %collective-permute-start.9 = (bf16[1,2,32,1024]{3,2,1,0:T(8,128)(2,1)}, bf16[1,2,32,1024]{3,2,1,0:T(8,128)(2,1)S(1)}, u32[]{:S(2)}, u32[]{:S(2)}) collective-permute-start(bf16[1,2,32,1024]{3,2,1,0:T(8,128)(2,1)} %get-tuple-element.51), channel_id=1, source_target_pairs={{0,6},{1,7},{2,4},{3,5},{4,2},{5,3},{6,0},{7,1},{8,14},{9,15},{10,... | collective-permute-start | bytes 393224 | tf_op jit(solution)/shard_map/mixed_exchange/ppermute | solution.py:435
  75.7 6.9 %collective-permute-start.13 = (bf16[1,2,32,1024]{3,2,1,0:T(8,128)(2,1)S(1)}, bf16[1,2,32,1024]{3,2,1,0:T(8,128)(2,1)S(1)}, u32[]{:S(2)}, u32[]{:S(2)}) collective-permute-start(bf16[1,2,32,1024]{3,2,1,0:T(8,128)(2,1)S(1)} %add_convert_fusion), channel_id=1, source_target_pairs={{0,1},{1,0},{2,3},{3,2},{4,5},{5,4},{6,7},{7,6},{8,9},{9,8},{10,11... | collective-permute-start | bytes 393224 | tf_op jit(solution)/shard_map/mixed_exchange/ppermute | solution.py:435
  83.6 5.8 %collective-permute-start.14 = (bf16[1,2,32,1024]{3,2,1,0:T(8,128)(2,1)S(1)}, bf16[1,2,32,1024]{3,2,1,0:T(8,128)(2,1)S(1)}, u32[]{:S(2)}, u32[]{:S(2)}) collective-permute-start(bf16[1,2,32,1024]{3,2,1,0:T(8,128)(2,1)S(1)} %fusion.6.refs_0_), channel_id=1, source_target_pairs={{0,1},{1,0},{2,3},{3,2},{4,5},{5,4},{6,7},{7,6},{8,9},{9,8},{10,11... | collective-permute-start | bytes 393224 | tf_op jit(solution)/shard_map/slope_share/ppermute | solution.py:435
  86.2 7.4 %collective-permute-start.19 = (bf16[1,2,32,1024]{3,2,1,0:T(8,128)(2,1)S(1)}, bf16[1,2,32,1024]{3,2,1,0:T(8,128)(2,1)S(1)}, u32[]{:S(2)}, u32[]{:S(2)}) collective-permute-start(bf16[1,2,32,1024]{3,2,1,0:T(8,128)(2,1)S(1)} %fusion.6.refs_0_), channel_id=1, source_target_pairs={{0,6},{1,7},{2,4},{3,5},{4,2},{5,3},{6,0},{7,1},{8,14},{9,15},{10,... | collective-permute-start | bytes 393224 | tf_op jit(solution)/shard_map/slope_share/ppermute | solution.py:435
  86.5 7.1 %collective-permute-start.17 = (bf16[1,2,32,1024]{3,2,1,0:T(8,128)(2,1)S(1)}, bf16[1,2,32,1024]{3,2,1,0:T(8,128)(2,1)S(1)}, u32[]{:S(2)}, u32[]{:S(2)}) collective-permute-start(bf16[1,2,32,1024]{3,2,1,0:T(8,128)(2,1)S(1)} %fusion.6.refs_0_), channel_id=1, source_target_pairs={{0,4},{1,5},{2,6},{3,7},{4,0},{5,1},{6,2},{7,3},{8,12},{9,13},{10,... | collective-permute-start | bytes 393224 | tf_op jit(solution)/shard_map/slope_share/ppermute | solution.py:435
  86.6 7.3 %collective-permute-start.15 = (bf16[1,2,32,1024]{3,2,1,0:T(8,128)(2,1)S(1)}, bf16[1,2,32,1024]{3,2,1,0:T(8,128)(2,1)S(1)}, u32[]{:S(2)}, u32[]{:S(2)}) collective-permute-start(bf16[1,2,32,1024]{3,2,1,0:T(8,128)(2,1)S(1)} %fusion.6.refs_0_), channel_id=1, source_target_pairs={{0,2},{1,3},{2,0},{3,1},{4,6},{5,7},{6,4},{7,5},{8,10},{9,11},{10,... | collective-permute-start | bytes 393224 | tf_op jit(solution)/shard_map/slope_share/ppermute | solution.py:435
  89.5 9.7 %collective-permute-start.20 = (bf16[1,2,32,1024]{3,2,1,0:T(8,128)(2,1)S(1)}, bf16[1,2,32,1024]{3,2,1,0:T(8,128)(2,1)S(1)}, u32[]{:S(2)}, u32[]{:S(2)}) collective-permute-start(bf16[1,2,32,1024]{3,2,1,0:T(8,128)(2,1)S(1)} %collective-permute-done.14.refs_1_), channel_id=1, source_target_pairs={{0,6},{1,7},{2,4},{3,5},{4,2},{5,3},{6,0},{7,1},{8,14},{9,15},{10,... | collective-permute-start | bytes 393224 | tf_op jit(solution)/shard_map/slope_share/ppermute | solution.py:435
  90.7 8.5 %collective-permute-start.18 = (bf16[1,2,32,1024]{3,2,1,0:T(8,128)(2,1)S(1)}, bf16[1,2,32,1024]{3,2,1,0:T(8,128)(2,1)S(1)}, u32[]{:S(2)}, u32[]{:S(2)}) collective-permute-start(bf16[1,2,32,1024]{3,2,1,0:T(8,128)(2,1)S(1)} %collective-permute-done.14.refs_1_), channel_id=1, source_target_pairs={{0,4},{1,5},{2,6},{3,7},{4,0},{5,1},{6,2},{7,3},{8,12},{9,13},{10,... | collective-permute-start | bytes 393224 | tf_op jit(solution)/shard_map/slope_share/ppermute | solution.py:435
  93.6 6.0 %collective-permute-start.16 = (bf16[1,2,32,1024]{3,2,1,0:T(8,128)(2,1)S(1)}, bf16[1,2,32,1024]{3,2,1,0:T(8,128)(2,1)S(1)}, u32[]{:S(2)}, u32[]{:S(2)}) collective-permute-start(bf16[1,2,32,1024]{3,2,1,0:T(8,128)(2,1)S(1)} %collective-permute-done.14.refs_1_), channel_id=1, source_target_pairs={{0,2},{1,3},{2,0},{3,1},{4,6},{5,7},{6,4},{7,5},{8,10},{9,11},{10,... | collective-permute-start | bytes 393224 | tf_op jit(solution)/shard_map/slope_share/ppermute | solution.py:435
  114.8 55.0 %all-to-all-start.1 = ((bf16[32,2,32,512]{3,2,1,0:T(8,128)(2,1)}), bf16[32,2,32,512]{3,2,1,0:T(8,128)(2,1)}, u32[]{:S(2)}, u32[]{:S(2)}) async-start(bf16[32,2,32,512]{3,2,1,0:T(8,128)(2,1)} %derivatives.3), calls=%async_computation.1 | async-start | bytes 4194304 | tf_op jit(solution)/shard_map/derivative_exchange/all_to_all | solution.py:518
  197.7 12.7 %all-to-all-start.5 = ((f32[16,8,128]{2,1,0:T(8,128)}), f32[16,8,128]{2,1,0:T(8,128)S(1)}, u32[]{:S(2)}, u32[]{:S(2)}) async-start(f32[16,8,128]{2,1,0:T(8,128)} %broadcast_in_dim.18), calls=%async_computation.5 | async-start | bytes 131072 | tf_op jit(solution)/shard_map/gram_sum/all_to_all | solution.py:38
  (13 other events, 64.8 us)
